TPU v7x, 512 devices: a whole 4x8x8 slice. The times are simulated.
512 devices in a mesh: heads: 8 (over y), ctx: 64 (over z, x, core).
Axes of the slice: x: 4, y: 8, z: 8, core: 2. Of those that a mesh axis runs over, the one named last changes fastest.
Arguments:
- queries: bfloat16 [32, 16384, 128], P('heads', 'ctx'), may hold values from -6 to 6
- key_rows: bfloat16 [32, 16384, 128], P('heads', 'ctx'), may hold values from -6 to 6
- value_rows: bfloat16 [32, 16384, 128], P('heads', 'ctx'), may hold values from -6 to 6
- level_weights: float32 [32, 15, 16384], P('heads', None, 'ctx'), may hold values from 0.1 to 3
- norm_gain: float32 [32, 128], P('heads'), may hold values from 0.1 to 1.9
- grad_normed: bfloat16 [32, 16384, 128], P('heads', 'ctx'), may hold values from -6 to 6
Outputs:
- normed: bfloat16 [32, 16384, 128], P('heads', 'ctx')
- grad_queries: bfloat16 [32, 16384, 128], P('heads', 'ctx')
- grad_keys: bfloat16 [32, 16384, 128], P('heads', 'ctx')
- grad_values: bfloat16 [32, 16384, 128], P('heads', 'ctx')
- grad_level_weights: float32 [32, 15, 16384], P('heads', None, 'ctx')
All inputs are finite; a program needn't handle non-finite values.
Results may differ from a plain program's by a relative error of at most 0.006.
Values sent between devices are 32-bit elements; how exact they have to be, the bound alone decides.
No kernel may reach another device: no remote copies, remote signals or barrier semaphores. Data moves between devices by JAX's collectives and lax.ppermute only.
A program may use at most 64 MiB of HBM per device.

v0:
```python
import math

import jax
import jax.numpy as jnp
from jax import lax
from jax.sharding import PartitionSpec as P

EPS = 1e-06
HIGH = lax.Precision.HIGHEST


def from_partner(value, axis, bit):
    mask = 2**bit
    pairs = [(source, source ^ mask) for source in range(lax.axis_size(axis))]
    return lax.ppermute(value, axis, pairs)


def level_scale(number, head_dim):
    return 2.0 ** (-max(number - 1, 0) / 2.0) / math.sqrt(head_dim)


def level_matrix(count):
    position = jnp.arange(count, dtype=jnp.int32)
    differ = jnp.bitwise_xor(position[:, None], position[None, :])
    bucket = jnp.zeros((count, count), jnp.int32)
    for exponent in range(count.bit_length() - 1):
        bucket = bucket + (differ >= 2**exponent).astype(jnp.int32)
    causal = position[None, :] <= position[:, None]
    return (bucket, causal)


def near_weights(factors, bucket, causal, head_dim):
    weights = jnp.zeros(factors[0].shape + (bucket.shape[1],), jnp.float32)
    for number in range(len(factors)):
        scaled = factors[number] * level_scale(number, head_dim)
        weights = weights + jnp.where(
            (bucket == number) & causal, scaled[..., None], jnp.float32(0.0)
        )
    return weights


def pair_level(matrix, step_bit):
    return from_partner(matrix, "ctx", step_bit)


def shards(queries, key_rows, value_rows, level_weights, norm_gain, grad_normed):
    heads_here, tokens_here, head_dim = queries.shape
    local_levels = tokens_here.bit_length()
    far_levels = lax.axis_size("ctx").bit_length() - 1
    block_index = lax.axis_index("ctx")
    width = heads_here * lax.axis_size("heads") * head_dim
    key_value = jnp.einsum("hsd,hse->hde", key_rows, value_rows, preferred_element_type=jnp.float32)
    group_sum = key_value
    far_list = []
    for step_bit in range(far_levels):
        partner = from_partner(group_sum, "ctx", step_bit)
        bit_set = block_index >> step_bit & 1
        far_list.append(jnp.where(bit_set == 1, partner, jnp.float32(0.0)))
        group_sum = group_sum + partner
    states = jnp.stack(far_list, 0)
    bucket, causal = level_matrix(tokens_here)
    weights = near_weights(
        [level_weights[:, number, :] for number in range(local_levels)], bucket, causal, head_dim
    )
    scores = jnp.einsum("htd,hsd->hts", queries, key_rows, preferred_element_type=jnp.float32)
    weighted = (weights * scores).astype(jnp.bfloat16)
    near_out = jnp.einsum("hts,hse->hte", weighted, value_rows, preferred_element_type=jnp.float32)
    far_scale = jnp.stack(
        [
            level_weights[:, local_levels + depth, :] * level_scale(local_levels + depth, head_dim)
            for depth in range(far_levels)
        ],
        0,
    )
    query_wide = queries.astype(jnp.float32)
    far_terms = jnp.einsum("htd,mhde->mhte", query_wide, states, precision=HIGH)
    attended = near_out + jnp.sum(far_scale[..., None] * far_terms, 0)
    totals = lax.psum(jnp.sum(attended * attended, axis=(0, 2)), "heads")
    inv_rms = lax.rsqrt(totals / width + EPS)
    normed = (attended * inv_rms[None, :, None] * norm_gain[:, None, :]).astype(jnp.bfloat16)
    scaled = norm_gain[:, None, :] * grad_normed.astype(jnp.float32)
    inner_sum = lax.psum(jnp.sum(scaled * attended, axis=(0, 2)), "heads")
    grad_out = (
        inv_rms[None, :, None] * scaled - attended * (inv_rms**3 * inner_sum / width)[None, :, None]
    ).astype(jnp.bfloat16)
    grad_wide = grad_out.astype(jnp.float32)
    grad_mix = jnp.einsum("hte,hse->hts", grad_out, value_rows, preferred_element_type=jnp.float32)
    product = grad_mix * scores
    near_grads = [
        level_scale(number, head_dim)
        * jnp.sum(jnp.where((bucket == number) & causal, product, jnp.float32(0.0)), axis=2)
        for number in range(local_levels)
    ]
    far_grads = [
        level_scale(local_levels + depth, head_dim) * jnp.sum(grad_wide * far_terms[depth], axis=2)
        for depth in range(far_levels)
    ]
    grad_scores = (weights * grad_mix).astype(jnp.bfloat16)
    grad_q = jnp.einsum("hts,hsd->htd", grad_scores, key_rows, preferred_element_type=jnp.float32)
    grad_q = grad_q + jnp.sum(
        far_scale[..., None] * jnp.einsum("hte,mhde->mhtd", grad_wide, states, precision=HIGH), 0
    )
    scaled_queries = (far_scale[..., None] * queries[None]).astype(jnp.bfloat16)
    grad_states = jnp.einsum(
        "mhtd,hte->mhde", scaled_queries, grad_out, preferred_element_type=jnp.float32
    )
    grad_kv = jnp.zeros((heads_here, head_dim, head_dim), jnp.float32)
    for depth in range(far_levels):
        level_total = grad_states[depth]
        for step_bit in range(depth + 1):
            partner = pair_level(level_total, step_bit)
            if step_bit < depth:
                level_total = level_total + partner
            else:
                bit_set = block_index >> step_bit & 1
                grad_kv = grad_kv + jnp.where(bit_set == 0, partner, jnp.float32(0.0))
    grad_kv = grad_kv.astype(jnp.bfloat16)
    grad_k = jnp.einsum("hts,htd->hsd", grad_scores, queries, preferred_element_type=jnp.float32)
    grad_k = grad_k + jnp.einsum(
        "hse,hde->hsd", value_rows, grad_kv, preferred_element_type=jnp.float32
    )
    grad_v = jnp.einsum("hts,hte->hse", weighted, grad_out, preferred_element_type=jnp.float32)
    grad_v = grad_v + jnp.einsum(
        "hsd,hde->hse", key_rows, grad_kv, preferred_element_type=jnp.float32
    )
    grad_rates = jnp.stack(near_grads + far_grads, axis=1)
    return (
        normed,
        grad_q.astype(jnp.bfloat16),
        grad_k.astype(jnp.bfloat16),
        grad_v.astype(jnp.bfloat16),
        grad_rates,
    )


def solution(mesh):
    in_specs = (
        P("heads", "ctx", None),
        P("heads", "ctx", None),
        P("heads", "ctx", None),
        P("heads", None, "ctx"),
        P("heads", None),
        P("heads", "ctx", None),
    )
    out_specs = (
        P("heads", "ctx", None),
        P("heads", "ctx", None),
        P("heads", "ctx", None),
        P("heads", "ctx", None),
        P("heads", None, "ctx"),
    )
    return jax.shard_map(shards, mesh=mesh, in_specs=in_specs, out_specs=out_specs, check_vma=False)
```

profile of v0, /device:TPU:1, one launch (start us, length us, event | category | flops | bytes accessed | tf_op | source)
XLA Modules:
  0.0 203.1 jit_solution(10442193959074506911)
XLA Ops:
  2.8 8.8 %collective-permute-start = (f32[4,128,128]{2,1,0:T(8,128)S(1)}, f32[4,128,128]{2,1,0:T(8,128)S(1)}, u32[]{:S(2)}, u32[]{:S(2)}) collective-permute-start(f32[4,128,128]{2,1,0:T(8,128)S(1)} %fusion.42), channel_id=1, source_target_pairs={{0,1},{1,0},{2,3},{3,2},{4,5},{5,4},{6,7},{7,6},{8,9},{9,8},{10,11... | collective-permute-start | bytes 786440 | tf_op jit(solution)/shard_map/ppermute | solution.py:15
  13.4 3.2 %multiply_convert_fusion.5 = (bf16[4,256,256]{1,2,0:T(8,128)(2,1)}, f32[4,256,256]{1,2,0:T(8,128)}) fusion(f32[4,256]{1,0:T(4,128)S(1)} %get-tuple-element.48, pred[256,256]{0,1:T(8,128)(4,1)S(1)} %get-tuple-element.65, f32[4,256]{1,0:T(4,128)S(1)} %get-tuple-element.49, pred[256,256]{0,1:T(8,128)(4,1)S(1)} %get-tuple-element.66, ...), kind=kOutput, calls=%fused_computation.32 | convolution fusion | flops 72089600 | bytes 2723840 | tf_op jit(solution)/shard_map/htd,hsd->hts/dot_general | solution.py:65
  21.0 6.5 %collective-permute-done.1 = f32[4,128,128]{2,1,0:T(8,128)S(1)} collective-permute-done((f32[4,128,128]{2,1,0:T(8,128)S(1)}, f32[4,128,128]{2,1,0:T(8,128)S(1)}, u32[]{:S(2)}, u32[]{:S(2)}) %collective-permute-start.1) | collective-permute-done | bytes 262176 | tf_op jit(solution)/shard_map/ppermute | solution.py:15
  30.8 7.1 %collective-permute-done.2 = f32[4,128,128]{2,1,0:T(8,128)S(1)} collective-permute-done((f32[4,128,128]{2,1,0:T(8,128)S(1)}, f32[4,128,128]{2,1,0:T(8,128)S(1)}, u32[]{:S(2)}, u32[]{:S(2)}) %collective-permute-start.2) | collective-permute-done | bytes 262176 | tf_op jit(solution)/shard_map/ppermute | solution.py:15
  42.5 3.6 %collective-permute-done.3 = f32[4,128,128]{2,1,0:T(8,128)S(1)} collective-permute-done((f32[4,128,128]{2,1,0:T(8,128)S(1)}, f32[4,128,128]{2,1,0:T(8,128)S(1)}, u32[]{:S(2)}, u32[]{:S(2)}) %collective-permute-start.3) | collective-permute-done | bytes 262176 | tf_op jit(solution)/shard_map/ppermute | solution.py:15
  48.1 14.6 %collective-permute-done.4 = f32[4,128,128]{2,1,0:T(8,128)S(1)} collective-permute-done((f32[4,128,128]{2,1,0:T(8,128)S(1)}, f32[4,128,128]{2,1,0:T(8,128)S(1)}, u32[]{:S(2)}, u32[]{:S(2)}) %collective-permute-start.4) | collective-permute-done | bytes 262176 | tf_op jit(solution)/shard_map/ppermute | solution.py:15
  62.7 4.3 %collective-permute-start.5 = (f32[4,128,128]{2,1,0:T(8,128)S(1)}, f32[4,128,128]{2,1,0:T(8,128)S(1)}, u32[]{:S(2)}, u32[]{:S(2)}) collective-permute-start(f32[4,128,128]{2,1,0:T(8,128)S(1)} %add.399), channel_id=1, source_target_pairs={{0,32},{1,33},{2,34},{3,35},{4,36},{5,37},{6,38},{7,39},{8,40},{9,... | collective-permute-start | bytes 786440 | tf_op jit(solution)/shard_map/ppermute | solution.py:15
  67.1 14.6 %collective-permute-done.5 = f32[4,128,128]{2,1,0:T(8,128)S(1)} collective-permute-done((f32[4,128,128]{2,1,0:T(8,128)S(1)}, f32[4,128,128]{2,1,0:T(8,128)S(1)}, u32[]{:S(2)}, u32[]{:S(2)}) %collective-permute-start.5) | collective-permute-done | bytes 262176 | tf_op jit(solution)/shard_map/ppermute | solution.py:15
  84.5 11.5 %all-reduce = (f32[256]{0:T(256)}, f32[256]{0:T(256)}) all-reduce(f32[256]{0:T(256)S(1)} %get-tuple-element.31, f32[256]{0:T(256)S(1)} %get-tuple-element.30), channel_id=1, replica_groups=mesh['heads'=8,'ctx'=64] {'heads'}, use_global_device_ids=true, to_apply=%region_2.3 | all-reduce | flops 512 | bytes 4096 | tf_op jit(solution)/shard_map/psum | solution.py:78
  96.8 2.4 %fusion.14 = (f32[4,256]{1,0:T(4,128)S(1)}, f32[4,256]{1,0:T(4,128)S(1)}, f32[4,256]{1,0:T(4,128)S(1)}, f32[4,256]{1,0:T(4,128)S(1)}, f32[4,256]{1,0:T(4,128)S(1...) fusion(f32[6,4,256,128]{2,3,1,0:T(8,128)S(1)} %get-tuple-element.59, ...), kind=kLoop, calls=%fused_computation.39 | loop fusion | flops 2877440 | bytes 4485120 | tf_op jit(solution)/shard_map/reduce_sum | solution.py:95
  102.3 6.9 %collective-permute-start.12 = (f32[4,128,128]{2,1,0:T(8,128)S(1)}, f32[4,128,128]{2,1,0:T(8,128)S(1)}, u32[]{:S(2)}, u32[]{:S(2)}) collective-permute-start(f32[4,128,128]{2,1,0:T(8,128)S(1)} %get-tuple-element.38), channel_id=1, source_target_pairs={{0,1},{1,0},{2,3},{3,2},{4,5},{5,4},{6,7},{7,6},{8,9},{9,8},{10,11... | collective-permute-start | bytes 786440 | tf_op jit(solution)/shard_map/ppermute | solution.py:15
  111.2 2.4 %collective-permute-start.21 = (f32[4,128,128]{2,1,0:T(8,128)S(1)}, f32[4,128,128]{2,1,0:T(8,128)S(1)}, u32[]{:S(2)}, u32[]{:S(2)}) collective-permute-start(f32[4,128,128]{2,1,0:T(8,128)S(1)} %get-tuple-element.36), channel_id=1, source_target_pairs={{0,1},{1,0},{2,3},{3,2},{4,5},{5,4},{6,7},{7,6},{8,9},{9,8},{10,11... | collective-permute-start | bytes 786440 | tf_op jit(solution)/shard_map/ppermute | solution.py:15
  115.5 2.4 %collective-permute-start.9 = (f32[4,128,128]{2,1,0:T(8,128)S(1)}, f32[4,128,128]{2,1,0:T(8,128)S(1)}, u32[]{:S(2)}, u32[]{:S(2)}) collective-permute-start(f32[4,128,128]{2,1,0:T(8,128)S(1)} %get-tuple-element.39), channel_id=1, source_target_pairs={{0,1},{1,0},{2,3},{3,2},{4,5},{5,4},{6,7},{7,6},{8,9},{9,8},{10,11... | collective-permute-start | bytes 786440 | tf_op jit(solution)/shard_map/ppermute | solution.py:15
  121.0 3.1 %collective-permute-start.22 = (f32[4,128,128]{2,1,0:T(8,128)S(1)}, f32[4,128,128]{2,1,0:T(8,128)S(1)}, u32[]{:S(2)}, u32[]{:S(2)}) collective-permute-start(f32[4,128,128]{2,1,0:T(8,128)S(1)} %get-tuple-element.42), channel_id=1, source_target_pairs={{0,2},{1,3},{2,0},{3,1},{4,6},{5,7},{6,4},{7,5},{8,10},{9,11},{10,... | collective-permute-start | bytes 786440 | tf_op jit(solution)/shard_map/ppermute | solution.py:15
  126.4 3.9 %collective-permute-done.22 = f32[4,128,128]{2,1,0:T(8,128)S(1)} collective-permute-done((f32[4,128,128]{2,1,0:T(8,128)S(1)}, f32[4,128,128]{2,1,0:T(8,128)S(1)}, u32[]{:S(2)}, u32[]{:S(2)}) %collective-permute-start.22) | collective-permute-done | bytes 262176 | tf_op jit(solution)/shard_map/ppermute | solution.py:15
  130.3 4.8 %collective-permute-start.23 = (f32[4,128,128]{2,1,0:T(8,128)S(1)}, f32[4,128,128]{2,1,0:T(8,128)S(1)}, u32[]{:S(2)}, u32[]{:S(2)}) collective-permute-start(f32[4,128,128]{2,1,0:T(8,128)S(1)} %add.419), channel_id=1, source_target_pairs={{0,4},{1,5},{2,6},{3,7},{4,0},{5,1},{6,2},{7,3},{8,12},{9,13},{10,... | collective-permute-start | bytes 786440 | tf_op jit(solution)/shard_map/ppermute | solution.py:15
  137.7 3.7 %collective-permute-start.18 = (f32[4,128,128]{2,1,0:T(8,128)S(1)}, f32[4,128,128]{2,1,0:T(8,128)S(1)}, u32[]{:S(2)}, u32[]{:S(2)}) collective-permute-start(f32[4,128,128]{2,1,0:T(8,128)S(1)} %add.414), channel_id=1, source_target_pairs={{0,4},{1,5},{2,6},{3,7},{4,0},{5,1},{6,2},{7,3},{8,12},{9,13},{10,... | collective-permute-start | bytes 786440 | tf_op jit(solution)/shard_map/ppermute | solution.py:15
  148.0 3.1 %collective-permute-start.14 = (f32[4,128,128]{2,1,0:T(8,128)S(1)}, f32[4,128,128]{2,1,0:T(8,128)S(1)}, u32[]{:S(2)}, u32[]{:S(2)}) collective-permute-start(f32[4,128,128]{2,1,0:T(8,128)S(1)} %add.410), channel_id=1, source_target_pairs={{0,4},{1,5},{2,6},{3,7},{4,0},{5,1},{6,2},{7,3},{8,12},{9,13},{10,... | collective-permute-start | bytes 786440 | tf_op jit(solution)/shard_map/ppermute | solution.py:15
  151.1 3.8 %collective-permute-done.18 = f32[4,128,128]{2,1,0:T(8,128)S(1)} collective-permute-done((f32[4,128,128]{2,1,0:T(8,128)S(1)}, f32[4,128,128]{2,1,0:T(8,128)S(1)}, u32[]{:S(2)}, u32[]{:S(2)}) %collective-permute-start.18) | collective-permute-done | bytes 262176 | tf_op jit(solution)/shard_map/ppermute | solution.py:15
  156.9 6.0 %collective-permute-start.25 = (f32[4,128,128]{2,1,0:T(8,128)S(1)}, f32[4,128,128]{2,1,0:T(8,128)S(1)}, u32[]{:S(2)}, u32[]{:S(2)}) collective-permute-start(f32[4,128,128]{2,1,0:T(8,128)S(1)} %add.421), channel_id=1, source_target_pairs={{0,16},{1,17},{2,18},{3,19},{4,20},{5,21},{6,22},{7,23},{8,24},{9,... | collective-permute-start | bytes 786440 | tf_op jit(solution)/shard_map/ppermute | solution.py:15
  168.8 3.3 %collective-permute-start.15 = (f32[4,128,128]{2,1,0:T(8,128)}, f32[4,128,128]{2,1,0:T(8,128)}, u32[]{:S(2)}, u32[]{:S(2)}) collective-permute-start(f32[4,128,128]{2,1,0:T(8,128)} %add.411), channel_id=1, source_target_pairs={{0,8},{1,9},{2,10},{3,11},{4,12},{5,13},{6,14},{7,15},{8,0},{9,1},... | collective-permute-start | bytes 786440 | tf_op jit(solution)/shard_map/ppermute | solution.py:15
  173.8 3.7 %collective-permute-start.20 = (f32[4,128,128]{2,1,0:T(8,128)}, f32[4,128,128]{2,1,0:T(8,128)}, u32[]{:S(2)}, u32[]{:S(2)}) collective-permute-start(f32[4,128,128]{2,1,0:T(8,128)} %add.416), channel_id=1, source_target_pairs={{0,16},{1,17},{2,18},{3,19},{4,20},{5,21},{6,22},{7,23},{8,24},{9,... | collective-permute-start | bytes 786440 | tf_op jit(solution)/shard_map/ppermute | solution.py:15
  178.2 4.6 %collective-permute-start.26 = (f32[4,128,128]{2,1,0:T(8,128)}, f32[4,128,128]{2,1,0:T(8,128)}, u32[]{:S(2)}, u32[]{:S(2)}) collective-permute-start(f32[4,128,128]{2,1,0:T(8,128)} %add.422), channel_id=1, source_target_pairs={{0,32},{1,33},{2,34},{3,35},{4,36},{5,37},{6,38},{7,39},{8,40},{9,... | collective-permute-start | bytes 786440 | tf_op jit(solution)/shard_map/ppermute | solution.py:15
  186.2 13.7 %collective-permute-done.20 = f32[4,128,128]{2,1,0:T(8,128)} collective-permute-done((f32[4,128,128]{2,1,0:T(8,128)}, f32[4,128,128]{2,1,0:T(8,128)}, u32[]{:S(2)}, u32[]{:S(2)}) %collective-permute-start.20) | collective-permute-done | bytes 262176 | tf_op jit(solution)/shard_map/ppermute | solution.py:15
  (204 shorter events, 59.4 us)
Async XLA Ops:
  2.8 14.7 %collective-permute-start = (f32[4,128,128]{2,1,0:T(8,128)S(1)}, f32[4,128,128]{2,1,0:T(8,128)S(1)}, u32[]{:S(2)}, u32[]{:S(2)}) collective-permute-start(f32[4,128,128]{2,1,0:T(8,128)S(1)} %fusion.42), channel_id=1, source_target_pairs={{0,1},{1,0},{2,3},{3,2},{4,5},{5,4},{6,7},{7,6},{8,9},{9,8},{10,11... | collective-permute-start | bytes 786440 | tf_op jit(solution)/shard_map/ppermute | solution.py:15
  17.5 10.0 %collective-permute-start.1 = (f32[4,128,128]{2,1,0:T(8,128)S(1)}, f32[4,128,128]{2,1,0:T(8,128)S(1)}, u32[]{:S(2)}, u32[]{:S(2)}) collective-permute-start(f32[4,128,128]{2,1,0:T(8,128)S(1)} %add.395), channel_id=1, source_target_pairs={{0,2},{1,3},{2,0},{3,1},{4,6},{5,7},{6,4},{7,5},{8,10},{9,11},{10,... | collective-permute-start | bytes 786440 | tf_op jit(solution)/shard_map/ppermute | solution.py:15
  27.5 10.4 %collective-permute-start.2 = (f32[4,128,128]{2,1,0:T(8,128)S(1)}, f32[4,128,128]{2,1,0:T(8,128)S(1)}, u32[]{:S(2)}, u32[]{:S(2)}) collective-permute-start(f32[4,128,128]{2,1,0:T(8,128)S(1)} %add.396), channel_id=1, source_target_pairs={{0,4},{1,5},{2,6},{3,7},{4,0},{5,1},{6,2},{7,3},{8,12},{9,13},{10,... | collective-permute-start | bytes 786440 | tf_op jit(solution)/shard_map/ppermute | solution.py:15
  46.1 16.6 %collective-permute-start.4 = (f32[4,128,128]{2,1,0:T(8,128)S(1)}, f32[4,128,128]{2,1,0:T(8,128)S(1)}, u32[]{:S(2)}, u32[]{:S(2)}) collective-permute-start(f32[4,128,128]{2,1,0:T(8,128)S(1)} %add.398), channel_id=1, source_target_pairs={{0,16},{1,17},{2,18},{3,19},{4,20},{5,21},{6,22},{7,23},{8,24},{9,... | collective-permute-start | bytes 786440 | tf_op jit(solution)/shard_map/ppermute | solution.py:15
  62.7 18.9 %collective-permute-start.5 = (f32[4,128,128]{2,1,0:T(8,128)S(1)}, f32[4,128,128]{2,1,0:T(8,128)S(1)}, u32[]{:S(2)}, u32[]{:S(2)}) collective-permute-start(f32[4,128,128]{2,1,0:T(8,128)S(1)} %add.399), channel_id=1, source_target_pairs={{0,32},{1,33},{2,34},{3,35},{4,36},{5,37},{6,38},{7,39},{8,40},{9,... | collective-permute-start | bytes 786440 | tf_op jit(solution)/shard_map/ppermute | solution.py:15
  102.3 15.8 %collective-permute-start.12 = (f32[4,128,128]{2,1,0:T(8,128)S(1)}, f32[4,128,128]{2,1,0:T(8,128)S(1)}, u32[]{:S(2)}, u32[]{:S(2)}) collective-permute-start(f32[4,128,128]{2,1,0:T(8,128)S(1)} %get-tuple-element.38), channel_id=1, source_target_pairs={{0,1},{1,0},{2,3},{3,2},{4,5},{5,4},{6,7},{7,6},{8,9},{9,8},{10,11... | collective-permute-start | bytes 786440 | tf_op jit(solution)/shard_map/ppermute | solution.py:15
  109.2 10.9 %collective-permute-start.16 = (f32[4,128,128]{2,1,0:T(8,128)S(1)}, f32[4,128,128]{2,1,0:T(8,128)S(1)}, u32[]{:S(2)}, u32[]{:S(2)}) collective-permute-start(f32[4,128,128]{2,1,0:T(8,128)S(1)} %get-tuple-element.37), channel_id=1, source_target_pairs={{0,1},{1,0},{2,3},{3,2},{4,5},{5,4},{6,7},{7,6},{8,9},{9,8},{10,11... | collective-permute-start | bytes 786440 | tf_op jit(solution)/shard_map/ppermute | solution.py:15
  111.2 9.0 %collective-permute-start.21 = (f32[4,128,128]{2,1,0:T(8,128)S(1)}, f32[4,128,128]{2,1,0:T(8,128)S(1)}, u32[]{:S(2)}, u32[]{:S(2)}) collective-permute-start(f32[4,128,128]{2,1,0:T(8,128)S(1)} %get-tuple-element.36), channel_id=1, source_target_pairs={{0,1},{1,0},{2,3},{3,2},{4,5},{5,4},{6,7},{7,6},{8,9},{9,8},{10,11... | collective-permute-start | bytes 786440 | tf_op jit(solution)/shard_map/ppermute | solution.py:15
  118.1 60.1 %collective-permute-start.6 = (f32[4,128,128]{2,1,0:T(8,128)S(1)}, f32[4,128,128]{2,1,0:T(8,128)S(1)}, u32[]{:S(2)}, u32[]{:S(2)}) collective-permute-start(f32[4,128,128]{2,1,0:T(8,128)S(1)} %get-tuple-element.35), channel_id=1, source_target_pairs={{0,1},{1,0},{2,3},{3,2},{4,5},{5,4},{6,7},{7,6},{8,9},{9,8},{10,11... | collective-permute-start | bytes 786440 | tf_op jit(solution)/shard_map/ppermute | solution.py:15
  121.0 9.3 %collective-permute-start.22 = (f32[4,128,128]{2,1,0:T(8,128)S(1)}, f32[4,128,128]{2,1,0:T(8,128)S(1)}, u32[]{:S(2)}, u32[]{:S(2)}) collective-permute-start(f32[4,128,128]{2,1,0:T(8,128)S(1)} %get-tuple-element.42), channel_id=1, source_target_pairs={{0,2},{1,3},{2,0},{3,1},{4,6},{5,7},{6,4},{7,5},{8,10},{9,11},{10,... | collective-permute-start | bytes 786440 | tf_op jit(solution)/shard_map/ppermute | solution.py:15
  124.2 13.5 %collective-permute-start.17 = (f32[4,128,128]{2,1,0:T(8,128)S(1)}, f32[4,128,128]{2,1,0:T(8,128)S(1)}, u32[]{:S(2)}, u32[]{:S(2)}) collective-permute-start(f32[4,128,128]{2,1,0:T(8,128)S(1)} %get-tuple-element.43), channel_id=1, source_target_pairs={{0,2},{1,3},{2,0},{3,1},{4,6},{5,7},{6,4},{7,5},{8,10},{9,11},{10,... | collective-permute-start | bytes 786440 | tf_op jit(solution)/shard_map/ppermute | solution.py:15
  130.3 13.4 %collective-permute-start.23 = (f32[4,128,128]{2,1,0:T(8,128)S(1)}, f32[4,128,128]{2,1,0:T(8,128)S(1)}, u32[]{:S(2)}, u32[]{:S(2)}) collective-permute-start(f32[4,128,128]{2,1,0:T(8,128)S(1)} %add.419), channel_id=1, source_target_pairs={{0,4},{1,5},{2,6},{3,7},{4,0},{5,1},{6,2},{7,3},{8,12},{9,13},{10,... | collective-permute-start | bytes 786440 | tf_op jit(solution)/shard_map/ppermute | solution.py:15
  135.4 12.5 %collective-permute-start.13 = (f32[4,128,128]{2,1,0:T(8,128)S(1)}, f32[4,128,128]{2,1,0:T(8,128)S(1)}, u32[]{:S(2)}, u32[]{:S(2)}) collective-permute-start(f32[4,128,128]{2,1,0:T(8,128)S(1)} %get-tuple-element.44), channel_id=1, source_target_pairs={{0,2},{1,3},{2,0},{3,1},{4,6},{5,7},{6,4},{7,5},{8,10},{9,11},{10,... | collective-permute-start | bytes 786440 | tf_op jit(solution)/shard_map/ppermute | solution.py:15
  137.7 17.2 %collective-permute-start.18 = (f32[4,128,128]{2,1,0:T(8,128)S(1)}, f32[4,128,128]{2,1,0:T(8,128)S(1)}, u32[]{:S(2)}, u32[]{:S(2)}) collective-permute-start(f32[4,128,128]{2,1,0:T(8,128)S(1)} %add.414), channel_id=1, source_target_pairs={{0,4},{1,5},{2,6},{3,7},{4,0},{5,1},{6,2},{7,3},{8,12},{9,13},{10,... | collective-permute-start | bytes 786440 | tf_op jit(solution)/shard_map/ppermute | solution.py:15
  143.7 13.2 %collective-permute-start.24 = (f32[4,128,128]{2,1,0:T(8,128)S(1)}, f32[4,128,128]{2,1,0:T(8,128)S(1)}, u32[]{:S(2)}, u32[]{:S(2)}) collective-permute-start(f32[4,128,128]{2,1,0:T(8,128)S(1)} %add.420), channel_id=1, source_target_pairs={{0,8},{1,9},{2,10},{3,11},{4,12},{5,13},{6,14},{7,15},{8,0},{9,1},... | collective-permute-start | bytes 786440 | tf_op jit(solution)/shard_map/ppermute | solution.py:15
  146.0 17.3 %collective-permute-start.10 = (f32[4,128,128]{2,1,0:T(8,128)S(1)}, f32[4,128,128]{2,1,0:T(8,128)S(1)}, u32[]{:S(2)}, u32[]{:S(2)}) collective-permute-start(f32[4,128,128]{2,1,0:T(8,128)S(1)} %get-tuple-element.45), channel_id=1, source_target_pairs={{0,2},{1,3},{2,0},{3,1},{4,6},{5,7},{6,4},{7,5},{8,10},{9,11},{10,... | collective-permute-start | bytes 786440 | tf_op jit(solution)/shard_map/ppermute | solution.py:15
  148.0 18.2 %collective-permute-start.14 = (f32[4,128,128]{2,1,0:T(8,128)S(1)}, f32[4,128,128]{2,1,0:T(8,128)S(1)}, u32[]{:S(2)}, u32[]{:S(2)}) collective-permute-start(f32[4,128,128]{2,1,0:T(8,128)S(1)} %add.410), channel_id=1, source_target_pairs={{0,4},{1,5},{2,6},{3,7},{4,0},{5,1},{6,2},{7,3},{8,12},{9,13},{10,... | collective-permute-start | bytes 786440 | tf_op jit(solution)/shard_map/ppermute | solution.py:15
  155.0 13.8 %collective-permute-start.19 = (f32[4,128,128]{2,1,0:T(8,128)S(1)}, f32[4,128,128]{2,1,0:T(8,128)S(1)}, u32[]{:S(2)}, u32[]{:S(2)}) collective-permute-start(f32[4,128,128]{2,1,0:T(8,128)S(1)} %add.415), channel_id=1, source_target_pairs={{0,8},{1,9},{2,10},{3,11},{4,12},{5,13},{6,14},{7,15},{8,0},{9,1},... | collective-permute-start | bytes 786440 | tf_op jit(solution)/shard_map/ppermute | solution.py:15
  156.9 16.8 %collective-permute-start.25 = (f32[4,128,128]{2,1,0:T(8,128)S(1)}, f32[4,128,128]{2,1,0:T(8,128)S(1)}, u32[]{:S(2)}, u32[]{:S(2)}) collective-permute-start(f32[4,128,128]{2,1,0:T(8,128)S(1)} %add.421), channel_id=1, source_target_pairs={{0,16},{1,17},{2,18},{3,19},{4,20},{5,21},{6,22},{7,23},{8,24},{9,... | collective-permute-start | bytes 786440 | tf_op jit(solution)/shard_map/ppermute | solution.py:15
  163.3 22.8 %collective-permute-start.8 = (f32[4,128,128]{2,1,0:T(8,128)}, f32[4,128,128]{2,1,0:T(8,128)}, u32[]{:S(2)}, u32[]{:S(2)}) collective-permute-start(f32[4,128,128]{2,1,0:T(8,128)} %get-tuple-element.41), channel_id=1, source_target_pairs={{0,2},{1,3},{2,0},{3,1},{4,6},{5,7},{6,4},{7,5},{8,10},{9,11},{10,... | collective-permute-start | bytes 786440 | tf_op jit(solution)/shard_map/ppermute | solution.py:15
  166.2 20.0 %collective-permute-start.11 = (f32[4,128,128]{2,1,0:T(8,128)}, f32[4,128,128]{2,1,0:T(8,128)}, u32[]{:S(2)}, u32[]{:S(2)}) collective-permute-start(f32[4,128,128]{2,1,0:T(8,128)} %add.407), channel_id=1, source_target_pairs={{0,4},{1,5},{2,6},{3,7},{4,0},{5,1},{6,2},{7,3},{8,12},{9,13},{10,... | collective-permute-start | bytes 786440 | tf_op jit(solution)/shard_map/ppermute | solution.py:15
  168.8 17.3 %collective-permute-start.15 = (f32[4,128,128]{2,1,0:T(8,128)}, f32[4,128,128]{2,1,0:T(8,128)}, u32[]{:S(2)}, u32[]{:S(2)}) collective-permute-start(f32[4,128,128]{2,1,0:T(8,128)} %add.411), channel_id=1, source_target_pairs={{0,8},{1,9},{2,10},{3,11},{4,12},{5,13},{6,14},{7,15},{8,0},{9,1},... | collective-permute-start | bytes 786440 | tf_op jit(solution)/shard_map/ppermute | solution.py:15
  173.8 26.1 %collective-permute-start.20 = (f32[4,128,128]{2,1,0:T(8,128)}, f32[4,128,128]{2,1,0:T(8,128)}, u32[]{:S(2)}, u32[]{:S(2)}) collective-permute-start(f32[4,128,128]{2,1,0:T(8,128)} %add.416), channel_id=1, source_target_pairs={{0,16},{1,17},{2,18},{3,19},{4,20},{5,21},{6,22},{7,23},{8,24},{9,... | collective-permute-start | bytes 786440 | tf_op jit(solution)/shard_map/ppermute | solution.py:15
  178.2 21.7 %collective-permute-start.26 = (f32[4,128,128]{2,1,0:T(8,128)}, f32[4,128,128]{2,1,0:T(8,128)}, u32[]{:S(2)}, u32[]{:S(2)}) collective-permute-start(f32[4,128,128]{2,1,0:T(8,128)} %add.422), channel_id=1, source_target_pairs={{0,32},{1,33},{2,34},{3,35},{4,36},{5,37},{6,38},{7,39},{8,40},{9,... | collective-permute-start | bytes 786440 | tf_op jit(solution)/shard_map/ppermute | solution.py:15
  (54 other events, 354.1 us)
where the time goes:
time: 205 us; the launch traced here: 203 us
  starting transfers between devices  84.9 us (41%)
  waiting for transfers between devices  71.1 us (35%)
  other arithmetic  16.4 us (8%)
  matrix products  13.2 us (6%)
  blocking collectives  11.5 us (6%)
  local copies, waits for them, and re-layouts  4.26 us (2%)
    ppermute x27, starting transfers between devices, from_partner(): return lax.ppermute(value, axis, pairs)  84.9 us
    ppermute x27, waiting for transfers between devices, from_partner(): return lax.ppermute(value, axis, pairs)  71.1 us
    psum x1, blocking collectives, shards(): totals = lax.psum(jnp.sum(attended * attended, axis=(0, 2)), 'heads')  11.5 us
  transfers between devices with their start and end apart: 27, of which 10 were waited for; matrix products, arithmetic and copies ran while one was open for 10% of the time, Pallas kernels for 0%

commit v1 on v0

v1 whole, which is shorter than its diff:
```python
import math

import jax
import jax.numpy as jnp
from jax import lax
from jax.experimental import pallas as pl
from jax.experimental.pallas import tpu as pltpu
from jax.sharding import Mesh
from jax.sharding import PartitionSpec as P

EPS = 1e-06
HIGH = lax.Precision.HIGHEST
F32 = jnp.float32
BF16 = jnp.bfloat16

NH = 4
TOK = 256
HD = 128
LOCAL = 9
FAR = 6
PLANE = 3
WIDTH = 32 * HD
MIB = 2**20

CTX = ("z", "x", "core")
ROWS = ("z", "x")
FLAT = ("x", "core")


def level_scale(number):
    return 2.0 ** (-max(number - 1, 0) / 2.0) / math.sqrt(HD)


def dot(a, b, ca, cb, precision=None):
    return lax.dot_general(
        a, b, (((ca,), (cb,)), ((), ())), precision=precision, preferred_element_type=F32
    )


def call(body, outs, operands, flops, moved, limit=32):
    vmem = pl.BlockSpec(memory_space=pltpu.VMEM)
    return pl.pallas_call(
        body,
        out_shape=[jax.ShapeDtypeStruct(s, d) for s, d in outs],
        in_specs=[vmem] * len(operands),
        out_specs=[vmem] * len(outs),
        cost_estimate=pl.CostEstimate(flops=flops, bytes_accessed=moved, transcendentals=0),
        compiler_params=pltpu.CompilerParams(vmem_limit_bytes=limit * MIB),
    )(*operands)


def key_value_body(k_ref, v_ref, kv_ref):
    for h in range(NH):
        kv_ref[h] = dot(k_ref[h], v_ref[h], 0, 0)


def level_masks():
    s = lax.broadcasted_iota(jnp.int32, (TOK, TOK), 0)
    t = lax.broadcasted_iota(jnp.int32, (TOK, TOK), 1)
    differ = s ^ t
    bucket = jnp.zeros((TOK, TOK), jnp.int32)
    for exponent in range(LOCAL - 1):
        bucket = bucket + (differ >= 2**exponent).astype(jnp.int32)
    return jnp.where(s <= t, bucket, -1)


def near_body(q_ref, k_ref, v_ref, lw_ref, sc_ref, wt_ref, wd_ref, no_ref, sq_ref, sqt_ref):
    level = level_masks()
    for h in range(NH):
        q, k, v = q_ref[h], k_ref[h], v_ref[h]
        lw = lw_ref[h]
        scores = dot(k, q, 1, 1)
        weights = jnp.zeros((TOK, TOK), F32)
        for number in range(LOCAL):
            row = lw[number : number + 1, :] * level_scale(number)
            weights = jnp.where(level == number, row, weights)
        weighted = (weights * scores).astype(BF16)
        sc_ref[h] = scores
        wt_ref[h] = weights
        wd_ref[h] = weighted
        no_ref[h] = dot(weighted, v, 0, 0)
        q_t = q.astype(F32).T
        for m in range(FAR):
            row = lw[LOCAL + m : LOCAL + m + 1, :] * level_scale(LOCAL + m)
            scaled_t = (q_t * row).astype(BF16)
            sqt_ref[h, m * HD : (m + 1) * HD, :] = scaled_t
            sq_ref[h, :, m * HD : (m + 1) * HD] = scaled_t.astype(F32).T.astype(BF16)


def plane_body(gath_ref, sq_ref, no_ref, part_ref, st_ref):
    p = lax.axis_index("x") * 2 + lax.axis_index("core")
    zero = jnp.float32(0.0)
    for h in range(NH):
        one = gath_ref[jnp.maximum(p - 1, 0), h]
        s0 = jnp.where((p & 1) == 1, one, zero)
        base = jnp.maximum((p >> 1) * 2 - 2, 0)
        s1 = jnp.where((p & 2) == 2, gath_ref[base, h] + gath_ref[base + 1, h], zero)
        four = (gath_ref[0, h] + gath_ref[1, h]) + (gath_ref[2, h] + gath_ref[3, h])
        s2 = jnp.where((p & 4) == 4, four, zero)
        states = jnp.concatenate([s0, s1, s2], axis=0).astype(BF16)
        st_ref[h] = states
        part_ref[h] = no_ref[h] + dot(sq_ref[h, :, : PLANE * HD], states, 1, 0)


def owner_forward_body(in_ref, out_ref):
    sums = []
    for z in range(8):
        total = in_ref[8 * z]
        for p in range(1, 8):
            total = total + in_ref[8 * z + p]
        sums.append(total)
    nothing = jnp.zeros((8, HD), F32)
    pair0 = sums[0] + sums[1]
    pair2 = sums[4] + sums[5]
    four = pair0 + (sums[2] + sums[3])
    for z in range(8):
        first = sums[z - 1] if z & 1 else nothing
        second = (pair2 if z & 4 else pair0) if z & 2 else nothing
        third = four if z & 4 else nothing
        for x in range(4):
            out_ref[4 * z + x, 0] = first
            out_ref[4 * z + x, 1] = second
            out_ref[4 * z + x, 2] = third


def attend_body(pc_ref, part_ref, sq_ref, gn_ref, gain_ref, att_ref, st_ref, pay_ref):
    squares = jnp.zeros((TOK, HD), F32)
    inner = jnp.zeros((TOK, HD), F32)
    for h in range(NH):
        states = []
        for m in range(PLANE):
            tiles = []
            for i in range(16):
                tiles.append(pc_ref[i % 2, 8 * h + i // 2, m])
            states.append(jnp.concatenate(tiles, axis=0))
        states = jnp.concatenate(states, axis=0).astype(BF16)
        st_ref[h] = states
        att = part_ref[h] + dot(sq_ref[h, :, PLANE * HD :], states, 1, 0)
        att_ref[h] = att
        scaled = gain_ref[h : h + 1, :] * gn_ref[h].astype(F32)
        squares = squares + att * att
        inner = inner + scaled * att
    ones = jnp.ones((8, HD), F32)
    squares_row = dot(ones, squares, 1, 1, HIGH)
    inner_row = dot(ones, inner, 1, 1, HIGH)
    half = TOK // 2
    tile = jnp.concatenate(
        [
            squares_row[0:1, :half],
            squares_row[0:1, half:],
            inner_row[0:1, :half],
            inner_row[0:1, half:],
            jnp.zeros((4, HD), F32),
        ],
        axis=0,
    )
    for peer in range(8):
        pay_ref[peer] = tile


def token_columns(recv_ref):
    total = recv_ref[0]
    for peer in range(1, 8):
        total = total + recv_ref[peer]
    inv = lax.rsqrt(total[0:2] / WIDTH + EPS)
    coef = inv * inv * inv * total[2:4] / WIDTH
    table = jnp.concatenate([inv, coef, jnp.zeros((4, HD), F32)], axis=0).T
    inv_col = jnp.concatenate([table[:, 0:1], table[:, 1:2]], axis=0)
    coef_col = jnp.concatenate([table[:, 2:3], table[:, 3:4]], axis=0)
    return inv_col, coef_col


def grad_body(recv_ref, att_ref, gn_ref, gain_ref, sqt_ref, go_ref, own_ref, send_ref, flat_ref):
    core = lax.axis_index("core")
    p = lax.axis_index("x") * 2 + core
    inv_col, coef_col = token_columns(recv_ref)
    zero = jnp.float32(0.0)
    for h in range(NH):
        scaled = gain_ref[h : h + 1, :] * gn_ref[h].astype(F32)
        go = (inv_col * scaled - att_ref[h] * coef_col).astype(BF16)
        go_ref[h] = go
        states = dot(sqt_ref[h], go, 1, 0)
        for m in range(PLANE):
            for k in range(8):
                row = (PLANE + m) * HD + 16 * k
                even = states[row : row + 8]
                odd = states[row + 8 : row + 16]
                own_ref[8 * h + k, m] = jnp.where(core == 0, even, odd)
                send_ref[8 * h + k, m] = jnp.where(core == 0, odd, even)
        for peer in range(8):
            value = jnp.zeros((HD, HD), F32)
            for m in range(PLANE):
                if not (peer >> m) & 1:
                    chosen = (p >> m) == (peer >> m) + 1
                    value = jnp.where(chosen, states[m * HD : (m + 1) * HD], value)
            flat_ref[peer, h] = value


def pair_body(own_ref, gath_ref, out_ref):
    other = 1 - lax.axis_index("core")
    out_ref[...] = own_ref[...] + gath_ref[other]


def owner_backward_body(in_ref, out_ref):
    grads = []
    for m in range(PLANE):
        rows = []
        for z in range(8):
            total = in_ref[4 * z, m]
            for x in range(1, 4):
                total = total + in_ref[4 * z + x, m]
            rows.append(total)
        grads.append(rows)
    pair2 = grads[1][2] + grads[1][3]
    pair6 = grads[1][6] + grads[1][7]
    four = (grads[2][4] + grads[2][5]) + (grads[2][6] + grads[2][7])
    for z in range(8):
        total = jnp.zeros((8, HD), F32)
        if not z & 1:
            total = total + grads[0][z + 1]
        if not z & 2:
            total = total + (pair6 if z & 4 else pair2)
        if not z & 4:
            total = total + four
        for p in range(8):
            out_ref[8 * z + p] = total


def back_body(
    q_ref, k_ref, v_ref, lw_ref, go_ref, att_ref, gain_ref, recv_ref, sc_ref, wt_ref, wd_ref,
    low_ref, high_ref, nm_ref, gq_ref, gk_ref, gv_ref, gl_ref,
):
    level = level_masks()
    inv_col, _ = token_columns(recv_ref)
    for h in range(NH):
        q, k, v, go = q_ref[h], k_ref[h], v_ref[h], go_ref[h]
        lw = lw_ref[h]
        nm_ref[h] = (att_ref[h] * inv_col * gain_ref[h : h + 1, :]).astype(BF16)
        mix = dot(v, go, 1, 1)
        product = mix * sc_ref[h]
        rows = []
        for number in range(LOCAL):
            picked = jnp.where(level == number, product, jnp.float32(0.0))
            rows.append(level_scale(number) * jnp.sum(picked, axis=0, keepdims=True))
        grad_scores = (wt_ref[h] * mix).astype(BF16)
        gk_ref[h] = dot(grad_scores, q, 1, 0)
        gv_ref[h] = dot(wd_ref[h], go, 1, 0)
        q_t = q.astype(F32).T
        far_t = jnp.zeros((HD, TOK), F32)
        for part, states_ref in enumerate((low_ref, high_ref)):
            turned = dot(states_ref[h], go, 1, 1)
            for m in range(PLANE):
                piece = turned[m * HD : (m + 1) * HD]
                number = LOCAL + part * PLANE + m
                row = lw[number : number + 1, :] * level_scale(number)
                far_t = far_t + row * piece
                rows.append(level_scale(number) * jnp.sum(piece * q_t, axis=0, keepdims=True))
        gq_ref[h] = (dot(grad_scores, k, 0, 0) + far_t.T).astype(BF16)
        gl_ref[h] = jnp.concatenate(rows, axis=0)


def final_body(piece_ref, flat_ref, k_ref, v_ref, gk_ref, gv_ref, outk_ref, outv_ref):
    for h in range(NH):
        grad_kv = (piece_ref[h] + flat_ref[h]).astype(BF16)
        outk_ref[h] = (gk_ref[h] + dot(v_ref[h], grad_kv, 1, 1)).astype(BF16)
        outv_ref[h] = (gv_ref[h] + dot(k_ref[h], grad_kv, 1, 0)).astype(BF16)


def swap(value, axes):
    return lax.all_to_all(value, axes, split_axis=0, concat_axis=0, tiled=True)


def shards(queries, key_rows, value_rows, level_weights, norm_gain, grad_normed):
    tokens = (NH, TOK, HD)
    square = (NH, TOK, TOK)
    matrix = (NH, HD, HD)
    stacked = (NH, PLANE * HD, HD)
    pieces = (32, PLANE, 8, HD)

    (kv,) = call(key_value_body, [(matrix, F32)], (key_rows, value_rows), 2**25, MIB)
    gathered = lax.all_gather(kv, FLAT, axis=0, tiled=False)
    owned = swap(kv.reshape(64, 8, HD), CTX)
    scores, weights, weighted, near_out, sq, sqt = call(
        near_body,
        [
            (square, F32),
            (square, F32),
            (square, BF16),
            (tokens, F32),
            ((NH, TOK, FAR * HD), BF16),
            ((NH, FAR * HD, TOK), BF16),
        ],
        (queries, key_rows, value_rows, level_weights),
        2**27,
        8 * MIB,
    )
    (outgoing,) = call(owner_forward_body, [(pieces, F32)], (owned,), 2**17, MIB // 2)
    arrived = swap(outgoing, ROWS)
    part, low = call(
        plane_body, [(tokens, F32), (stacked, BF16)], (gathered, sq, near_out), 2**27, 5 * MIB
    )
    both = lax.all_gather(arrived, "core", axis=0, tiled=False)
    attended, high, payload = call(
        attend_body,
        [(tokens, F32), (stacked, BF16), ((8, 8, HD), F32)],
        (both, part, sq, grad_normed, norm_gain),
        2**27,
        4 * MIB,
    )
    sums = swap(payload, "heads")
    grad_out, own, send, flat = call(
        grad_body,
        [(tokens, BF16), (pieces, F32), (pieces, F32), ((8,) + matrix, F32)],
        (sums, attended, grad_normed, norm_gain, sqt),
        2**28,
        6 * MIB,
    )
    flat_sum = lax.psum_scatter(flat, FLAT, scatter_dimension=0, tiled=False)
    sibling = lax.all_gather(send, "core", axis=0, tiled=False)
    (joined,) = call(pair_body, [(pieces, F32)], (own, sibling), 2**17, 3 * MIB // 2)
    returned = swap(joined, ROWS)
    normed, grad_q, near_k, near_v, grad_rates = call(
        back_body,
        [
            (tokens, BF16),
            (tokens, BF16),
            (tokens, F32),
            (tokens, F32),
            ((NH, LOCAL + FAR, TOK), F32),
        ],
        (
            queries, key_rows, value_rows, level_weights, grad_out, attended, norm_gain, sums,
            scores, weights, weighted, low, high,
        ),
        2**28,
        8 * MIB,
    )
    (spread,) = call(owner_backward_body, [((64, 8, HD), F32)], (returned,), 2**17, MIB // 2)
    total = swap(spread, CTX).reshape(matrix)
    grad_k, grad_v = call(
        final_body,
        [(tokens, BF16), (tokens, BF16)],
        (total, flat_sum, key_rows, value_rows, near_k, near_v),
        2**26,
        3 * MIB,
    )
    return normed, grad_q, grad_k, grad_v, grad_rates


def solution(mesh):
    grid = Mesh(mesh.devices.reshape(8, 8, 4, 2), ("heads",) + CTX)
    rows = P("heads", CTX, None)
    rates = P("heads", None, CTX)
    return jax.shard_map(
        shards,
        mesh=grid,
        in_specs=(rows, rows, rows, rates, P("heads", None), rows),
        out_specs=(rows, rows, rows, rows, rates),
        check_vma=False,
    )
```

time: 205 us -> 141 us (0.69)
  starting transfers between devices: 84.9 us -> 11.9 us
  waiting for transfers between devices: 71.1 us -> 13.3 us
  blocking collectives: 11.5 us -> 67.3 us
  local copies, waits for them, and re-layouts: 4.26 us -> 21.5 us
  other arithmetic: 16.4 us -> 0 us
  matrix products: 13.2 us -> 0 us
  between operations: 1.81 us -> 14.2 us
  Pallas kernels: 0 us -> 11.7 us
    ppermute x27 -> x0, starting transfers between devices: 84.9 us -> none  [from_partner(): return lax.ppermute(value, axis, pairs)]
    ppermute x27 -> x0, waiting for transfers between devices: 71.1 us -> none  [from_partner(): return lax.ppermute(value, axis, pairs)]
    all_to_all x0 -> x3, blocking collectives: none -> 59.2 us  [swap(): return lax.all_to_all(value, axes, split_axis=0, concat_axis=0, tiled=True)]
    unnamed x104 -> x66, local copies, waits for them, and re-layouts: 3.01 us -> 21.5 us
    all_to_all x0 -> x2, waiting for transfers between devices: none -> 13.2 us  [swap(): return lax.all_to_all(value, axes, split_axis=0, concat_axis=0, tiled=True)]
    dot_general x12 -> x0, matrix products: 13.2 us -> none  [the longest x1 3.21 us: shards(): jnp.einsum('htd,hsd->hts', queries, key_rows, preferred_element_type=jnp....]
    all_to_all x0 -> x2, starting transfers between devices: none -> 11.8 us  [swap(): return lax.all_to_all(value, axes, split_axis=0, concat_axis=0, tiled=True)]
    pallas_call x0 -> x10, Pallas kernels: none -> 11.7 us  [call(): pl.pallas_call(body, out_shape=[jax.ShapeDtypeStruct(s, d) for s, d in ou...]
  transfers between devices with their start and end apart: 27 -> 4, of which waited for: 10 -> 2; matrix products, arithmetic and copies ran while one was open for 10% -> 0% of each run, Pallas kernels for 0% -> 4%
where the time goes in v1:
time: 141 us; the launch traced here: 140 us
  blocking collectives  67.3 us (48%)
  local copies, waits for them, and re-layouts  21.5 us (15%)
  between operations  14.2 us (10%)
  waiting for transfers between devices  13.3 us (9%)
  starting transfers between devices  11.9 us (8%)
  Pallas kernels  11.7 us (8%)
    all_to_all x3, blocking collectives, swap(): return lax.all_to_all(value, axes, split_axis=0, concat_axis=0, tiled=True)  59.2 us
    unnamed x66, local copies, waits for them, and re-layouts  21.5 us
    all_to_all x2, waiting for transfers between devices, swap(): return lax.all_to_all(value, axes, split_axis=0, concat_axis=0, tiled=True)  13.2 us
    all_to_all x2, starting transfers between devices, swap(): return lax.all_to_all(value, axes, split_axis=0, concat_axis=0, tiled=True)  11.8 us
    pallas_call x10, Pallas kernels, call(): pl.pallas_call(body, out_shape=[jax.ShapeDtypeStruct(s, d) for s, d in ou...  11.7 us
    all_gather x1, blocking collectives, shards(): sibling = lax.all_gather(send, 'core', axis=0, tiled=False)  4.07 us
    all_gather x1, blocking collectives, shards(): both = lax.all_gather(arrived, 'core', axis=0, tiled=False)  4.06 us
  transfers between devices with their start and end apart: 4, of which 2 were waited for; matrix products, arithmetic and copies ran while one was open for 0% of the time, Pallas kernels for 4%

profile of v1, /device:TPU:1, one launch (start us, length us, event | category | flops | bytes accessed | tf_op | source)
XLA Modules:
  0.0 139.9 jit_solution(2333928997307912652)
XLA Ops:
  9.1 1.0 shard_map.101
  10.1 28.0 %all_to_all.25.in_ref = f32[64,8,128]{2,1,0:T(8,128)S(1)} all-to-all(f32[64,8,128]{2,1,0:T(8,128)} %bitcast), channel_id=1, replica_groups=mesh['heads'=8,'z'=8,'x'=4,'core'=2] {'z','x','core'}, dimensions={0} | all-to-all | bytes 524288 | tf_op jit(solution)/shard_map/all_to_all | solution.py:270
  38.9 4.6 %all-to-all-start.1 = ((f32[32,3,8,128]{3,2,1,0:T(8,128)}), f32[32,3,8,128]{3,2,1,0:T(8,128)}, u32[]{:S(2)}, u32[]{:S(2)}) async-start(f32[32,3,8,128]{3,2,1,0:T(8,128)} %shard_map.102), calls=%async_computation.1 | async-start | bytes 786432 | tf_op jit(solution)/shard_map/all_to_all | solution.py:270
  43.6 1.3 shard_map.103
  45.0 1.1 copy-done.5
  46.1 1.0 copy-done.9
  47.1 1.0 copy-done.11
  48.9 9.0 %all-to-all-done.1 = f32[32,3,8,128]{3,2,1,0:T(8,128)} async-done(((f32[32,3,8,128]{3,2,1,0:T(8,128)}), f32[32,3,8,128]{3,2,1,0:T(8,128)}, u32[]{:S(2)}, u32[]{:S(2)}) %all-to-all-start.1) | async-done | bytes 393248 | tf_op jit(solution)/shard_map/all_to_all | solution.py:270
  57.9 4.1 %all-gather = f32[64,3,8,128]{3,2,1,0:T(8,128)S(1)} all-gather(f32[32,3,8,128]{3,2,1,0:T(8,128)} %all-to-all-done.1), channel_id=2, replica_groups=mesh['heads'=8,'z'=8,'x'=4,'core'=2] {'core'}, dimensions={0}, use_global_device_ids=true | all-gather | bytes 1179648 | tf_op jit(solution)/shard_map/all_gather | solution.py:302
  62.0 1.6 %copy-done.4 = f32[32,128,128]{2,1,0:T(8,128)S(1)} copy-done((f32[32,128,128]{2,1,0:T(8,128)S(1)}, f32[32,128,128]{2,1,0:T(8,128)}, u32[]{:S(2)}) %copy-start.4) | copy-done | bytes 2097176
  66.2 13.6 %all_to_all.26.recv_ref = f32[8,8,128]{2,1,0:T(8,128)S(1)} all-to-all(f32[8,8,128]{2,1,0:T(8,128)S(1)} %get-tuple-element.30), channel_id=1, replica_groups=mesh['heads'=8,'z'=8,'x'=4,'core'=2] {'heads'}, dimensions={0} | all-to-all | bytes 65536 | tf_op jit(solution)/shard_map/all_to_all | solution.py:270
  79.7 2.1 %shard_map.106 = (bf16[4,256,128]{2,1,0:T(8,128)(2,1)S(1)}, f32[32,3,8,128]{3,2,1,0:T(8,128)S(1)}, f32[32,3,8,128]{3,2,1,0:T(8,128)S(1)}, f32[8,4,128,128]{3,2,1,0:T(8,128)}) custom-call(f32[8,8,128]{2,1,0:T(8,128)S(1)} %all_to_all.26.recv_ref, f32[4,256,128]{2,1,0:T(8,128)S(1)} %get-tuple-element.31.att_ref, bf16[4,256,128]{2,1,0:T(8,128)(2,1)S(1)} %copy-done.13, ...), custom_call_target="tpu_custom_call" | custom-call | flops 268435456 | bytes 6291456 | tf_op jit(solution)/shard_map/pallas_call | solution.py:42
  84.1 4.1 %all-gather.2 = f32[64,3,8,128]{3,2,1,0:T(8,128)S(1)} all-gather(f32[32,3,8,128]{3,2,1,0:T(8,128)} %copy-done.26), channel_id=4, replica_groups=mesh['heads'=8,'z'=8,'x'=4,'core'=2] {'core'}, dimensions={0}, use_global_device_ids=true | all-gather | bytes 1179648 | tf_op jit(solution)/shard_map/all_gather | solution.py:319
  88.2 1.0 copy-done.25
  89.2 17.6 %all_to_all.27.in_ref = f32[32,3,8,128]{3,2,1,0:T(8,128)S(1)} all-to-all(f32[32,3,8,128]{3,2,1,0:T(8,128)S(1)} %shard_map.108), channel_id=1, replica_groups=mesh['heads'=8,'z'=8,'x'=4,'core'=2] {'z','x'}, dimensions={0} | all-to-all | bytes 786432 | tf_op jit(solution)/shard_map/all_to_all | solution.py:270
  107.6 7.2 %all-to-all-start.4 = ((f32[64,8,128]{2,1,0:T(8,128)}), f32[64,8,128]{2,1,0:T(8,128)}, u32[]{:S(2)}, u32[]{:S(2)}) async-start(f32[64,8,128]{2,1,0:T(8,128)} %shard_map.109), calls=%async_computation.4 | async-start | bytes 524288 | tf_op jit(solution)/shard_map/all_to_all | solution.py:270
  114.8 1.0 copy-done.15
  115.9 1.0 copy-done.21
  116.9 1.0 copy-done.23
  118.8 2.7 %shard_map.107 = (bf16[4,256,128]{2,1,0:T(8,128)(2,1)}, bf16[4,256,128]{2,1,0:T(8,128)(2,1)}, f32[4,256,128]{2,1,0:T(8,128)S(1)}, f32[4,256,128]{2,1,0:T(8,128)S(1)}, f32[4,15,256]{2,1,0:T(8,128)S(1)}) custom-call(bf16[4,256,128]{2,1,0:T(8,128)(2,1)S(1)} %copy-done.8, bf16[4,256,128]{2,1,0:T(8,128)(2,1)S(1)} %copy-done.1, ...), custom_call_target="tpu_custom_call" | custom-call | flops 268435456 | bytes 8388608 | tf_op jit(solution)/shard_map/pallas_call | solution.py:42
  123.8 4.2 %all-to-all-done.4 = f32[64,8,128]{2,1,0:T(8,128)} async-done(((f32[64,8,128]{2,1,0:T(8,128)}), f32[64,8,128]{2,1,0:T(8,128)}, u32[]{:S(2)}, u32[]{:S(2)}) %all-to-all-start.4) | async-done | bytes 262176 | tf_op jit(solution)/shard_map/all_to_all | solution.py:270
  128.0 1.0 copy-done.17
  129.0 1.0 copy-done.19
  131.0 2.0 %shard_map.110 = (bf16[4,256,128]{2,1,0:T(8,128)(2,1)}, bf16[4,256,128]{2,1,0:T(8,128)(2,1)}) custom-call(f32[4,128,128]{2,1,0:T(8,128)} %bitcast.4.piece_ref, f32[4,128,128]{2,1,0:T(8,128)S(1)} %bitcast.9, bf16[4,256,128]{2,1,0:T(8,128)(2,1)S(1)} %copy-done.1, bf16[4,256,128]{2,1,0:T(8,128)(2,1)S(1)} %copy-done.3, f32[4,256,128]{2,1,0:T(8,128)S(1)} %copy-done.17, ...), custom_call_target="tpu_custom_call" | custom-call | flops 67108864 | bytes 3145728 | tf_op jit(solution)/shard_map/pallas_call | solution.py:42
  (67 shorter events, 13.4 us)
Async XLA Ops:
  7.2 54.8 %all-gather.5.cloned.1.call-start = ((), (), s32[]{:S(2)}) async-start(), calls=%async_computation.7 | async-start | bytes 2359296 | tf_op jit(solution)/shard_map/all_gather | solution.py:281
  9.1 34.4 %copy-start.31 = (f32[4,15,256]{2,0,1:T(4,128)S(1)}, f32[4,15,256]{2,0,1:T(4,128)}, u32[]{:S(2)}) copy-start(f32[4,15,256]{2,0,1:T(4,128)} %param.9) | copy-start | bytes 184324
  9.1 34.5 %copy-start.1 = (bf16[4,256,128]{2,1,0:T(8,128)(2,1)S(1)}, bf16[4,256,128]{2,1,0:T(8,128)(2,1)}, u32[]{:S(2)}) copy-start(bf16[4,256,128]{2,1,0:T(8,128)(2,1)} %k_ref.7) | copy-start | bytes 786436
  9.1 34.5 %copy-start.3 = (bf16[4,256,128]{2,1,0:T(8,128)(2,1)S(1)}, bf16[4,256,128]{2,1,0:T(8,128)(2,1)}, u32[]{:S(2)}) copy-start(bf16[4,256,128]{2,1,0:T(8,128)(2,1)} %v_ref.7) | copy-start | bytes 786436
  9.1 34.5 %copy-start.7 = (bf16[4,256,128]{2,1,0:T(8,128)(2,1)S(1)}, bf16[4,256,128]{2,1,0:T(8,128)(2,1)}, u32[]{:S(2)}) copy-start(bf16[4,256,128]{2,1,0:T(8,128)(2,1)} %q_ref.3) | copy-start | bytes 786436
  38.9 19.0 %all-to-all-start.1 = ((f32[32,3,8,128]{3,2,1,0:T(8,128)}), f32[32,3,8,128]{3,2,1,0:T(8,128)}, u32[]{:S(2)}, u32[]{:S(2)}) async-start(f32[32,3,8,128]{3,2,1,0:T(8,128)} %shard_map.102), calls=%async_computation.1 | async-start | bytes 786432 | tf_op jit(solution)/shard_map/all_to_all | solution.py:270
  43.5 84.5 %reduce-scatter.2.cloned.1.call-start = ((), (), s32[]{:S(2)}) async-start(), calls=%async_computation.6 | async-start | bytes 2359296 | tf_op jit(solution)/shard_map/reduce_scatter | solution.py:318
  45.0 1.2 copy-start.5
  46.1 1.0 copy-start.9
  47.1 1.0 copy-start.11
  62.0 1.6 %copy-start.4 = (f32[32,128,128]{2,1,0:T(8,128)S(1)}, f32[32,128,128]{2,1,0:T(8,128)}, u32[]{:S(2)}) copy-start(f32[32,128,128]{2,1,0:T(8,128)} %all-gather.5.cloned.1.call-done) | copy-start | bytes 6291460
  63.6 1.2 copy-start.13
  63.6 1.2 copy-start.30
  64.7 15.0 %copy-start.6 = (bf16[4,768,256]{2,1,0:T(8,128)(2,1)S(1)}, bf16[4,768,256]{2,1,0:T(8,128)(2,1)}, u32[]{:S(2)}) copy-start(bf16[4,768,256]{2,1,0:T(8,128)(2,1)} %copy-done.5) | copy-start | bytes 4718596
  84.1 30.7 %copy-start.8 = (bf16[4,256,128]{2,1,0:T(8,128)(2,1)S(1)}, bf16[4,256,128]{2,1,0:T(8,128)(2,1)}, u32[]{:S(2)}) copy-start(bf16[4,256,128]{2,1,0:T(8,128)(2,1)} %q_ref.3) | copy-start | bytes 786436
  84.1 30.7 %copy-start.10 = (f32[4,256,256]{2,1,0:T(8,128)S(1)}, f32[4,256,256]{2,1,0:T(8,128)}, u32[]{:S(2)}) copy-start(f32[4,256,256]{2,1,0:T(8,128)} %copy-done.9) | copy-start | bytes 3145732
  84.1 30.7 %copy-start.12 = (f32[4,256,256]{2,1,0:T(8,128)S(1)}, f32[4,256,256]{2,1,0:T(8,128)}, u32[]{:S(2)}) copy-start(f32[4,256,256]{2,1,0:T(8,128)} %copy-done.11) | copy-start | bytes 3145732
  88.2 1.0 copy-start.25
  107.6 20.4 %all-to-all-start.4 = ((f32[64,8,128]{2,1,0:T(8,128)}), f32[64,8,128]{2,1,0:T(8,128)}, u32[]{:S(2)}, u32[]{:S(2)}) async-start(f32[64,8,128]{2,1,0:T(8,128)} %shard_map.109), calls=%async_computation.4 | async-start | bytes 524288 | tf_op jit(solution)/shard_map/all_to_all | solution.py:270
  114.8 1.1 copy-start.15
  115.9 1.0 copy-start.21
  116.9 1.0 copy-start.23
  128.0 1.0 copy-start.17
  129.0 1.0 copy-start.19
  (12 other events, 9.9 us)
Sparse Core Ops, SparseCore 0:
  10.7 36.8 all-gather.4
  84.2 30.9 reduce-scatter.1

commit v2 on v1

v2 whole, which is shorter than its diff:
```python
import math

import jax
import jax.numpy as jnp
from jax import lax
from jax.experimental import pallas as pl
from jax.experimental.pallas import tpu as pltpu
from jax.sharding import Mesh
from jax.sharding import PartitionSpec as P

EPS = 1e-06
F32 = jnp.float32
BF16 = jnp.bfloat16

NH = 4
TOK = 256
HD = 128
LOCAL = 9
FAR = 6
PLANE = 3
WIDTH = 32 * HD
MIB = 2**20
ALONE = 60

CTX = ("z", "x", "core")
ROWS = ("z", "x")

TOKENS = (NH, TOK, HD)
TURNED = (NH, HD, TOK)
MATRIX = (NH, HD, HD)
HALF = (NH // 2, HD, HD)
STACKED = (NH, PLANE * HD, HD)
PIECES = (32, PLANE, 8, HD)


def level_scale(number):
    return 2.0 ** (-max(number - 1, 0) / 2.0) / math.sqrt(HD)


def dot(a, b, ca, cb):
    return lax.dot_general(a, b, (((ca,), (cb,)), ((), ())), preferred_element_type=F32)


def call(body, outs, operands, flops, moved, far_in=(), far_out=(), limit=16, after=(), views={}):
    near = pl.BlockSpec(memory_space=pltpu.VMEM)
    far = pl.BlockSpec(memory_space=pltpu.HBM)
    count = len(operands)
    shapes = [views[i][0] if i in views else a.shape for i, a in enumerate(operands)]
    buffers = [pltpu.VMEM(shapes[i], operands[i].dtype) for i in far_in]
    buffers += [pltpu.VMEM(*outs[i]) for i in far_out]

    def split(shape):
        return shape[0] == NH and len(shape) > 2

    parts = [NH if split(shapes[i]) else 1 for i in far_in]
    parts += [NH if split(outs[i][0]) else 1 for i in far_out]
    copies = sum(parts)

    def wrapped(*refs):
        refs = list(refs)
        sems = refs.pop() if copies else None
        del refs[count : count + len(after)]
        scratch = refs[count + len(outs) :]
        used = refs[: count + len(outs)]
        whole, before, behind, last = [], [[] for _ in range(NH)], [[] for _ in range(NH)], []
        sem = 0
        for slot, i in enumerate(far_in):
            held = scratch[slot]
            if i in views:
                used[i] = views[i][1](used[i])
            if parts[slot] == NH:
                for h in range(NH):
                    before[h].append(
                        pltpu.make_async_copy(used[i].at[h], held.at[h], sems.at[sem + h])
                    )
            else:
                whole.append(pltpu.make_async_copy(used[i], held, sems.at[sem]))
            sem += parts[slot]
            used[i] = held
        for slot, i in enumerate(far_out, len(far_in)):
            held = scratch[slot]
            if parts[slot] == NH:
                for h in range(NH):
                    behind[h].append(
                        pltpu.make_async_copy(held.at[h], used[count + i].at[h], sems.at[sem + h])
                    )
            else:
                last.append(pltpu.make_async_copy(held, used[count + i], sems.at[sem]))
            sem += parts[slot]
            used[count + i] = held
        for copy in whole + sum(before, []):
            copy.start()
        for copy in whole:
            copy.wait()
        step = body(*used)
        for h in range(NH):
            for copy in before[h]:
                copy.wait()
            if step is not None:
                step(h)
            for copy in behind[h]:
                copy.start()
        for copy in last:
            copy.start()
        for copy in sum(behind, []) + last:
            copy.wait()

    return pl.pallas_call(
        wrapped,
        out_shape=[jax.ShapeDtypeStruct(s, d) for s, d in outs],
        in_specs=[far if i in far_in else near for i in range(count)]
        + [pl.BlockSpec(memory_space=pl.ANY)] * len(after),
        out_specs=[far if i in far_out else near for i in range(len(outs))],
        scratch_shapes=buffers + ([pltpu.SemaphoreType.DMA((copies,))] if copies else []),
        cost_estimate=pl.CostEstimate(flops=flops, bytes_accessed=moved, transcendentals=0),
        compiler_params=pltpu.CompilerParams(vmem_limit_bytes=int(limit * MIB)),
    )(*operands, *after)


def key_value_body(k_ref, v_ref, kv_ref):
    def step(h):
        kv_ref[h] = dot(k_ref[h], v_ref[h], 0, 0)

    return step


def level_masks():
    s = lax.broadcasted_iota(jnp.int32, (TOK, TOK), 0)
    t = lax.broadcasted_iota(jnp.int32, (TOK, TOK), 1)
    differ = s ^ t
    bucket = jnp.zeros((TOK, TOK), jnp.int32)
    for exponent in range(LOCAL - 1):
        bucket = bucket + (differ >= 2**exponent).astype(jnp.int32)
    return jnp.where(s <= t, bucket, -1)


def level_row(lw_ref, number, h):
    return lw_ref[number, h : h + 1, :] * level_scale(number)


def near_weights(lw_ref, level, h):
    weights = jnp.zeros((TOK, TOK), F32)
    for number in range(LOCAL):
        weights = jnp.where(level == number, level_row(lw_ref, number, h), weights)
    return weights


def scaled_queries(q_t, lw_ref, part, h):
    levels = [LOCAL + part * PLANE + m for m in range(PLANE)]
    return jnp.concatenate([q_t * level_row(lw_ref, n, h) for n in levels], axis=0).astype(BF16)


def near_body(
    lw_ref, gain_ref, wide_ref, both_ref, q_ref, k_ref, v_ref, gn_ref, mixed_ref, st_ref, qt_ref
):
    level = level_masks()
    odd = lax.axis_index("core") == 1

    def step(h):
        q = q_ref[h]
        scores = dot(k_ref[h], q, 1, 1)
        weighted = (near_weights(lw_ref, level, h) * scores).astype(BF16)
        q_t = q.astype(F32).T
        qt_ref[h] = q_t.astype(BF16)
        s0 = jnp.where(odd, both_ref[h], jnp.float32(0.0))
        s1 = wide_ref[h // 2, 0, h % 2]
        s2 = wide_ref[h // 2, 1, h % 2]
        states = jnp.concatenate([s0, s1, s2], axis=0).astype(BF16)
        st_ref[h] = states
        far = dot(states, scaled_queries(q_t, lw_ref, 0, h), 0, 0)
        mixed_ref[h, 0] = dot(v_ref[h], weighted, 0, 0) + far
        mixed_ref[h, 1] = (gain_ref[h : h + 1, :] * gn_ref[h].astype(F32)).T

    return step


def half_body(both_ref, out_ref):
    first = lax.axis_index("core") * (NH // 2)
    for h in range(NH // 2):
        out_ref[h] = both_ref[0, first + h] + both_ref[1, first + h]


def collect_body(step1_ref, step2_ref, out_ref):
    odd = (lax.axis_index("x") & 1) == 1
    for h in range(NH // 2):
        out_ref[0, h] = jnp.where(odd, step1_ref[h], jnp.float32(0.0))
        out_ref[1, h] = step2_ref[h]


def add_body(a_ref, b_ref, out_ref):
    out_ref[...] = a_ref[...] + b_ref[...]


def add_odd_body(a_ref, b_ref, out_ref):
    odd = (lax.axis_index("x") & 1) == 1
    out_ref[...] = jnp.where(odd, a_ref[...], jnp.float32(0.0)) + b_ref[...]


def owner_forward_body(in_ref, out_ref):
    sums = []
    for z in range(8):
        total = in_ref[8 * z]
        for p in range(1, 8):
            total = total + in_ref[8 * z + p]
        sums.append(total)
    nothing = jnp.zeros((8, HD), F32)
    pair0 = sums[0] + sums[1]
    pair2 = sums[4] + sums[5]
    four = pair0 + (sums[2] + sums[3])
    for z in range(8):
        first = sums[z - 1] if z & 1 else nothing
        second = (pair2 if z & 4 else pair0) if z & 2 else nothing
        third = four if z & 4 else nothing
        for x in range(4):
            out_ref[4 * z + x, 0] = first
            out_ref[4 * z + x, 1] = second
            out_ref[4 * z + x, 2] = third


def attend_body(pc_ref, lw_ref, mixed_ref, qt_ref, att_ref, st_ref, pay_ref):
    squares = jnp.zeros((HD, TOK), F32)
    inner = jnp.zeros((HD, TOK), F32)
    for h in range(NH):
        tiles = []
        for m in range(PLANE):
            for i in range(16):
                tiles.append(pc_ref[i % 2, 8 * h + i // 2, m])
        states = jnp.concatenate(tiles, axis=0).astype(BF16)
        st_ref[h] = states
        sq = scaled_queries(qt_ref[h].astype(F32), lw_ref, 1, h)
        att = mixed_ref[h, 0] + dot(states, sq, 0, 0)
        att_ref[h] = att
        squares = squares + att * att
        inner = inner + mixed_ref[h, 1] * att
    squares = jnp.sum(squares, axis=0, keepdims=True)
    inner = jnp.sum(inner, axis=0, keepdims=True)
    rows = [squares[:, :HD], squares[:, HD:], inner[:, :HD], inner[:, HD:]]
    tile = jnp.concatenate(rows + [jnp.zeros((4, HD), F32)], axis=0)
    for peer in range(8):
        pay_ref[peer] = tile


def token_rows(recv_ref):
    total = recv_ref[0]
    for peer in range(1, 8):
        total = total + recv_ref[peer]
    inv = lax.rsqrt(total[0:2] / WIDTH + EPS)
    coef = inv * inv * inv * total[2:4] / WIDTH
    inv_row = jnp.concatenate([inv[0:1], inv[1:2]], axis=1)
    coef_row = jnp.concatenate([coef[0:1], coef[1:2]], axis=1)
    return inv_row, coef_row


def grad_body(
    recv_ref, lw_ref, att_ref, mixed_ref, qt_ref, own_ref, send_ref, keep_ref, give_ref
):
    first = lax.axis_index("core") == 0
    inv_row, coef_row = token_rows(recv_ref)
    for h in range(NH):
        go = (inv_row * mixed_ref[h, 1] - att_ref[h] * coef_row).astype(BF16)
        q_t = qt_ref[h].astype(F32)
        states = dot(scaled_queries(q_t, lw_ref, 1, h), go, 1, 1)
        for m in range(PLANE):
            for k in range(8):
                row = m * HD + 16 * k
                even = states[row : row + 8]
                odd = states[row + 8 : row + 16]
                own_ref[8 * h + k, m] = jnp.where(first, even, odd)
                send_ref[8 * h + k, m] = jnp.where(first, odd, even)
        states = dot(scaled_queries(q_t, lw_ref, 0, h), go, 1, 1)
        mine = first if h < NH // 2 else jnp.logical_not(first)
        for m in range(PLANE):
            value = states[m * HD : (m + 1) * HD]

            @pl.when(mine)
            def _keep(value=value, m=m, h=h):
                keep_ref[m, h % 2] = value

            @pl.when(jnp.logical_not(mine))
            def _give(value=value, m=m, h=h):
                give_ref[m, h % 2] = value


def pair_body(own_ref, gath_ref, out_ref):
    other = 1 - lax.axis_index("core")
    out_ref[...] = own_ref[...] + gath_ref[other]


def join_body(keep_ref, gath_ref, first_ref, second_ref):
    other = 1 - lax.axis_index("core")
    for h in range(NH // 2):
        first_ref[h] = keep_ref[1, h] + gath_ref[other, 1, h]
        second_ref[h] = keep_ref[2, h] + gath_ref[other, 2, h]


def merge_body(back1_ref, back2_ref, keep_ref, gath_ref, mine_ref, send_ref):
    first = lax.axis_index("core") == 0
    zero = jnp.float32(0.0)
    for h in range(NH // 2):
        total = back1_ref[h] + back2_ref[h]
        mine_ref[h] = total + jnp.where(first, gath_ref[1, 0, h], zero)
        send_ref[h] = total + jnp.where(first, zero, keep_ref[0, h])


def owner_backward_body(in_ref, out_ref):
    grads = []
    for m in range(PLANE):
        rows = []
        for z in range(8):
            total = in_ref[4 * z, m]
            for x in range(1, 4):
                total = total + in_ref[4 * z + x, m]
            rows.append(total)
        grads.append(rows)
    pair2 = grads[1][2] + grads[1][3]
    pair6 = grads[1][6] + grads[1][7]
    four = (grads[2][4] + grads[2][5]) + (grads[2][6] + grads[2][7])
    for z in range(8):
        total = jnp.zeros((8, HD), F32)
        if not z & 1:
            total = total + grads[0][z + 1]
        if not z & 2:
            total = total + (pair6 if z & 4 else pair2)
        if not z & 4:
            total = total + four
        for p in range(8):
            out_ref[8 * z + p] = total


def back_body(
    recv_ref, gain_ref, lw_ref, q_ref, k_ref, v_ref, mixed_ref, att_ref, low_ref, high_ref,
    nm_ref, gq_ref, gk_ref, gv_ref, gl_ref,
):
    level = level_masks()
    inv_row, coef_row = token_rows(recv_ref)

    def step(h):
        q, k, att = q_ref[h], k_ref[h], att_ref[h]
        go = (inv_row * mixed_ref[h] - att * coef_row).astype(BF16)
        nm_ref[h] = ((att * inv_row).T * gain_ref[h : h + 1, :]).astype(BF16)
        scores = dot(k, q, 1, 1)
        weights = near_weights(lw_ref, level, h)
        mix = dot(v_ref[h], go, 1, 0)
        gv_ref[h] = dot((weights * scores).astype(BF16), go, 1, 1)
        grad_scores = (weights * mix).astype(BF16)
        gk_ref[h] = dot(grad_scores, q, 1, 0)
        product = mix * scores
        rows = []
        for number in range(LOCAL):
            picked = jnp.where(level == number, product, jnp.float32(0.0))
            rows.append(level_scale(number) * jnp.sum(picked, axis=0, keepdims=True))
        q_t = q.astype(F32).T
        far_t = dot(k, grad_scores, 0, 0)
        for part, states_ref in enumerate((low_ref, high_ref)):
            turned = dot(states_ref[h], go, 1, 0)
            for m in range(PLANE):
                piece = turned[m * HD : (m + 1) * HD]
                number = LOCAL + part * PLANE + m
                far_t = far_t + level_row(lw_ref, number, h) * piece
                rows.append(level_scale(number) * jnp.sum(piece * q_t, axis=0, keepdims=True))
        gq_ref[h] = far_t.T.astype(BF16)
        for number in range(LOCAL + FAR):
            gl_ref[number, h : h + 1, :] = rows[number]

    return step


def final_body(piece_ref, mine_ref, wide_ref, k_ref, v_ref, gk_ref, gv_ref, outk_ref, outv_ref):
    first = lax.axis_index("core") == 0

    def step(h):
        mine = first if h < NH // 2 else jnp.logical_not(first)
        plane = jnp.where(mine, mine_ref[h % 2], wide_ref[h // 2, h % 2])
        grad_kv = (piece_ref[h] + plane).astype(BF16)
        outk_ref[h] = (gk_ref[h] + dot(v_ref[h], grad_kv, 1, 1)).astype(BF16)
        outv_ref[h] = (gv_ref[h] + dot(k_ref[h], grad_kv, 1, 0)).astype(BF16)

    return step


def swap(value, axes):
    return lax.all_to_all(value, axes, split_axis=0, concat_axis=0, tiled=True)


def both_cores(value):
    return lax.all_gather(value, "core", axis=0, tiled=False)


def shards(queries, key_rows, value_rows, level_weights, norm_gain, grad_normed):
    rates = jnp.transpose(level_weights, (1, 0, 2))
    (kv,) = call(
        key_value_body, [(MATRIX, F32)], (key_rows, value_rows), 2**25, MIB, (0, 1), (), ALONE
    )
    owned = swap(kv.reshape(64, 8, HD), CTX)
    both = both_cores(kv)
    (pair,) = call(half_body, [(HALF, F32)], (both,), 2**16, MIB)
    step1 = lax.ppermute(pair, "x", [(0, 1), (1, 0), (2, 3), (3, 2)])
    owned, step1 = lax.optimization_barrier((owned, step1))
    (outgoing,) = call(owner_forward_body, [(PIECES, F32)], (owned,), 2**17, MIB // 2)
    arrived = swap(outgoing, ROWS)
    (twice,) = call(add_body, [(HALF, F32)], (pair, step1), 2**16, MIB, after=(outgoing,))
    step2 = lax.ppermute(twice, "x", [(0, 3), (1, 2)])
    (wide,) = call(
        collect_body,
        [((2,) + HALF, F32)],
        (step1, step2),
        2**16,
        MIB,
    )
    mixed, low, q_turned = call(
        near_body,
        [((NH, 2, HD, TOK), F32), (STACKED, BF16), (TURNED, BF16)],
        (
            rates, norm_gain, both_cores(wide), both, queries, key_rows, value_rows, grad_normed,
        ),
        2**28,
        4 * MIB,
        tuple(range(8)),
        tuple(range(3)),
        ALONE,
        views={3: (MATRIX, lambda ref: ref.at[0])},
    )
    attended, high, payload = call(
        attend_body,
        [(TURNED, F32), (STACKED, BF16), ((8, 8, HD), F32)],
        (both_cores(arrived), rates, mixed, q_turned),
        2**27,
        4 * MIB,
    )
    sums = swap(payload, "heads")
    own, send, keep, give = call(
        grad_body,
        [
            (PIECES, F32),
            (PIECES, F32),
            ((PLANE,) + HALF, F32),
            ((PLANE,) + HALF, F32),
        ],
        (sums, rates, attended, mixed, q_turned),
        2**28,
        6 * MIB,
    )
    (joined,) = call(pair_body, [(PIECES, F32)], (own, both_cores(send)), 2**17, 3 * MIB // 2)
    returned = swap(joined, ROWS)
    given = both_cores(give)
    first, second = call(join_body, [(HALF, F32), (HALF, F32)], (keep, given), 2**17, MIB)
    back2 = lax.ppermute(second, "x", [(3, 0), (2, 1)])
    normed, grad_q, near_k, near_v, grad_rates = call(
        back_body,
        [(TOKENS, BF16), (TOKENS, BF16), (TOKENS, F32), (TOKENS, F32), ((LOCAL + FAR, NH, TOK), F32)],
        (
            sums, norm_gain, rates, queries, key_rows, value_rows, mixed, attended, low, high,
        ),
        2**28,
        5 * MIB,
        tuple(range(10)),
        tuple(range(5)),
        ALONE,
        views={6: (TURNED, lambda ref: ref.at[:, 1])},
    )
    returned, back2 = lax.optimization_barrier((returned, back2))
    (spread,) = call(owner_backward_body, [((64, 8, HD), F32)], (returned,), 2**17, MIB // 2)
    total = swap(spread, CTX).reshape(MATRIX)
    (onward,) = call(add_odd_body, [(HALF, F32)], (first, back2), 2**16, MIB, after=(spread,))
    back1 = lax.ppermute(onward, "x", [(0, 1), (1, 0), (3, 2)])
    mine, theirs = call(
        merge_body, [(HALF, F32), (HALF, F32)], (back1, back2, keep, given), 2**16, MIB
    )
    grad_k, grad_v = call(
        final_body,
        [(TOKENS, BF16), (TOKENS, BF16)],
        (total, mine, both_cores(theirs), key_rows, value_rows, near_k, near_v),
        2**26,
        3 * MIB,
    )
    return normed, grad_q, grad_k, grad_v, jnp.transpose(grad_rates, (1, 0, 2))


def solution(mesh):
    grid = Mesh(mesh.devices.reshape(8, 8, 4, 2), ("heads",) + CTX)
    rows = P("heads", CTX, None)
    rates = P("heads", None, CTX)
    return jax.shard_map(
        shards,
        mesh=grid,
        in_specs=(rows, rows, rows, rates, P("heads", None), rows),
        out_specs=(rows, rows, rows, rows, rates),
        check_vma=False,
    )
```

time: 141 us -> 124 us (0.88)
  starting transfers between devices: 11.9 us -> 49 us
  blocking collectives: 67.3 us -> 31.6 us
  local copies, waits for them, and re-layouts: 21.5 us -> 1.73 us
  between operations: 14.2 us -> 0.86 us
  waiting for transfers between devices: 13.3 us -> 23.2 us
  Pallas kernels: 11.7 us -> 16.5 us
    all_to_all x3 -> x1, blocking collectives: 59.2 us -> 13.5 us  [swap(): return lax.all_to_all(value, axes, split_axis=0, concat_axis=0, tiled=True)]
    all_to_all x2 -> x4, starting transfers between devices: 11.8 us -> 36.9 us  [swap(): return lax.all_to_all(value, axes, split_axis=0, concat_axis=0, tiled=True)]
    unnamed x66 -> x26, local copies, waits for them, and re-layouts: 21.5 us -> 1.73 us
    ppermute x0 -> x4, waiting for transfers between devices: none -> 18.1 us  [the longest x1 9.08 us: shards(): back2 = lax.ppermute(second, 'x', [(3, 0), (2, 1)])]
    ppermute x0 -> x4, starting transfers between devices: none -> 12.2 us  [the longest x1 4.35 us: shards(): step2 = lax.ppermute(twice, 'x', [(0, 3), (1, 2)])]
    all_gather x2 -> x6, blocking collectives: 8.13 us -> 18.1 us  [both_cores(): return lax.all_gather(value, 'core', axis=0, tiled=False)]
    all_to_all x2 -> x4, waiting for transfers between devices: 13.2 us -> 5.1 us  [swap(): return lax.all_to_all(value, axes, split_axis=0, concat_axis=0, tiled=True)]
    pallas_call x10 -> x15, Pallas kernels: 11.7 us -> 16.5 us  [call(): pl.pallas_call(wrapped, out_shape=[jax.ShapeDtypeStruct(s, d) for s, d in...]
  transfers between devices with their start and end apart: 4 -> 8, of which waited for: 2 -> 7; matrix products, arithmetic and copies ran while one was open for 0% -> 0% of each run, Pallas kernels for 4% -> 7%
where the time goes in v2:
time: 124 us; the launch traced here: 123 us
  starting transfers between devices  49 us (40%)
  blocking collectives  31.6 us (25%)
  waiting for transfers between devices  23.2 us (19%)
  Pallas kernels  16.5 us (13%)
  local copies, waits for them, and re-layouts  1.73 us (1%)
    all_to_all x4, starting transfers between devices, swap(): return lax.all_to_all(value, axes, split_axis=0, concat_axis=0, tiled=True)  36.9 us
    all_gather x6, blocking collectives, both_cores(): return lax.all_gather(value, 'core', axis=0, tiled=False)  18.1 us
    pallas_call x15, Pallas kernels, call(): pl.pallas_call(wrapped, out_shape=[jax.ShapeDtypeStruct(s, d) for s, d in...  16.5 us
    all_to_all x1, blocking collectives, swap(): return lax.all_to_all(value, axes, split_axis=0, concat_axis=0, tiled=True)  13.5 us
    ppermute x1, waiting for transfers between devices, shards(): back2 = lax.ppermute(second, 'x', [(3, 0), (2, 1)])  9.08 us
    all_to_all x4, waiting for transfers between devices, swap(): return lax.all_to_all(value, axes, split_axis=0, concat_axis=0, tiled=True)  5.1 us
    ppermute x1, waiting for transfers between devices, shards(): step1 = lax.ppermute(pair, 'x', [(0, 1), (1, 0), (2, 3), (3, 2)])  5.06 us
    ppermute x1, starting transfers between devices, shards(): step2 = lax.ppermute(twice, 'x', [(0, 3), (1, 2)])  4.35 us
  transfers between devices with their start and end apart: 8, of which 7 were waited for; matrix products, arithmetic and copies ran while one was open for 0% of the time, Pallas kernels for 7%

profile of v2, /device:TPU:1, one launch (start us, length us, event | category | flops | bytes accessed | tf_op | source)
XLA Modules:
  0.0 123.0 jit_solution(6327687140262604322)
XLA Ops:
  0.6 2.5 %shard_map.101 = f32[4,128,128]{2,1,0:T(8,128)} custom-call(bf16[4,256,128]{2,1,0:T(8,128)(2,1)} %refs_3_.3, bf16[4,256,128]{2,1,0:T(8,128)(2,1)} %refs_4_.5), custom_call_target="tpu_custom_call" | custom-call | flops 33554432 | bytes 1048576 | tf_op jit(solution)/shard_map/pallas_call | solution.py:108
  3.1 15.0 %all-to-all-start = ((f32[64,8,128]{2,1,0:T(8,128)}), f32[64,8,128]{2,1,0:T(8,128)S(1)}, u32[]{:S(2)}, u32[]{:S(2)}) async-start(f32[64,8,128]{2,1,0:T(8,128)} %bitcast.22), calls=%async_computation | async-start | bytes 524288 | tf_op jit(solution)/shard_map/all_to_all | solution.py:382
  18.1 2.3 %all-gather = f32[8,128,128]{2,1,0:T(8,128)S(1)} all-gather(f32[4,128,128]{2,1,0:T(8,128)S(1)} %copy-done.12), channel_id=2, replica_groups=mesh['heads'=8,'z'=8,'x'=4,'core'=2] {'core'}, dimensions={0}, use_global_device_ids=true | all-gather | bytes 786432 | tf_op jit(solution)/shard_map/all_gather | solution.py:386
  20.4 3.2 %collective-permute-start = (f32[2,128,128]{2,1,0:T(8,128)S(1)}, f32[2,128,128]{2,1,0:T(8,128)S(1)}, u32[]{:S(2)}, u32[]{:S(2)}) collective-permute-start(f32[2,128,128]{2,1,0:T(8,128)S(1)} %shard_map.102.refs_0_), channel_id=1, source_target_pairs={{0,2},{2,0},{4,6},{6,4},{1,3},{3,1},{5,7},{7,5},{8,10},{10,8},{12,... | collective-permute-start | bytes 393224 | tf_op jit(solution)/shard_map/ppermute | solution.py:397
  23.6 5.1 %collective-permute-done.refs_1_.refs_0_ = f32[2,128,128]{2,1,0:T(8,128)S(1)} collective-permute-done((f32[2,128,128]{2,1,0:T(8,128)S(1)}, f32[2,128,128]{2,1,0:T(8,128)S(1)}, u32[]{:S(2)}, u32[]{:S(2)}) %collective-permute-start) | collective-permute-done | bytes 131104 | tf_op jit(solution)/shard_map/ppermute | solution.py:397
  28.7 2.6 %all-to-all-done.refs_0_ = f32[64,8,128]{2,1,0:T(8,128)S(1)} async-done(((f32[64,8,128]{2,1,0:T(8,128)}), f32[64,8,128]{2,1,0:T(8,128)S(1)}, u32[]{:S(2)}, u32[]{:S(2)}) %all-to-all-start) | async-done | bytes 262176 | tf_op jit(solution)/shard_map/all_to_all | solution.py:382
  32.0 5.7 %all-to-all-start.1 = ((f32[32,3,8,128]{3,2,1,0:T(8,128)}), f32[32,3,8,128]{3,2,1,0:T(8,128)S(1)}, u32[]{:S(2)}, u32[]{:S(2)}) async-start(f32[32,3,8,128]{3,2,1,0:T(8,128)} %shard_map.103.refs_2_), calls=%async_computation.1 | async-start | bytes 786432 | tf_op jit(solution)/shard_map/all_to_all | solution.py:382
  37.7 4.4 %collective-permute-start.1 = (f32[2,128,128]{2,1,0:T(8,128)S(1)}, f32[2,128,128]{2,1,0:T(8,128)S(1)}, u32[]{:S(2)}, u32[]{:S(2)}) collective-permute-start(f32[2,128,128]{2,1,0:T(8,128)S(1)} %shard_map.104), channel_id=1, source_target_pairs={{0,6},{2,4},{1,7},{3,5},{8,14},{10,12},{9,15},{11,13},{16,22},{18,... | collective-permute-start | bytes 393224 | tf_op jit(solution)/shard_map/ppermute | solution.py:402
  42.1 3.7 %collective-permute-done.1.refs_1_ = f32[2,128,128]{2,1,0:T(8,128)S(1)} collective-permute-done((f32[2,128,128]{2,1,0:T(8,128)S(1)}, f32[2,128,128]{2,1,0:T(8,128)S(1)}, u32[]{:S(2)}, u32[]{:S(2)}) %collective-permute-start.1) | collective-permute-done | bytes 131104 | tf_op jit(solution)/shard_map/ppermute | solution.py:402
  45.9 4.2 %all-gather.2 = f32[4,2,128,128]{3,2,1,0:T(8,128)} all-gather(f32[2,2,128,128]{3,2,1,0:T(8,128)S(1)} %shard_map.105), channel_id=4, replica_groups=mesh['heads'=8,'z'=8,'x'=4,'core'=2] {'core'}, dimensions={0}, use_global_device_ids=true | all-gather | bytes 786432 | tf_op jit(solution)/shard_map/all_gather | solution.py:386
  50.1 3.8 %shard_map.106 = (f32[4,2,128,256]{3,2,1,0:T(8,128)}, bf16[4,384,128]{2,1,0:T(8,128)(2,1)}, bf16[4,128,256]{2,1,0:T(8,128)(2,1)}) custom-call(f32[15,4,256]{2,1,0:T(4,128)} %bitcast.18, f32[4,128]{1,0:T(4,128)} %refs_1_.5, f32[2,2,2,128,128]{4,3,2,1,0:T(8,128)} %bitcast.23, f32[2,4,128,128]{3,2,1,0:T(8,128)} %bitcast.13, bf16[4,256,128]{2,1,0:T(8,128)(2,1)} %refs_3_.2, ...), custom_call_target="tpu_custom_call" | custom-call | flops 268435456 | bytes 4194304 | tf_op jit(solution)/shard_map/pallas_call | solution.py:108
  54.0 2.5 %all-gather.1 = f32[64,3,8,128]{3,2,1,0:T(8,128)S(1)} all-gather(f32[32,3,8,128]{3,2,1,0:T(8,128)S(1)} %all-to-all-done.1), channel_id=3, replica_groups=mesh['heads'=8,'z'=8,'x'=4,'core'=2] {'core'}, dimensions={0}, use_global_device_ids=true | all-gather | bytes 1179648 | tf_op jit(solution)/shard_map/all_gather | solution.py:386
  58.5 13.5 %all_to_all.25.refs_0_ = f32[8,8,128]{2,1,0:T(8,128)S(1)} all-to-all(f32[8,8,128]{2,1,0:T(8,128)S(1)} %get-tuple-element.34), channel_id=1, replica_groups=mesh['heads'=8,'z'=8,'x'=4,'core'=2] {'heads'}, dimensions={0} | all-to-all | bytes 65536 | tf_op jit(solution)/shard_map/all_to_all | solution.py:382
  72.1 1.2 shard_map.109
  73.3 3.7 %all-gather.3 = f32[64,3,8,128]{3,2,1,0:T(8,128)S(1)} all-gather(f32[32,3,8,128]{3,2,1,0:T(8,128)S(1)} %get-tuple-element.41), channel_id=5, replica_groups=mesh['heads'=8,'z'=8,'x'=4,'core'=2] {'core'}, dimensions={0}, use_global_device_ids=true | all-gather | bytes 1179648 | tf_op jit(solution)/shard_map/all_gather | solution.py:386
  77.8 9.3 %all-to-all-start.3 = ((f32[32,3,8,128]{3,2,1,0:T(8,128)}), f32[32,3,8,128]{3,2,1,0:T(8,128)S(1)}, u32[]{:S(2)}, u32[]{:S(2)}) async-start(f32[32,3,8,128]{3,2,1,0:T(8,128)} %shard_map.110), calls=%async_computation.3 | async-start | bytes 786432 | tf_op jit(solution)/shard_map/all_to_all | solution.py:382
  87.1 2.6 %all-gather.4 = f32[6,2,128,128]{3,2,1,0:T(8,128)S(1)} all-gather(f32[3,2,128,128]{3,2,1,0:T(8,128)S(1)} %get-tuple-element.43), channel_id=6, replica_groups=mesh['heads'=8,'z'=8,'x'=4,'core'=2] {'core'}, dimensions={0}, use_global_device_ids=true | all-gather | bytes 1179648 | tf_op jit(solution)/shard_map/all_gather | solution.py:386
  89.8 1.3 %collective-permute-start.2 = (f32[2,128,128]{2,1,0:T(8,128)S(1)}, f32[2,128,128]{2,1,0:T(8,128)S(1)}, u32[]{:S(2)}, u32[]{:S(2)}) collective-permute-start(f32[2,128,128]{2,1,0:T(8,128)S(1)} %get-tuple-element.44), channel_id=1, source_target_pairs={{6,0},{4,2},{7,1},{5,3},{14,8},{12,10},{15,9},{13,11},{22,16},{20,... | collective-permute-start | bytes 393224 | tf_op jit(solution)/shard_map/ppermute | solution.py:447
  91.1 9.1 %collective-permute-done.2.refs_1_ = f32[2,128,128]{2,1,0:T(8,128)S(1)} collective-permute-done((f32[2,128,128]{2,1,0:T(8,128)S(1)}, f32[2,128,128]{2,1,0:T(8,128)S(1)}, u32[]{:S(2)}, u32[]{:S(2)}) %collective-permute-start.2) | collective-permute-done | bytes 131104 | tf_op jit(solution)/shard_map/ppermute | solution.py:447
  101.7 7.0 %all-to-all-start.4 = ((f32[64,8,128]{2,1,0:T(8,128)}), f32[64,8,128]{2,1,0:T(8,128)S(1)}, u32[]{:S(2)}, u32[]{:S(2)}) async-start(f32[64,8,128]{2,1,0:T(8,128)} %shard_map.112.refs_2_), calls=%async_computation.4 | async-start | bytes 524288 | tf_op jit(solution)/shard_map/all_to_all | solution.py:382
  108.7 3.3 %collective-permute-start.3 = (f32[2,128,128]{2,1,0:T(8,128)S(1)}, f32[2,128,128]{2,1,0:T(8,128)S(1)}, u32[]{:S(2)}, u32[]{:S(2)}) collective-permute-start(f32[2,128,128]{2,1,0:T(8,128)S(1)} %shard_map.113), channel_id=1, source_target_pairs={{0,2},{2,0},{6,4},{1,3},{3,1},{7,5},{8,10},{10,8},{14,12},{9,11},{... | collective-permute-start | bytes 393224 | tf_op jit(solution)/shard_map/ppermute | solution.py:465
  112.0 5.1 %shard_map.108 = (bf16[4,256,128]{2,1,0:T(8,128)(2,1)}, bf16[4,256,128]{2,1,0:T(8,128)(2,1)}, f32[4,256,128]{2,1,0:T(8,128)}, f32[4,256,128]{2,1,0:T(8,128)}, f32[15,4,256]{2,1,0:T(4,128)}) custom-call(f32[8,8,128]{2,1,0:T(8,128)} %copy-done.11, f32[4,128]{1,0:T(4,128)} %refs_1_.5, f32[15,4,256]{2,1,0:T(4,128)} %bitcast.19, bf16[4,256,128]{2,1,0:T(8,128)(2,1)} %refs_3_.2, ...), custom_call_target="tpu_custom_call" | custom-call | flops 268435456 | bytes 5242880 | tf_op jit(solution)/shard_map/pallas_call | solution.py:108
  117.5 2.7 %all-gather.5 = f32[4,128,128]{2,1,0:T(8,128)S(1)} all-gather(f32[2,128,128]{2,1,0:T(8,128)S(1)} %get-tuple-element.49), channel_id=7, replica_groups=mesh['heads'=8,'z'=8,'x'=4,'core'=2] {'core'}, dimensions={0}, use_global_device_ids=true | all-gather | bytes 393216 | tf_op jit(solution)/shard_map/all_gather | solution.py:386
  120.2 1.7 %all-to-all-done.4 = f32[64,8,128]{2,1,0:T(8,128)S(1)} async-done(((f32[64,8,128]{2,1,0:T(8,128)}), f32[64,8,128]{2,1,0:T(8,128)S(1)}, u32[]{:S(2)}, u32[]{:S(2)}) %all-to-all-start.4) | async-done | bytes 262176 | tf_op jit(solution)/shard_map/all_to_all | solution.py:382
  (40 shorter events, 6.7 us)
Async XLA Ops:
  3.1 15.0 %copy-start.12 = (f32[4,128,128]{2,1,0:T(8,128)S(1)}, f32[4,128,128]{2,1,0:T(8,128)}, u32[]{:S(2)}) copy-start(f32[4,128,128]{2,1,0:T(8,128)} %shard_map.101) | copy-start | bytes 786436
  3.1 28.2 %all-to-all-start = ((f32[64,8,128]{2,1,0:T(8,128)}), f32[64,8,128]{2,1,0:T(8,128)S(1)}, u32[]{:S(2)}, u32[]{:S(2)}) async-start(f32[64,8,128]{2,1,0:T(8,128)} %bitcast.22), calls=%async_computation | async-start | bytes 524288 | tf_op jit(solution)/shard_map/all_to_all | solution.py:382
  20.4 11.7 %copy-start.1 = (f32[8,128,128]{2,1,0:T(8,128)}, f32[8,128,128]{2,1,0:T(8,128)S(1)}, u32[]{:S(2)}) copy-start(f32[8,128,128]{2,1,0:T(8,128)S(1)} %all-gather) | copy-start | bytes 1572868
  20.4 8.3 %collective-permute-start = (f32[2,128,128]{2,1,0:T(8,128)S(1)}, f32[2,128,128]{2,1,0:T(8,128)S(1)}, u32[]{:S(2)}, u32[]{:S(2)}) collective-permute-start(f32[2,128,128]{2,1,0:T(8,128)S(1)} %shard_map.102.refs_0_), channel_id=1, source_target_pairs={{0,2},{2,0},{4,6},{6,4},{1,3},{3,1},{5,7},{7,5},{8,10},{10,8},{12,... | collective-permute-start | bytes 393224 | tf_op jit(solution)/shard_map/ppermute | solution.py:397
  32.0 21.9 %all-to-all-start.1 = ((f32[32,3,8,128]{3,2,1,0:T(8,128)}), f32[32,3,8,128]{3,2,1,0:T(8,128)S(1)}, u32[]{:S(2)}, u32[]{:S(2)}) async-start(f32[32,3,8,128]{3,2,1,0:T(8,128)} %shard_map.103.refs_2_), calls=%async_computation.1 | async-start | bytes 786432 | tf_op jit(solution)/shard_map/all_to_all | solution.py:382
  37.7 8.1 %collective-permute-start.1 = (f32[2,128,128]{2,1,0:T(8,128)S(1)}, f32[2,128,128]{2,1,0:T(8,128)S(1)}, u32[]{:S(2)}, u32[]{:S(2)}) collective-permute-start(f32[2,128,128]{2,1,0:T(8,128)S(1)} %shard_map.104), channel_id=1, source_target_pairs={{0,6},{2,4},{1,7},{3,5},{8,14},{10,12},{9,15},{11,13},{16,22},{18,... | collective-permute-start | bytes 393224 | tf_op jit(solution)/shard_map/ppermute | solution.py:402
  53.9 2.5 %copy-start = (f32[4,2,128,256]{3,2,1,0:T(8,128)S(1)}, f32[4,2,128,256]{3,2,1,0:T(8,128)}, u32[]{:S(2)}) copy-start(f32[4,2,128,256]{3,2,1,0:T(8,128)} %get-tuple-element.32.refs_2_.refs_6_.refs_3_) | copy-start | bytes 3145732
  53.9 2.5 %copy-start.7 = (f32[4,15,256]{2,0,1:T(4,128)S(1)}, f32[4,15,256]{2,0,1:T(4,128)}, u32[]{:S(2)}) copy-start(f32[4,15,256]{2,0,1:T(4,128)} %param.9) | copy-start | bytes 184324
  56.5 1.0 copy-start.5
  57.4 14.7 %copy-start.6 = (bf16[4,128,256]{2,1,0:T(8,128)(2,1)S(1)}, bf16[4,128,256]{2,1,0:T(8,128)(2,1)}, u32[]{:S(2)}) copy-start(bf16[4,128,256]{2,1,0:T(8,128)(2,1)} %get-tuple-element.33.refs_3_.refs_4_) | copy-start | bytes 786436
  57.8 0.7 copy-start.10
  58.5 14.7 %copy-start.4 = (f32[4,128,256]{2,1,0:T(8,128)}, f32[4,128,256]{2,1,0:T(8,128)S(1)}, u32[]{:S(2)}) copy-start(f32[4,128,256]{2,1,0:T(8,128)S(1)} %get-tuple-element.35.refs_7_.refs_2_) | copy-start | bytes 1572868
  72.1 1.2 copy-start.11
  77.8 23.2 %all-to-all-start.3 = ((f32[32,3,8,128]{3,2,1,0:T(8,128)}), f32[32,3,8,128]{3,2,1,0:T(8,128)S(1)}, u32[]{:S(2)}, u32[]{:S(2)}) async-start(f32[32,3,8,128]{3,2,1,0:T(8,128)} %shard_map.110), calls=%async_computation.3 | async-start | bytes 786432 | tf_op jit(solution)/shard_map/all_to_all | solution.py:382
  89.8 10.4 %collective-permute-start.2 = (f32[2,128,128]{2,1,0:T(8,128)S(1)}, f32[2,128,128]{2,1,0:T(8,128)S(1)}, u32[]{:S(2)}, u32[]{:S(2)}) collective-permute-start(f32[2,128,128]{2,1,0:T(8,128)S(1)} %get-tuple-element.44), channel_id=1, source_target_pairs={{6,0},{4,2},{7,1},{5,3},{14,8},{12,10},{15,9},{13,11},{22,16},{20,... | collective-permute-start | bytes 393224 | tf_op jit(solution)/shard_map/ppermute | solution.py:447
  101.7 20.1 %all-to-all-start.4 = ((f32[64,8,128]{2,1,0:T(8,128)}), f32[64,8,128]{2,1,0:T(8,128)S(1)}, u32[]{:S(2)}, u32[]{:S(2)}) async-start(f32[64,8,128]{2,1,0:T(8,128)} %shard_map.112.refs_2_), calls=%async_computation.4 | async-start | bytes 524288 | tf_op jit(solution)/shard_map/all_to_all | solution.py:382
  108.7 8.7 %collective-permute-start.3 = (f32[2,128,128]{2,1,0:T(8,128)S(1)}, f32[2,128,128]{2,1,0:T(8,128)S(1)}, u32[]{:S(2)}, u32[]{:S(2)}) collective-permute-start(f32[2,128,128]{2,1,0:T(8,128)S(1)} %shard_map.113), channel_id=1, source_target_pairs={{0,2},{2,0},{6,4},{1,3},{3,1},{7,5},{8,10},{10,8},{14,12},{9,11},{... | collective-permute-start | bytes 393224 | tf_op jit(solution)/shard_map/ppermute | solution.py:465
  117.4 4.5 %copy-start.3 = (bf16[4,256,128]{2,1,0:T(8,128)(2,1)S(1)}, bf16[4,256,128]{2,1,0:T(8,128)(2,1)}, u32[]{:S(2)}) copy-start(bf16[4,256,128]{2,1,0:T(8,128)(2,1)} %refs_4_.5) | copy-start | bytes 786436
  117.4 4.5 %copy-start.8 = (f32[4,256,128]{2,1,0:T(8,128)S(1)}, f32[4,256,128]{2,1,0:T(8,128)}, u32[]{:S(2)}) copy-start(f32[4,256,128]{2,1,0:T(8,128)} %get-tuple-element.50.refs_5_) | copy-start | bytes 1572868
  117.4 4.5 %copy-start.9 = (f32[4,256,128]{2,1,0:T(8,128)S(1)}, f32[4,256,128]{2,1,0:T(8,128)}, u32[]{:S(2)}) copy-start(f32[4,256,128]{2,1,0:T(8,128)} %get-tuple-element.51.refs_6_) | copy-start | bytes 1572868
  117.4 4.4 %copy-start.2 = (bf16[4,256,128]{2,1,0:T(8,128)(2,1)S(1)}, bf16[4,256,128]{2,1,0:T(8,128)(2,1)}, u32[]{:S(2)}) copy-start(bf16[4,256,128]{2,1,0:T(8,128)(2,1)} %refs_3_.3) | copy-start | bytes 786436

commit v3 on v2

--- a/solution.py
+++ b/solution.py
@@ -217,18 +217,23 @@
             out_ref[4 * z + x, 2] = third
 
 
-def attend_body(pc_ref, lw_ref, mixed_ref, qt_ref, att_ref, st_ref, pay_ref):
+def far_states(pc_ref, h):
+    tiles = []
+    for m in range(PLANE):
+        for i in range(16):
+            tiles.append(pc_ref[i % 2, 8 * h + i // 2, m])
+    return jnp.concatenate(tiles, axis=0).astype(BF16)
+
+
+def attend_body(pc_ref, lw_ref, q_ref, mixed_ref, att_ref, pay_ref):
     squares = jnp.zeros((HD, TOK), F32)
     inner = jnp.zeros((HD, TOK), F32)
     for h in range(NH):
-        tiles = []
+        states = far_states(pc_ref, h)
+        att = mixed_ref[h, 0]
         for m in range(PLANE):
-            for i in range(16):
-                tiles.append(pc_ref[i % 2, 8 * h + i // 2, m])
-        states = jnp.concatenate(tiles, axis=0).astype(BF16)
-        st_ref[h] = states
-        sq = scaled_queries(qt_ref[h].astype(F32), lw_ref, 1, h)
-        att = mixed_ref[h, 0] + dot(states, sq, 0, 0)
+            far = dot(states[m * HD : (m + 1) * HD], q_ref[h], 0, 1)
+            att = att + level_row(lw_ref, LOCAL + PLANE + m, h) * far
         att_ref[h] = att
         squares = squares + att * att
         inner = inner + mixed_ref[h, 1] * att
@@ -328,7 +333,7 @@
 
 
 def back_body(
-    recv_ref, gain_ref, lw_ref, q_ref, k_ref, v_ref, mixed_ref, att_ref, low_ref, high_ref,
+    recv_ref, gain_ref, lw_ref, q_ref, k_ref, v_ref, mixed_ref, att_ref, low_ref, pc_ref,
     nm_ref, gq_ref, gk_ref, gv_ref, gl_ref,
 ):
     level = level_masks()
@@ -351,8 +356,8 @@
             rows.append(level_scale(number) * jnp.sum(picked, axis=0, keepdims=True))
         q_t = q.astype(F32).T
         far_t = dot(k, grad_scores, 0, 0)
-        for part, states_ref in enumerate((low_ref, high_ref)):
-            turned = dot(states_ref[h], go, 1, 0)
+        for part in range(2):
+            turned = dot(far_states(pc_ref, h) if part else low_ref[h], go, 1, 0)
             for m in range(PLANE):
                 piece = turned[m * HD : (m + 1) * HD]
                 number = LOCAL + part * PLANE + m
@@ -413,17 +418,18 @@
         (
             rates, norm_gain, both_cores(wide), both, queries, key_rows, value_rows, grad_normed,
         ),
-        2**28,
+        2**34,
         4 * MIB,
         tuple(range(8)),
         tuple(range(3)),
         ALONE,
         views={3: (MATRIX, lambda ref: ref.at[0])},
     )
-    attended, high, payload = call(
+    gathered = both_cores(arrived)
+    attended, payload = call(
         attend_body,
-        [(TURNED, F32), (STACKED, BF16), ((8, 8, HD), F32)],
-        (both_cores(arrived), rates, mixed, q_turned),
+        [(TURNED, F32), ((8, 8, HD), F32)],
+        (gathered, rates, queries, mixed),
         2**27,
         4 * MIB,
     )
@@ -449,16 +455,16 @@
         back_body,
         [(TOKENS, BF16), (TOKENS, BF16), (TOKENS, F32), (TOKENS, F32), ((LOCAL + FAR, NH, TOK), F32)],
         (
-            sums, norm_gain, rates, queries, key_rows, value_rows, mixed, attended, low, high,
+            sums, norm_gain, rates, queries, key_rows, value_rows, mixed, attended, low, gathered,
         ),
-        2**28,
+        2**34,
         5 * MIB,
         tuple(range(10)),
         tuple(range(5)),
         ALONE,
         views={6: (TURNED, lambda ref: ref.at[:, 1])},
     )
-    returned, back2 = lax.optimization_barrier((returned, back2))
+    returned, back2, near_k = lax.optimization_barrier((returned, back2, near_k))
     (spread,) = call(owner_backward_body, [((64, 8, HD), F32)], (returned,), 2**17, MIB // 2)
     total = swap(spread, CTX).reshape(MATRIX)
     (onward,) = call(add_odd_body, [(HALF, F32)], (first, back2), 2**16, MIB, after=(spread,))

time: 124 us -> 118 us (0.952)
  starting transfers between devices: 49 us -> 41.1 us
  blocking collectives: 31.6 us -> 33.9 us
  waiting for transfers between devices: 23.2 us -> 24.7 us
    all_to_all x4, starting transfers between devices: 36.9 us -> 31.1 us  [swap(): return lax.all_to_all(value, axes, split_axis=0, concat_axis=0, tiled=True)]
    all_to_all x4, waiting for transfers between devices: 5.1 us -> 10.4 us  [swap(): return lax.all_to_all(value, axes, split_axis=0, concat_axis=0, tiled=True)]
    ppermute x1, waiting for transfers between devices: 9.08 us -> 3.85 us  [shards(): back2 = lax.ppermute(second, 'x', [(3, 0), (2, 1)])]
    ppermute x1, waiting for transfers between devices: 0.25 us -> 5.37 us  [shards(): back1 = lax.ppermute(onward, 'x', [(0, 1), (1, 0), (3, 2)])]
    ppermute x1, waiting for transfers between devices: 3.74 us -> 0.01 us  [shards(): step2 = lax.ppermute(twice, 'x', [(0, 3), (1, 2)])]
    all_gather x6, blocking collectives: 18.1 us -> 20.3 us  [both_cores(): return lax.all_gather(value, 'core', axis=0, tiled=False)]
    ppermute x1, starting transfers between devices: 4.35 us -> 2.19 us  [shards(): step2 = lax.ppermute(twice, 'x', [(0, 3), (1, 2)])]
  transfers between devices with their start and end apart: 8 -> 8, of which waited for: 7 -> 7; matrix products, arithmetic and copies ran while one was open for 0% -> 0% of each run, Pallas kernels for 7% -> 8%
where the time goes in v3:
time: 118 us
  starting transfers between devices  41.1 us (35%)
  blocking collectives  33.9 us (29%)
  waiting for transfers between devices  24.7 us (21%)
  Pallas kernels  16.7 us (14%)
    all_to_all x4, starting transfers between devices, swap(): return lax.all_to_all(value, axes, split_axis=0, concat_axis=0, tiled=True)  31.1 us
    all_gather x6, blocking collectives, both_cores(): return lax.all_gather(value, 'core', axis=0, tiled=False)  20.3 us
    pallas_call x15, Pallas kernels, call(): pl.pallas_call(wrapped, out_shape=[jax.ShapeDtypeStruct(s, d) for s, d in...  16.7 us
    all_to_all x1, blocking collectives, swap(): return lax.all_to_all(value, axes, split_axis=0, concat_axis=0, tiled=True)  13.6 us
    all_to_all x4, waiting for transfers between devices, swap(): return lax.all_to_all(value, axes, split_axis=0, concat_axis=0, tiled=True)  10.4 us
    ppermute x1, waiting for transfers between devices, shards(): back1 = lax.ppermute(onward, 'x', [(0, 1), (1, 0), (3, 2)])  5.37 us
    ppermute x1, waiting for transfers between devices, shards(): step1 = lax.ppermute(pair, 'x', [(0, 1), (1, 0), (2, 3), (3, 2)])  5.06 us
    ppermute x1, waiting for transfers between devices, shards(): back2 = lax.ppermute(second, 'x', [(3, 0), (2, 1)])  3.85 us
  transfers between devices with their start and end apart: 8, of which 7 were waited for; matrix products, arithmetic and copies ran while one was open for 0% of the time, Pallas kernels for 8%

profile of v3, /device:TPU:1, one launch (start us, length us, event | category | flops | bytes accessed | tf_op | source)
XLA Modules:
  0.0 117.7 jit_solution(5783907153781839634)
XLA Ops:
  0.6 2.5 %shard_map.101 = f32[4,128,128]{2,1,0:T(8,128)} custom-call(bf16[4,256,128]{2,1,0:T(8,128)(2,1)} %refs_3_.3, bf16[4,256,128]{2,1,0:T(8,128)(2,1)} %refs_4_.5), custom_call_target="tpu_custom_call" | custom-call | flops 33554432 | bytes 1048576 | tf_op jit(solution)/shard_map/pallas_call | solution.py:108
  3.1 15.0 %all-to-all-start = ((f32[64,8,128]{2,1,0:T(8,128)}), f32[64,8,128]{2,1,0:T(8,128)S(1)}, u32[]{:S(2)}, u32[]{:S(2)}) async-start(f32[64,8,128]{2,1,0:T(8,128)} %bitcast.23), calls=%async_computation | async-start | bytes 524288 | tf_op jit(solution)/shard_map/all_to_all | solution.py:387
  18.1 2.3 %all-gather = f32[8,128,128]{2,1,0:T(8,128)S(1)} all-gather(f32[4,128,128]{2,1,0:T(8,128)S(1)} %copy-done.12), channel_id=2, replica_groups=mesh['heads'=8,'z'=8,'x'=4,'core'=2] {'core'}, dimensions={0}, use_global_device_ids=true | all-gather | bytes 786432 | tf_op jit(solution)/shard_map/all_gather | solution.py:391
  20.4 3.2 %collective-permute-start = (f32[2,128,128]{2,1,0:T(8,128)S(1)}, f32[2,128,128]{2,1,0:T(8,128)S(1)}, u32[]{:S(2)}, u32[]{:S(2)}) collective-permute-start(f32[2,128,128]{2,1,0:T(8,128)S(1)} %shard_map.102.refs_0_), channel_id=1, source_target_pairs={{0,2},{2,0},{4,6},{6,4},{1,3},{3,1},{5,7},{7,5},{8,10},{10,8},{12,... | collective-permute-start | bytes 393224 | tf_op jit(solution)/shard_map/ppermute | solution.py:402
  23.6 5.1 %collective-permute-done.refs_1_.refs_0_ = f32[2,128,128]{2,1,0:T(8,128)S(1)} collective-permute-done((f32[2,128,128]{2,1,0:T(8,128)S(1)}, f32[2,128,128]{2,1,0:T(8,128)S(1)}, u32[]{:S(2)}, u32[]{:S(2)}) %collective-permute-start) | collective-permute-done | bytes 131104 | tf_op jit(solution)/shard_map/ppermute | solution.py:402
  28.7 2.6 %all-to-all-done.refs_0_ = f32[64,8,128]{2,1,0:T(8,128)S(1)} async-done(((f32[64,8,128]{2,1,0:T(8,128)}), f32[64,8,128]{2,1,0:T(8,128)S(1)}, u32[]{:S(2)}, u32[]{:S(2)}) %all-to-all-start) | async-done | bytes 262176 | tf_op jit(solution)/shard_map/all_to_all | solution.py:387
  32.1 2.2 %collective-permute-start.1 = (f32[2,128,128]{2,1,0:T(8,128)S(1)}, f32[2,128,128]{2,1,0:T(8,128)S(1)}, u32[]{:S(2)}, u32[]{:S(2)}) collective-permute-start(f32[2,128,128]{2,1,0:T(8,128)S(1)} %shard_map.104), channel_id=1, source_target_pairs={{0,6},{2,4},{1,7},{3,5},{8,14},{10,12},{9,15},{11,13},{16,22},{18,... | collective-permute-start | bytes 393224 | tf_op jit(solution)/shard_map/ppermute | solution.py:407
  34.3 5.2 %all-to-all-start.1 = ((f32[32,3,8,128]{3,2,1,0:T(8,128)}), f32[32,3,8,128]{3,2,1,0:T(8,128)S(1)}, u32[]{:S(2)}, u32[]{:S(2)}) async-start(f32[32,3,8,128]{3,2,1,0:T(8,128)} %shard_map.103.refs_2_), calls=%async_computation.1 | async-start | bytes 786432 | tf_op jit(solution)/shard_map/all_to_all | solution.py:387
  39.5 3.6 %all-gather.2 = f32[4,2,128,128]{3,2,1,0:T(8,128)} all-gather(f32[2,2,128,128]{3,2,1,0:T(8,128)S(1)} %shard_map.105), channel_id=4, replica_groups=mesh['heads'=8,'z'=8,'x'=4,'core'=2] {'core'}, dimensions={0}, use_global_device_ids=true | all-gather | bytes 786432 | tf_op jit(solution)/shard_map/all_gather | solution.py:391
  43.0 3.9 %shard_map.106 = (f32[4,2,128,256]{3,2,1,0:T(8,128)}, bf16[4,384,128]{2,1,0:T(8,128)(2,1)}, bf16[4,128,256]{2,1,0:T(8,128)(2,1)}) custom-call(f32[15,4,256]{2,1,0:T(4,128)} %bitcast.19, f32[4,128]{1,0:T(4,128)} %refs_1_.5, f32[2,2,2,128,128]{4,3,2,1,0:T(8,128)} %bitcast.24, f32[2,4,128,128]{3,2,1,0:T(8,128)} %bitcast.16, bf16[4,256,128]{2,1,0:T(8,128)(2,1)} %refs_3_.2, ...), custom_call_target="tpu_custom_call" | custom-call | flops 17179869184 | bytes 4194304 | tf_op jit(solution)/shard_map/pallas_call | solution.py:108
  47.0 5.3 %all-to-all-done.1 = f32[32,3,8,128]{3,2,1,0:T(8,128)S(1)} async-done(((f32[32,3,8,128]{3,2,1,0:T(8,128)}), f32[32,3,8,128]{3,2,1,0:T(8,128)S(1)}, u32[]{:S(2)}, u32[]{:S(2)}) %all-to-all-start.1) | async-done | bytes 393248 | tf_op jit(solution)/shard_map/all_to_all | solution.py:387
  52.3 5.4 %all-gather.1 = f32[64,3,8,128]{3,2,1,0:T(8,128)S(1)} all-gather(f32[32,3,8,128]{3,2,1,0:T(8,128)S(1)} %all-to-all-done.1), channel_id=3, replica_groups=mesh['heads'=8,'z'=8,'x'=4,'core'=2] {'core'}, dimensions={0}, use_global_device_ids=true | all-gather | bytes 1179648 | tf_op jit(solution)/shard_map/all_gather | solution.py:391
  58.6 13.6 %all_to_all.25.refs_0_ = f32[8,8,128]{2,1,0:T(8,128)S(1)} all-to-all(f32[8,8,128]{2,1,0:T(8,128)S(1)} %get-tuple-element.33), channel_id=1, replica_groups=mesh['heads'=8,'z'=8,'x'=4,'core'=2] {'heads'}, dimensions={0} | all-to-all | bytes 65536 | tf_op jit(solution)/shard_map/all_to_all | solution.py:387
  73.3 3.7 %all-gather.3 = f32[64,3,8,128]{3,2,1,0:T(8,128)S(1)} all-gather(f32[32,3,8,128]{3,2,1,0:T(8,128)S(1)} %get-tuple-element.40), channel_id=5, replica_groups=mesh['heads'=8,'z'=8,'x'=4,'core'=2] {'core'}, dimensions={0}, use_global_device_ids=true | all-gather | bytes 1179648 | tf_op jit(solution)/shard_map/all_gather | solution.py:391
  77.9 4.0 %all-to-all-start.3 = ((f32[32,3,8,128]{3,2,1,0:T(8,128)}), f32[32,3,8,128]{3,2,1,0:T(8,128)S(1)}, u32[]{:S(2)}, u32[]{:S(2)}) async-start(f32[32,3,8,128]{3,2,1,0:T(8,128)} %shard_map.110), calls=%async_computation.3 | async-start | bytes 786432 | tf_op jit(solution)/shard_map/all_to_all | solution.py:387
  81.8 2.6 %all-gather.4 = f32[6,2,128,128]{3,2,1,0:T(8,128)S(1)} all-gather(f32[3,2,128,128]{3,2,1,0:T(8,128)S(1)} %get-tuple-element.42), channel_id=6, replica_groups=mesh['heads'=8,'z'=8,'x'=4,'core'=2] {'core'}, dimensions={0}, use_global_device_ids=true | all-gather | bytes 1179648 | tf_op jit(solution)/shard_map/all_gather | solution.py:391
  84.5 1.3 %collective-permute-start.2 = (f32[2,128,128]{2,1,0:T(8,128)S(1)}, f32[2,128,128]{2,1,0:T(8,128)S(1)}, u32[]{:S(2)}, u32[]{:S(2)}) collective-permute-start(f32[2,128,128]{2,1,0:T(8,128)S(1)} %get-tuple-element.43), channel_id=1, source_target_pairs={{6,0},{4,2},{7,1},{5,3},{14,8},{12,10},{15,9},{13,11},{22,16},{20,... | collective-permute-start | bytes 393224 | tf_op jit(solution)/shard_map/ppermute | solution.py:453
  85.8 5.2 %shard_map.108 = (bf16[4,256,128]{2,1,0:T(8,128)(2,1)}, bf16[4,256,128]{2,1,0:T(8,128)(2,1)}, f32[4,256,128]{2,1,0:T(8,128)}, f32[4,256,128]{2,1,0:T(8,128)}, f32[15,4,256]{2,1,0:T(4,128)}) custom-call(f32[8,8,128]{2,1,0:T(8,128)} %copy-done.11, f32[4,128]{1,0:T(4,128)} %refs_1_.5, f32[15,4,256]{2,1,0:T(4,128)} %bitcast.20, bf16[4,256,128]{2,1,0:T(8,128)(2,1)} %refs_3_.2, ...), custom_call_target="tpu_custom_call" | custom-call | flops 17179869184 | bytes 5242880 | tf_op jit(solution)/shard_map/pallas_call | solution.py:108
  91.0 3.8 %collective-permute-done.2.refs_1_ = f32[2,128,128]{2,1,0:T(8,128)S(1)} collective-permute-done((f32[2,128,128]{2,1,0:T(8,128)S(1)}, f32[2,128,128]{2,1,0:T(8,128)S(1)}, u32[]{:S(2)}, u32[]{:S(2)}) %collective-permute-start.2) | collective-permute-done | bytes 131104 | tf_op jit(solution)/shard_map/ppermute | solution.py:453
  96.4 7.0 %all-to-all-start.4 = ((f32[64,8,128]{2,1,0:T(8,128)}), f32[64,8,128]{2,1,0:T(8,128)S(1)}, u32[]{:S(2)}, u32[]{:S(2)}) async-start(f32[64,8,128]{2,1,0:T(8,128)} %shard_map.112.refs_2_), calls=%async_computation.4 | async-start | bytes 524288 | tf_op jit(solution)/shard_map/all_to_all | solution.py:387
  103.5 3.3 %collective-permute-start.3 = (f32[2,128,128]{2,1,0:T(8,128)S(1)}, f32[2,128,128]{2,1,0:T(8,128)S(1)}, u32[]{:S(2)}, u32[]{:S(2)}) collective-permute-start(f32[2,128,128]{2,1,0:T(8,128)S(1)} %shard_map.113), channel_id=1, source_target_pairs={{0,2},{2,0},{6,4},{1,3},{3,1},{7,5},{8,10},{10,8},{14,12},{9,11},{... | collective-permute-start | bytes 393224 | tf_op jit(solution)/shard_map/ppermute | solution.py:471
  106.8 5.4 %collective-permute-done.3.refs_0_ = f32[2,128,128]{2,1,0:T(8,128)S(1)} collective-permute-done((f32[2,128,128]{2,1,0:T(8,128)S(1)}, f32[2,128,128]{2,1,0:T(8,128)S(1)}, u32[]{:S(2)}, u32[]{:S(2)}) %collective-permute-start.3) | collective-permute-done | bytes 131104 | tf_op jit(solution)/shard_map/ppermute | solution.py:471
  112.2 2.7 %all-gather.5 = f32[4,128,128]{2,1,0:T(8,128)S(1)} all-gather(f32[2,128,128]{2,1,0:T(8,128)S(1)} %get-tuple-element.49), channel_id=7, replica_groups=mesh['heads'=8,'z'=8,'x'=4,'core'=2] {'core'}, dimensions={0}, use_global_device_ids=true | all-gather | bytes 393216 | tf_op jit(solution)/shard_map/all_gather | solution.py:391
  114.9 1.7 %all-to-all-done.4 = f32[64,8,128]{2,1,0:T(8,128)S(1)} async-done(((f32[64,8,128]{2,1,0:T(8,128)}), f32[64,8,128]{2,1,0:T(8,128)S(1)}, u32[]{:S(2)}, u32[]{:S(2)}) %all-to-all-start.4) | async-done | bytes 262176 | tf_op jit(solution)/shard_map/all_to_all | solution.py:387
  (40 shorter events, 6.4 us)
Async XLA Ops:
  3.1 15.0 %copy-start.12 = (f32[4,128,128]{2,1,0:T(8,128)S(1)}, f32[4,128,128]{2,1,0:T(8,128)}, u32[]{:S(2)}) copy-start(f32[4,128,128]{2,1,0:T(8,128)} %shard_map.101) | copy-start | bytes 786436
  3.1 28.2 %all-to-all-start = ((f32[64,8,128]{2,1,0:T(8,128)}), f32[64,8,128]{2,1,0:T(8,128)S(1)}, u32[]{:S(2)}, u32[]{:S(2)}) async-start(f32[64,8,128]{2,1,0:T(8,128)} %bitcast.23), calls=%async_computation | async-start | bytes 524288 | tf_op jit(solution)/shard_map/all_to_all | solution.py:387
  20.4 11.7 %copy-start.2 = (f32[8,128,128]{2,1,0:T(8,128)}, f32[8,128,128]{2,1,0:T(8,128)S(1)}, u32[]{:S(2)}) copy-start(f32[8,128,128]{2,1,0:T(8,128)S(1)} %all-gather) | copy-start | bytes 1572868
  20.4 8.3 %collective-permute-start = (f32[2,128,128]{2,1,0:T(8,128)S(1)}, f32[2,128,128]{2,1,0:T(8,128)S(1)}, u32[]{:S(2)}, u32[]{:S(2)}) collective-permute-start(f32[2,128,128]{2,1,0:T(8,128)S(1)} %shard_map.102.refs_0_), channel_id=1, source_target_pairs={{0,2},{2,0},{4,6},{6,4},{1,3},{3,1},{5,7},{7,5},{8,10},{10,8},{12,... | collective-permute-start | bytes 393224 | tf_op jit(solution)/shard_map/ppermute | solution.py:402
  32.1 7.4 %collective-permute-start.1 = (f32[2,128,128]{2,1,0:T(8,128)S(1)}, f32[2,128,128]{2,1,0:T(8,128)S(1)}, u32[]{:S(2)}, u32[]{:S(2)}) collective-permute-start(f32[2,128,128]{2,1,0:T(8,128)S(1)} %shard_map.104), channel_id=1, source_target_pairs={{0,6},{2,4},{1,7},{3,5},{8,14},{10,12},{9,15},{11,13},{16,22},{18,... | collective-permute-start | bytes 393224 | tf_op jit(solution)/shard_map/ppermute | solution.py:407
  34.3 18.0 %all-to-all-start.1 = ((f32[32,3,8,128]{3,2,1,0:T(8,128)}), f32[32,3,8,128]{3,2,1,0:T(8,128)S(1)}, u32[]{:S(2)}, u32[]{:S(2)}) async-start(f32[32,3,8,128]{3,2,1,0:T(8,128)} %shard_map.103.refs_2_), calls=%async_computation.1 | async-start | bytes 786432 | tf_op jit(solution)/shard_map/all_to_all | solution.py:387
  43.0 14.7 %copy-start.8 = (bf16[4,256,128]{2,1,0:T(8,128)(2,1)S(1)}, bf16[4,256,128]{2,1,0:T(8,128)(2,1)}, u32[]{:S(2)}) copy-start(bf16[4,256,128]{2,1,0:T(8,128)(2,1)} %refs_3_.2) | copy-start | bytes 786436
  46.9 10.8 %copy-start = (f32[4,2,128,256]{3,2,1,0:T(8,128)S(1)}, f32[4,2,128,256]{3,2,1,0:T(8,128)}, u32[]{:S(2)}) copy-start(f32[4,2,128,256]{3,2,1,0:T(8,128)} %get-tuple-element.32.refs_3_.refs_6_) | copy-start | bytes 3145732
  46.9 10.8 %copy-start.10 = (f32[4,15,256]{2,0,1:T(4,128)S(1)}, f32[4,15,256]{2,0,1:T(4,128)}, u32[]{:S(2)}) copy-start(f32[4,15,256]{2,0,1:T(4,128)} %param.9) | copy-start | bytes 184324
  57.7 0.9 copy-start.1
  57.7 14.4 %copy-start.9 = (bf16[4,128,256]{2,1,0:T(8,128)(2,1)S(1)}, bf16[4,128,256]{2,1,0:T(8,128)(2,1)}, u32[]{:S(2)}) copy-start(bf16[4,128,256]{2,1,0:T(8,128)(2,1)} %get-tuple-element.38.refs_4_) | copy-start | bytes 786436
  58.6 14.7 %copy-start.7 = (f32[4,128,256]{2,1,0:T(8,128)}, f32[4,128,256]{2,1,0:T(8,128)S(1)}, u32[]{:S(2)}) copy-start(f32[4,128,256]{2,1,0:T(8,128)S(1)} %get-tuple-element.34.refs_7_.refs_2_) | copy-start | bytes 1572868
  72.1 1.2 %copy-start.11 = (f32[8,8,128]{2,1,0:T(8,128)}, f32[8,8,128]{2,1,0:T(8,128)S(1)}, u32[]{:S(2)}) copy-start(f32[8,8,128]{2,1,0:T(8,128)S(1)} %all_to_all.25.refs_0_) | copy-start | bytes 98308
  77.9 17.9 %all-to-all-start.3 = ((f32[32,3,8,128]{3,2,1,0:T(8,128)}), f32[32,3,8,128]{3,2,1,0:T(8,128)S(1)}, u32[]{:S(2)}, u32[]{:S(2)}) async-start(f32[32,3,8,128]{3,2,1,0:T(8,128)} %shard_map.110), calls=%async_computation.3 | async-start | bytes 786432 | tf_op jit(solution)/shard_map/all_to_all | solution.py:387
  84.5 10.4 %collective-permute-start.2 = (f32[2,128,128]{2,1,0:T(8,128)S(1)}, f32[2,128,128]{2,1,0:T(8,128)S(1)}, u32[]{:S(2)}, u32[]{:S(2)}) collective-permute-start(f32[2,128,128]{2,1,0:T(8,128)S(1)} %get-tuple-element.43), channel_id=1, source_target_pairs={{6,0},{4,2},{7,1},{5,3},{14,8},{12,10},{15,9},{13,11},{22,16},{20,... | collective-permute-start | bytes 393224 | tf_op jit(solution)/shard_map/ppermute | solution.py:453
  96.4 20.1 %all-to-all-start.4 = ((f32[64,8,128]{2,1,0:T(8,128)}), f32[64,8,128]{2,1,0:T(8,128)S(1)}, u32[]{:S(2)}, u32[]{:S(2)}) async-start(f32[64,8,128]{2,1,0:T(8,128)} %shard_map.112.refs_2_), calls=%async_computation.4 | async-start | bytes 524288 | tf_op jit(solution)/shard_map/all_to_all | solution.py:387
  103.5 8.7 %collective-permute-start.3 = (f32[2,128,128]{2,1,0:T(8,128)S(1)}, f32[2,128,128]{2,1,0:T(8,128)S(1)}, u32[]{:S(2)}, u32[]{:S(2)}) collective-permute-start(f32[2,128,128]{2,1,0:T(8,128)S(1)} %shard_map.113), channel_id=1, source_target_pairs={{0,2},{2,0},{6,4},{1,3},{3,1},{7,5},{8,10},{10,8},{14,12},{9,11},{... | collective-permute-start | bytes 393224 | tf_op jit(solution)/shard_map/ppermute | solution.py:471
  112.1 4.5 %copy-start.4 = (bf16[4,256,128]{2,1,0:T(8,128)(2,1)S(1)}, bf16[4,256,128]{2,1,0:T(8,128)(2,1)}, u32[]{:S(2)}) copy-start(bf16[4,256,128]{2,1,0:T(8,128)(2,1)} %refs_4_.5) | copy-start | bytes 786436
  112.1 4.5 %copy-start.5 = (f32[4,256,128]{2,1,0:T(8,128)S(1)}, f32[4,256,128]{2,1,0:T(8,128)}, u32[]{:S(2)}) copy-start(f32[4,256,128]{2,1,0:T(8,128)} %get-tuple-element.50.refs_5_) | copy-start | bytes 1572868
  112.1 4.5 %copy-start.6 = (f32[4,256,128]{2,1,0:T(8,128)S(1)}, f32[4,256,128]{2,1,0:T(8,128)}, u32[]{:S(2)}) copy-start(f32[4,256,128]{2,1,0:T(8,128)} %get-tuple-element.51.refs_6_) | copy-start | bytes 1572868
  112.2 4.4 %copy-start.3 = (bf16[4,256,128]{2,1,0:T(8,128)(2,1)S(1)}, bf16[4,256,128]{2,1,0:T(8,128)(2,1)}, u32[]{:S(2)}) copy-start(bf16[4,256,128]{2,1,0:T(8,128)(2,1)} %refs_3_.3) | copy-start | bytes 786436

commit v4 on v3

--- a/solution.py
+++ b/solution.py
@@ -41,7 +41,7 @@
     return lax.dot_general(a, b, (((ca,), (cb,)), ((), ())), preferred_element_type=F32)
 
 
-def call(body, outs, operands, flops, moved, far_in=(), far_out=(), limit=16, after=(), views={}):
+def call(body, outs, operands, flops, moved, far_in=(), far_out=(), limit=16, after=(), views={}, whole_in=False):
     near = pl.BlockSpec(memory_space=pltpu.VMEM)
     far = pl.BlockSpec(memory_space=pltpu.HBM)
     count = len(operands)
@@ -52,7 +52,7 @@
     def split(shape):
         return shape[0] == NH and len(shape) > 2
 
-    parts = [NH if split(shapes[i]) else 1 for i in far_in]
+    parts = [NH if split(shapes[i]) and not whole_in else 1 for i in far_in]
     parts += [NH if split(outs[i][0]) else 1 for i in far_out]
     copies = sum(parts)
 
@@ -240,7 +240,7 @@
     squares = jnp.sum(squares, axis=0, keepdims=True)
     inner = jnp.sum(inner, axis=0, keepdims=True)
     rows = [squares[:, :HD], squares[:, HD:], inner[:, :HD], inner[:, HD:]]
-    tile = jnp.concatenate(rows + [jnp.zeros((4, HD), F32)], axis=0)
+    tile = jnp.concatenate(rows, axis=0)
     for peer in range(8):
         pay_ref[peer] = tile
 
@@ -394,14 +394,23 @@
 def shards(queries, key_rows, value_rows, level_weights, norm_gain, grad_normed):
     rates = jnp.transpose(level_weights, (1, 0, 2))
     (kv,) = call(
-        key_value_body, [(MATRIX, F32)], (key_rows, value_rows), 2**25, MIB, (0, 1), (), ALONE
+        key_value_body,
+        [(MATRIX, F32)],
+        (key_rows, value_rows),
+        2**25,
+        MIB,
+        (0, 1),
+        (0,),
+        ALONE,
+        whole_in=True,
     )
     owned = swap(kv.reshape(64, 8, HD), CTX)
     both = both_cores(kv)
     (pair,) = call(half_body, [(HALF, F32)], (both,), 2**16, MIB)
     step1 = lax.ppermute(pair, "x", [(0, 1), (1, 0), (2, 3), (3, 2)])
-    owned, step1 = lax.optimization_barrier((owned, step1))
-    (outgoing,) = call(owner_forward_body, [(PIECES, F32)], (owned,), 2**17, MIB // 2)
+    (outgoing,) = call(
+        owner_forward_body, [(PIECES, F32)], (owned,), 2**17, MIB // 2, after=(pair,)
+    )
     arrived = swap(outgoing, ROWS)
     (twice,) = call(add_body, [(HALF, F32)], (pair, step1), 2**16, MIB, after=(outgoing,))
     step2 = lax.ppermute(twice, "x", [(0, 3), (1, 2)])
@@ -428,7 +437,7 @@
     gathered = both_cores(arrived)
     attended, payload = call(
         attend_body,
-        [(TURNED, F32), ((8, 8, HD), F32)],
+        [(TURNED, F32), ((8, 4, HD), F32)],
         (gathered, rates, queries, mixed),
         2**27,
         4 * MIB,

time: 118 us -> 117 us (level)
    all_to_all x4, waiting for transfers between devices: 10.4 us -> 15.5 us  [swap(): return lax.all_to_all(value, axes, split_axis=0, concat_axis=0, tiled=True)]
    ppermute x1, waiting for transfers between devices: 5.06 us -> 0.01 us  [shards(): step1 = lax.ppermute(pair, 'x', [(0, 1), (1, 0), (2, 3), (3, 2)])]
  transfers between devices with their start and end apart: 8 -> 8, of which waited for: 7 -> 6; matrix products, arithmetic and copies ran while one was open for 0% -> 0% of each run, Pallas kernels for 8% -> 9%
where the time goes in v4:
time: 117 us; the launch traced here: 116 us
  starting transfers between devices  40.3 us (34%)
  blocking collectives  33.6 us (29%)
  waiting for transfers between devices  24.7 us (21%)
  Pallas kernels  16.2 us (14%)
    all_to_all x4, starting transfers between devices, swap(): return lax.all_to_all(value, axes, split_axis=0, concat_axis=0, tiled=True)  30.3 us
    all_gather x6, blocking collectives, both_cores(): return lax.all_gather(value, 'core', axis=0, tiled=False)  20.4 us
    pallas_call x15, Pallas kernels, call(): pl.pallas_call(wrapped, out_shape=[jax.ShapeDtypeStruct(s, d) for s, d in...  16.2 us
    all_to_all x4, waiting for transfers between devices, swap(): return lax.all_to_all(value, axes, split_axis=0, concat_axis=0, tiled=True)  15.5 us
    all_to_all x1, blocking collectives, swap(): return lax.all_to_all(value, axes, split_axis=0, concat_axis=0, tiled=True)  13.2 us
    ppermute x1, waiting for transfers between devices, shards(): back1 = lax.ppermute(onward, 'x', [(0, 1), (1, 0), (3, 2)])  5.37 us
    ppermute x1, waiting for transfers between devices, shards(): back2 = lax.ppermute(second, 'x', [(3, 0), (2, 1)])  3.86 us
    ppermute x1, starting transfers between devices, shards(): back1 = lax.ppermute(onward, 'x', [(0, 1), (1, 0), (3, 2)])  3.29 us
  transfers between devices with their start and end apart: 8, of which 6 were waited for; matrix products, arithmetic and copies ran while one was open for 0% of the time, Pallas kernels for 9%

profile of v4, /device:TPU:1, one launch (start us, length us, event | category | flops | bytes accessed | tf_op | source)
XLA Modules:
  0.0 116.2 jit_solution(8259546198055052491)
XLA Ops:
  0.6 2.0 %shard_map.101 = f32[4,128,128]{2,1,0:T(8,128)} custom-call(bf16[4,256,128]{2,1,0:T(8,128)(2,1)} %refs_3_.3, bf16[4,256,128]{2,1,0:T(8,128)(2,1)} %refs_4_.5), custom_call_target="tpu_custom_call" | custom-call | flops 33554432 | bytes 1048576 | tf_op jit(solution)/shard_map/pallas_call | solution.py:108
  2.6 15.0 %all-to-all-start = ((f32[64,8,128]{2,1,0:T(8,128)}), f32[64,8,128]{2,1,0:T(8,128)S(1)}, u32[]{:S(2)}, u32[]{:S(2)}) async-start(f32[64,8,128]{2,1,0:T(8,128)} %bitcast.23), calls=%async_computation | async-start | bytes 524288 | tf_op jit(solution)/shard_map/all_to_all | solution.py:387
  17.6 2.3 %all-gather = f32[8,128,128]{2,1,0:T(8,128)S(1)} all-gather(f32[4,128,128]{2,1,0:T(8,128)S(1)} %copy-done.12), channel_id=2, replica_groups=mesh['heads'=8,'z'=8,'x'=4,'core'=2] {'core'}, dimensions={0}, use_global_device_ids=true | all-gather | bytes 786432 | tf_op jit(solution)/shard_map/all_gather | solution.py:391
  19.9 3.2 %collective-permute-start = (f32[2,128,128]{2,1,0:T(8,128)S(1)}, f32[2,128,128]{2,1,0:T(8,128)S(1)}, u32[]{:S(2)}, u32[]{:S(2)}) collective-permute-start(f32[2,128,128]{2,1,0:T(8,128)S(1)} %shard_map.102.refs_1_.refs_0_), channel_id=1, source_target_pairs={{0,2},{2,0},{4,6},{6,4},{1,3},{3,1},{5,7},{7,5},{8,10},{10,8},{12,... | collective-permute-start | bytes 393224 | tf_op jit(solution)/shard_map/ppermute | solution.py:410
  23.1 7.6 %all-to-all-done.refs_0_ = f32[64,8,128]{2,1,0:T(8,128)S(1)} async-done(((f32[64,8,128]{2,1,0:T(8,128)}), f32[64,8,128]{2,1,0:T(8,128)S(1)}, u32[]{:S(2)}, u32[]{:S(2)}) %all-to-all-start) | async-done | bytes 262176 | tf_op jit(solution)/shard_map/all_to_all | solution.py:387
  31.6 2.2 %collective-permute-start.1 = (f32[2,128,128]{2,1,0:T(8,128)S(1)}, f32[2,128,128]{2,1,0:T(8,128)S(1)}, u32[]{:S(2)}, u32[]{:S(2)}) collective-permute-start(f32[2,128,128]{2,1,0:T(8,128)S(1)} %shard_map.104), channel_id=1, source_target_pairs={{0,6},{2,4},{1,7},{3,5},{8,14},{10,12},{9,15},{11,13},{16,22},{18,... | collective-permute-start | bytes 393224 | tf_op jit(solution)/shard_map/ppermute | solution.py:416
  33.8 4.4 %all-to-all-start.1 = ((f32[32,3,8,128]{3,2,1,0:T(8,128)}), f32[32,3,8,128]{3,2,1,0:T(8,128)S(1)}, u32[]{:S(2)}, u32[]{:S(2)}) async-start(f32[32,3,8,128]{3,2,1,0:T(8,128)} %shard_map.103.refs_2_), calls=%async_computation.1 | async-start | bytes 786432 | tf_op jit(solution)/shard_map/all_to_all | solution.py:387
  38.2 3.6 %all-gather.2 = f32[4,2,128,128]{3,2,1,0:T(8,128)} all-gather(f32[2,2,128,128]{3,2,1,0:T(8,128)S(1)} %shard_map.105), channel_id=4, replica_groups=mesh['heads'=8,'z'=8,'x'=4,'core'=2] {'core'}, dimensions={0}, use_global_device_ids=true | all-gather | bytes 786432 | tf_op jit(solution)/shard_map/all_gather | solution.py:391
  41.8 3.9 %shard_map.106 = (f32[4,2,128,256]{3,2,1,0:T(8,128)}, bf16[4,384,128]{2,1,0:T(8,128)(2,1)}, bf16[4,128,256]{2,1,0:T(8,128)(2,1)}) custom-call(f32[15,4,256]{2,1,0:T(4,128)} %bitcast.19, f32[4,128]{1,0:T(4,128)} %refs_1_.5, f32[2,2,2,128,128]{4,3,2,1,0:T(8,128)} %bitcast.24, f32[2,4,128,128]{3,2,1,0:T(8,128)} %bitcast.16, bf16[4,256,128]{2,1,0:T(8,128)(2,1)} %refs_3_.2, ...), custom_call_target="tpu_custom_call" | custom-call | flops 17179869184 | bytes 4194304 | tf_op jit(solution)/shard_map/pallas_call | solution.py:108
  45.7 5.3 %all-to-all-done.1 = f32[32,3,8,128]{3,2,1,0:T(8,128)S(1)} async-done(((f32[32,3,8,128]{3,2,1,0:T(8,128)}), f32[32,3,8,128]{3,2,1,0:T(8,128)S(1)}, u32[]{:S(2)}, u32[]{:S(2)}) %all-to-all-start.1) | async-done | bytes 393248 | tf_op jit(solution)/shard_map/all_to_all | solution.py:387
  51.0 5.4 %all-gather.1 = f32[64,3,8,128]{3,2,1,0:T(8,128)S(1)} all-gather(f32[32,3,8,128]{3,2,1,0:T(8,128)S(1)} %all-to-all-done.1), channel_id=3, replica_groups=mesh['heads'=8,'z'=8,'x'=4,'core'=2] {'core'}, dimensions={0}, use_global_device_ids=true | all-gather | bytes 1179648 | tf_op jit(solution)/shard_map/all_gather | solution.py:391
  57.3 13.2 %all_to_all.25.refs_0_ = f32[8,4,128]{2,1,0:T(4,128)S(1)} all-to-all(f32[8,4,128]{2,1,0:T(4,128)S(1)} %get-tuple-element.29), channel_id=1, replica_groups=mesh['heads'=8,'z'=8,'x'=4,'core'=2] {'heads'}, dimensions={0} | all-to-all | bytes 32768 | tf_op jit(solution)/shard_map/all_to_all | solution.py:387
  70.6 1.2 shard_map.109
  71.7 3.8 %all-gather.3 = f32[64,3,8,128]{3,2,1,0:T(8,128)S(1)} all-gather(f32[32,3,8,128]{3,2,1,0:T(8,128)S(1)} %get-tuple-element.36), channel_id=5, replica_groups=mesh['heads'=8,'z'=8,'x'=4,'core'=2] {'core'}, dimensions={0}, use_global_device_ids=true | all-gather | bytes 1179648 | tf_op jit(solution)/shard_map/all_gather | solution.py:391
  76.3 4.0 %all-to-all-start.3 = ((f32[32,3,8,128]{3,2,1,0:T(8,128)}), f32[32,3,8,128]{3,2,1,0:T(8,128)S(1)}, u32[]{:S(2)}, u32[]{:S(2)}) async-start(f32[32,3,8,128]{3,2,1,0:T(8,128)} %shard_map.110), calls=%async_computation.3 | async-start | bytes 786432 | tf_op jit(solution)/shard_map/all_to_all | solution.py:387
  80.3 2.6 %all-gather.4 = f32[6,2,128,128]{3,2,1,0:T(8,128)S(1)} all-gather(f32[3,2,128,128]{3,2,1,0:T(8,128)S(1)} %get-tuple-element.38), channel_id=6, replica_groups=mesh['heads'=8,'z'=8,'x'=4,'core'=2] {'core'}, dimensions={0}, use_global_device_ids=true | all-gather | bytes 1179648 | tf_op jit(solution)/shard_map/all_gather | solution.py:391
  83.0 1.3 %collective-permute-start.2 = (f32[2,128,128]{2,1,0:T(8,128)S(1)}, f32[2,128,128]{2,1,0:T(8,128)S(1)}, u32[]{:S(2)}, u32[]{:S(2)}) collective-permute-start(f32[2,128,128]{2,1,0:T(8,128)S(1)} %get-tuple-element.39), channel_id=1, source_target_pairs={{6,0},{4,2},{7,1},{5,3},{14,8},{12,10},{15,9},{13,11},{22,16},{20,... | collective-permute-start | bytes 393224 | tf_op jit(solution)/shard_map/ppermute | solution.py:462
  84.3 5.2 %shard_map.108 = (bf16[4,256,128]{2,1,0:T(8,128)(2,1)}, bf16[4,256,128]{2,1,0:T(8,128)(2,1)}, f32[4,256,128]{2,1,0:T(8,128)}, f32[4,256,128]{2,1,0:T(8,128)}, f32[15,4,256]{2,1,0:T(4,128)}) custom-call(f32[8,4,128]{2,1,0:T(4,128)} %copy-done.11, f32[4,128]{1,0:T(4,128)} %refs_1_.5, f32[15,4,256]{2,1,0:T(4,128)} %bitcast.20, bf16[4,256,128]{2,1,0:T(8,128)(2,1)} %refs_3_.2, ...), custom_call_target="tpu_custom_call" | custom-call | flops 17179869184 | bytes 5242880 | tf_op jit(solution)/shard_map/pallas_call | solution.py:108
  89.5 3.9 %collective-permute-done.2.refs_1_ = f32[2,128,128]{2,1,0:T(8,128)S(1)} collective-permute-done((f32[2,128,128]{2,1,0:T(8,128)S(1)}, f32[2,128,128]{2,1,0:T(8,128)S(1)}, u32[]{:S(2)}, u32[]{:S(2)}) %collective-permute-start.2) | collective-permute-done | bytes 131104 | tf_op jit(solution)/shard_map/ppermute | solution.py:462
  94.9 7.0 %all-to-all-start.4 = ((f32[64,8,128]{2,1,0:T(8,128)}), f32[64,8,128]{2,1,0:T(8,128)S(1)}, u32[]{:S(2)}, u32[]{:S(2)}) async-start(f32[64,8,128]{2,1,0:T(8,128)} %shard_map.112.refs_2_), calls=%async_computation.4 | async-start | bytes 524288 | tf_op jit(solution)/shard_map/all_to_all | solution.py:387
  102.0 3.3 %collective-permute-start.3 = (f32[2,128,128]{2,1,0:T(8,128)S(1)}, f32[2,128,128]{2,1,0:T(8,128)S(1)}, u32[]{:S(2)}, u32[]{:S(2)}) collective-permute-start(f32[2,128,128]{2,1,0:T(8,128)S(1)} %shard_map.113), channel_id=1, source_target_pairs={{0,2},{2,0},{6,4},{1,3},{3,1},{7,5},{8,10},{10,8},{14,12},{9,11},{... | collective-permute-start | bytes 393224 | tf_op jit(solution)/shard_map/ppermute | solution.py:480
  105.3 5.4 %collective-permute-done.3.refs_0_ = f32[2,128,128]{2,1,0:T(8,128)S(1)} collective-permute-done((f32[2,128,128]{2,1,0:T(8,128)S(1)}, f32[2,128,128]{2,1,0:T(8,128)S(1)}, u32[]{:S(2)}, u32[]{:S(2)}) %collective-permute-start.3) | collective-permute-done | bytes 131104 | tf_op jit(solution)/shard_map/ppermute | solution.py:480
  110.7 2.7 %all-gather.5 = f32[4,128,128]{2,1,0:T(8,128)S(1)} all-gather(f32[2,128,128]{2,1,0:T(8,128)S(1)} %get-tuple-element.45), channel_id=7, replica_groups=mesh['heads'=8,'z'=8,'x'=4,'core'=2] {'core'}, dimensions={0}, use_global_device_ids=true | all-gather | bytes 393216 | tf_op jit(solution)/shard_map/all_gather | solution.py:391
  113.4 1.7 %all-to-all-done.4 = f32[64,8,128]{2,1,0:T(8,128)S(1)} async-done(((f32[64,8,128]{2,1,0:T(8,128)}), f32[64,8,128]{2,1,0:T(8,128)S(1)}, u32[]{:S(2)}, u32[]{:S(2)}) %all-to-all-start.4) | async-done | bytes 262176 | tf_op jit(solution)/shard_map/all_to_all | solution.py:387
  (40 shorter events, 5.3 us)
Async XLA Ops:
  2.6 15.0 %copy-start.12 = (f32[4,128,128]{2,1,0:T(8,128)S(1)}, f32[4,128,128]{2,1,0:T(8,128)}, u32[]{:S(2)}) copy-start(f32[4,128,128]{2,1,0:T(8,128)} %shard_map.101) | copy-start | bytes 786436
  2.6 28.1 %all-to-all-start = ((f32[64,8,128]{2,1,0:T(8,128)}), f32[64,8,128]{2,1,0:T(8,128)S(1)}, u32[]{:S(2)}, u32[]{:S(2)}) async-start(f32[64,8,128]{2,1,0:T(8,128)} %bitcast.23), calls=%async_computation | async-start | bytes 524288 | tf_op jit(solution)/shard_map/all_to_all | solution.py:387
  19.9 11.7 %copy-start.2 = (f32[8,128,128]{2,1,0:T(8,128)}, f32[8,128,128]{2,1,0:T(8,128)S(1)}, u32[]{:S(2)}) copy-start(f32[8,128,128]{2,1,0:T(8,128)S(1)} %all-gather) | copy-start | bytes 1572868
  19.9 11.6 %collective-permute-start = (f32[2,128,128]{2,1,0:T(8,128)S(1)}, f32[2,128,128]{2,1,0:T(8,128)S(1)}, u32[]{:S(2)}, u32[]{:S(2)}) collective-permute-start(f32[2,128,128]{2,1,0:T(8,128)S(1)} %shard_map.102.refs_1_.refs_0_), channel_id=1, source_target_pairs={{0,2},{2,0},{4,6},{6,4},{1,3},{3,1},{5,7},{7,5},{8,10},{10,8},{12,... | collective-permute-start | bytes 393224 | tf_op jit(solution)/shard_map/ppermute | solution.py:410
  31.6 6.6 %collective-permute-start.1 = (f32[2,128,128]{2,1,0:T(8,128)S(1)}, f32[2,128,128]{2,1,0:T(8,128)S(1)}, u32[]{:S(2)}, u32[]{:S(2)}) collective-permute-start(f32[2,128,128]{2,1,0:T(8,128)S(1)} %shard_map.104), channel_id=1, source_target_pairs={{0,6},{2,4},{1,7},{3,5},{8,14},{10,12},{9,15},{11,13},{16,22},{18,... | collective-permute-start | bytes 393224 | tf_op jit(solution)/shard_map/ppermute | solution.py:416
  33.8 17.3 %all-to-all-start.1 = ((f32[32,3,8,128]{3,2,1,0:T(8,128)}), f32[32,3,8,128]{3,2,1,0:T(8,128)S(1)}, u32[]{:S(2)}, u32[]{:S(2)}) async-start(f32[32,3,8,128]{3,2,1,0:T(8,128)} %shard_map.103.refs_2_), calls=%async_computation.1 | async-start | bytes 786432 | tf_op jit(solution)/shard_map/all_to_all | solution.py:387
  41.8 14.7 %copy-start.8 = (bf16[4,256,128]{2,1,0:T(8,128)(2,1)S(1)}, bf16[4,256,128]{2,1,0:T(8,128)(2,1)}, u32[]{:S(2)}) copy-start(bf16[4,256,128]{2,1,0:T(8,128)(2,1)} %refs_3_.2) | copy-start | bytes 786436
  45.7 10.8 %copy-start = (f32[4,2,128,256]{3,2,1,0:T(8,128)S(1)}, f32[4,2,128,256]{3,2,1,0:T(8,128)}, u32[]{:S(2)}) copy-start(f32[4,2,128,256]{3,2,1,0:T(8,128)} %get-tuple-element.28.refs_3_.refs_6_) | copy-start | bytes 3145732
  45.7 10.8 %copy-start.10 = (f32[4,15,256]{2,0,1:T(4,128)S(1)}, f32[4,15,256]{2,0,1:T(4,128)}, u32[]{:S(2)}) copy-start(f32[4,15,256]{2,0,1:T(4,128)} %param.9) | copy-start | bytes 184324
  56.4 0.9 copy-start.1
  56.5 14.1 %copy-start.9 = (bf16[4,128,256]{2,1,0:T(8,128)(2,1)S(1)}, bf16[4,128,256]{2,1,0:T(8,128)(2,1)}, u32[]{:S(2)}) copy-start(bf16[4,128,256]{2,1,0:T(8,128)(2,1)} %get-tuple-element.34.refs_4_) | copy-start | bytes 786436
  57.3 14.4 %copy-start.7 = (f32[4,128,256]{2,1,0:T(8,128)}, f32[4,128,256]{2,1,0:T(8,128)S(1)}, u32[]{:S(2)}) copy-start(f32[4,128,256]{2,1,0:T(8,128)S(1)} %get-tuple-element.30.refs_7_.refs_2_) | copy-start | bytes 1572868
  70.6 1.2 %copy-start.11 = (f32[8,4,128]{2,1,0:T(4,128)}, f32[8,4,128]{2,1,0:T(4,128)S(1)}, u32[]{:S(2)}) copy-start(f32[8,4,128]{2,1,0:T(4,128)S(1)} %all_to_all.25.refs_0_) | copy-start | bytes 49156
  76.3 17.9 %all-to-all-start.3 = ((f32[32,3,8,128]{3,2,1,0:T(8,128)}), f32[32,3,8,128]{3,2,1,0:T(8,128)S(1)}, u32[]{:S(2)}, u32[]{:S(2)}) async-start(f32[32,3,8,128]{3,2,1,0:T(8,128)} %shard_map.110), calls=%async_computation.3 | async-start | bytes 786432 | tf_op jit(solution)/shard_map/all_to_all | solution.py:387
  83.0 10.4 %collective-permute-start.2 = (f32[2,128,128]{2,1,0:T(8,128)S(1)}, f32[2,128,128]{2,1,0:T(8,128)S(1)}, u32[]{:S(2)}, u32[]{:S(2)}) collective-permute-start(f32[2,128,128]{2,1,0:T(8,128)S(1)} %get-tuple-element.39), channel_id=1, source_target_pairs={{6,0},{4,2},{7,1},{5,3},{14,8},{12,10},{15,9},{13,11},{22,16},{20,... | collective-permute-start | bytes 393224 | tf_op jit(solution)/shard_map/ppermute | solution.py:462
  94.9 20.1 %all-to-all-start.4 = ((f32[64,8,128]{2,1,0:T(8,128)}), f32[64,8,128]{2,1,0:T(8,128)S(1)}, u32[]{:S(2)}, u32[]{:S(2)}) async-start(f32[64,8,128]{2,1,0:T(8,128)} %shard_map.112.refs_2_), calls=%async_computation.4 | async-start | bytes 524288 | tf_op jit(solution)/shard_map/all_to_all | solution.py:387
  102.0 8.7 %collective-permute-start.3 = (f32[2,128,128]{2,1,0:T(8,128)S(1)}, f32[2,128,128]{2,1,0:T(8,128)S(1)}, u32[]{:S(2)}, u32[]{:S(2)}) collective-permute-start(f32[2,128,128]{2,1,0:T(8,128)S(1)} %shard_map.113), channel_id=1, source_target_pairs={{0,2},{2,0},{6,4},{1,3},{3,1},{7,5},{8,10},{10,8},{14,12},{9,11},{... | collective-permute-start | bytes 393224 | tf_op jit(solution)/shard_map/ppermute | solution.py:480
  110.6 4.5 %copy-start.4 = (bf16[4,256,128]{2,1,0:T(8,128)(2,1)S(1)}, bf16[4,256,128]{2,1,0:T(8,128)(2,1)}, u32[]{:S(2)}) copy-start(bf16[4,256,128]{2,1,0:T(8,128)(2,1)} %refs_4_.5) | copy-start | bytes 786436
  110.6 4.5 %copy-start.5 = (f32[4,256,128]{2,1,0:T(8,128)S(1)}, f32[4,256,128]{2,1,0:T(8,128)}, u32[]{:S(2)}) copy-start(f32[4,256,128]{2,1,0:T(8,128)} %get-tuple-element.46.refs_5_) | copy-start | bytes 1572868
  110.6 4.5 %copy-start.6 = (f32[4,256,128]{2,1,0:T(8,128)S(1)}, f32[4,256,128]{2,1,0:T(8,128)}, u32[]{:S(2)}) copy-start(f32[4,256,128]{2,1,0:T(8,128)} %get-tuple-element.47.refs_6_) | copy-start | bytes 1572868
  110.7 4.4 %copy-start.3 = (bf16[4,256,128]{2,1,0:T(8,128)(2,1)S(1)}, bf16[4,256,128]{2,1,0:T(8,128)(2,1)}, u32[]{:S(2)}) copy-start(bf16[4,256,128]{2,1,0:T(8,128)(2,1)} %refs_3_.3) | copy-start | bytes 786436

commit v5 on v4

--- a/solution.py
+++ b/solution.py
@@ -1,3 +1,4 @@
+import functools
 import math
 
 import jax
@@ -199,9 +200,9 @@
 def owner_forward_body(in_ref, out_ref):
     sums = []
     for z in range(8):
-        total = in_ref[8 * z]
-        for p in range(1, 8):
-            total = total + in_ref[8 * z + p]
+        total = in_ref[4 * z]
+        for x in range(1, 4):
+            total = total + in_ref[4 * z + x]
         sums.append(total)
     nothing = jnp.zeros((8, HD), F32)
     pair0 = sums[0] + sums[1]
@@ -221,7 +222,7 @@
     tiles = []
     for m in range(PLANE):
         for i in range(16):
-            tiles.append(pc_ref[i % 2, 8 * h + i // 2, m])
+            tiles.append(pc_ref[h // 2, 16 * (h % 2) + i, m])
     return jnp.concatenate(tiles, axis=0).astype(BF16)
 
 
@@ -264,26 +265,19 @@
     for h in range(NH):
         go = (inv_row * mixed_ref[h, 1] - att_ref[h] * coef_row).astype(BF16)
         q_t = qt_ref[h].astype(F32)
-        states = dot(scaled_queries(q_t, lw_ref, 1, h), go, 1, 1)
-        for m in range(PLANE):
-            for k in range(8):
-                row = m * HD + 16 * k
-                even = states[row : row + 8]
-                odd = states[row + 8 : row + 16]
-                own_ref[8 * h + k, m] = jnp.where(first, even, odd)
-                send_ref[8 * h + k, m] = jnp.where(first, odd, even)
-        states = dot(scaled_queries(q_t, lw_ref, 0, h), go, 1, 1)
+        far = dot(scaled_queries(q_t, lw_ref, 1, h), go, 1, 1)
+        plane = dot(scaled_queries(q_t, lw_ref, 0, h), go, 1, 1)
         mine = first if h < NH // 2 else jnp.logical_not(first)
-        for m in range(PLANE):
-            value = states[m * HD : (m + 1) * HD]
-
-            @pl.when(mine)
-            def _keep(value=value, m=m, h=h):
-                keep_ref[m, h % 2] = value
-
-            @pl.when(jnp.logical_not(mine))
-            def _give(value=value, m=m, h=h):
-                give_ref[m, h % 2] = value
+
+        def store(far_ref, plane_ref, far=far, plane=plane, h=h):
+            for m in range(PLANE):
+                for i in range(16):
+                    row = m * HD + 8 * i
+                    far_ref[16 * (h % 2) + i, m] = far[row : row + 8]
+                plane_ref[m, h % 2] = plane[m * HD : (m + 1) * HD]
+
+        pl.when(mine)(functools.partial(store, own_ref, keep_ref))
+        pl.when(jnp.logical_not(mine))(functools.partial(store, send_ref, give_ref))
 
 
 def pair_body(own_ref, gath_ref, out_ref):
@@ -298,11 +292,11 @@
         second_ref[h] = keep_ref[2, h] + gath_ref[other, 2, h]
 
 
-def merge_body(back1_ref, back2_ref, keep_ref, gath_ref, mine_ref, send_ref):
+def merge_body(piece_ref, back1_ref, back2_ref, keep_ref, gath_ref, mine_ref, send_ref):
     first = lax.axis_index("core") == 0
     zero = jnp.float32(0.0)
     for h in range(NH // 2):
-        total = back1_ref[h] + back2_ref[h]
+        total = piece_ref[h] + (back1_ref[h] + back2_ref[h])
         mine_ref[h] = total + jnp.where(first, gath_ref[1, 0, h], zero)
         send_ref[h] = total + jnp.where(first, zero, keep_ref[0, h])
 
@@ -328,8 +322,8 @@
             total = total + (pair6 if z & 4 else pair2)
         if not z & 4:
             total = total + four
-        for p in range(8):
-            out_ref[8 * z + p] = total
+        for x in range(4):
+            out_ref[4 * z + x] = total
 
 
 def back_body(
@@ -370,13 +364,12 @@
     return step
 
 
-def final_body(piece_ref, mine_ref, wide_ref, k_ref, v_ref, gk_ref, gv_ref, outk_ref, outv_ref):
+def final_body(mine_ref, wide_ref, k_ref, v_ref, gk_ref, gv_ref, outk_ref, outv_ref):
     first = lax.axis_index("core") == 0
 
     def step(h):
         mine = first if h < NH // 2 else jnp.logical_not(first)
-        plane = jnp.where(mine, mine_ref[h % 2], wide_ref[h // 2, h % 2])
-        grad_kv = (piece_ref[h] + plane).astype(BF16)
+        grad_kv = jnp.where(mine, mine_ref[h % 2], wide_ref[h // 2, h % 2]).astype(BF16)
         outk_ref[h] = (gk_ref[h] + dot(v_ref[h], grad_kv, 1, 1)).astype(BF16)
         outv_ref[h] = (gv_ref[h] + dot(k_ref[h], grad_kv, 1, 0)).astype(BF16)
 
@@ -404,15 +397,15 @@
         ALONE,
         whole_in=True,
     )
-    owned = swap(kv.reshape(64, 8, HD), CTX)
     both = both_cores(kv)
     (pair,) = call(half_body, [(HALF, F32)], (both,), 2**16, MIB)
+    owned = swap(pair.reshape(32, 8, HD), ROWS)
     step1 = lax.ppermute(pair, "x", [(0, 1), (1, 0), (2, 3), (3, 2)])
+    (twice,) = call(add_body, [(HALF, F32)], (pair, step1), 2**16, MIB)
     (outgoing,) = call(
-        owner_forward_body, [(PIECES, F32)], (owned,), 2**17, MIB // 2, after=(pair,)
+        owner_forward_body, [(PIECES, F32)], (owned,), 2**17, MIB // 2, after=(twice,)
     )
     arrived = swap(outgoing, ROWS)
-    (twice,) = call(add_body, [(HALF, F32)], (pair, step1), 2**16, MIB, after=(outgoing,))
     step2 = lax.ppermute(twice, "x", [(0, 3), (1, 2)])
     (wide,) = call(
         collect_body,
@@ -474,17 +467,17 @@
         views={6: (TURNED, lambda ref: ref.at[:, 1])},
     )
     returned, back2, near_k = lax.optimization_barrier((returned, back2, near_k))
-    (spread,) = call(owner_backward_body, [((64, 8, HD), F32)], (returned,), 2**17, MIB // 2)
-    total = swap(spread, CTX).reshape(MATRIX)
+    (spread,) = call(owner_backward_body, [((32, 8, HD), F32)], (returned,), 2**17, MIB // 2)
+    pieces = swap(spread, ROWS).reshape(HALF)
     (onward,) = call(add_odd_body, [(HALF, F32)], (first, back2), 2**16, MIB, after=(spread,))
     back1 = lax.ppermute(onward, "x", [(0, 1), (1, 0), (3, 2)])
     mine, theirs = call(
-        merge_body, [(HALF, F32), (HALF, F32)], (back1, back2, keep, given), 2**16, MIB
+        merge_body, [(HALF, F32), (HALF, F32)], (pieces, back1, back2, keep, given), 2**16, MIB
     )
     grad_k, grad_v = call(
         final_body,
         [(TOKENS, BF16), (TOKENS, BF16)],
-        (total, mine, both_cores(theirs), key_rows, value_rows, near_k, near_v),
+        (mine, both_cores(theirs), key_rows, value_rows, near_k, near_v),
         2**26,
         3 * MIB,
     )

time: 117 us -> 114 us (0.974)
  blocking collectives: 33.6 us -> 42.7 us
  starting transfers between devices: 40.3 us -> 31.8 us
  waiting for transfers between devices: 24.7 us -> 20.1 us
  Pallas kernels: 16.2 us -> 17.8 us
    all_to_all x4, starting transfers between devices: 30.3 us -> 21.1 us  [swap(): return lax.all_to_all(value, axes, split_axis=0, concat_axis=0, tiled=True)]
    all_gather x6, blocking collectives: 20.4 us -> 29.5 us  [both_cores(): return lax.all_gather(value, 'core', axis=0, tiled=False)]
    all_to_all x4, waiting for transfers between devices: 15.5 us -> 12.7 us  [swap(): return lax.all_to_all(value, axes, split_axis=0, concat_axis=0, tiled=True)]
    ppermute x1, starting transfers between devices: 2.19 us -> 4.35 us  [shards(): step2 = lax.ppermute(twice, 'x', [(0, 3), (1, 2)])]
    ppermute x1, waiting for transfers between devices: 5.37 us -> 3.65 us  [shards(): back1 = lax.ppermute(onward, 'x', [(0, 1), (1, 0), (3, 2)])]
    pallas_call x15, Pallas kernels: 16.2 us -> 17.8 us  [call(): pl.pallas_call(wrapped, out_shape=[jax.ShapeDtypeStruct(s, d) for s, d in...]
    ppermute x1, starting transfers between devices: 3.21 us -> 1.91 us  [shards(): step1 = lax.ppermute(pair, 'x', [(0, 1), (1, 0), (2, 3), (3, 2)])]
  transfers between devices with their start and end apart: 8 -> 8, of which waited for: 6 -> 6; matrix products, arithmetic and copies ran while one was open for 0% -> 0% of each run, Pallas kernels for 9% -> 10%
where the time goes in v5:
time: 114 us
  blocking collectives  42.7 us (37%)
  starting transfers between devices  31.8 us (28%)
  waiting for transfers between devices  20.1 us (18%)
  Pallas kernels  17.8 us (16%)
    all_gather x6, blocking collectives, both_cores(): return lax.all_gather(value, 'core', axis=0, tiled=False)  29.5 us
    all_to_all x4, starting transfers between devices, swap(): return lax.all_to_all(value, axes, split_axis=0, concat_axis=0, tiled=True)  21.1 us
    pallas_call x15, Pallas kernels, call(): pl.pallas_call(wrapped, out_shape=[jax.ShapeDtypeStruct(s, d) for s, d in...  17.8 us
    all_to_all x1, blocking collectives, swap(): return lax.all_to_all(value, axes, split_axis=0, concat_axis=0, tiled=True)  13.2 us
    all_to_all x4, waiting for transfers between devices, swap(): return lax.all_to_all(value, axes, split_axis=0, concat_axis=0, tiled=True)  12.7 us
    ppermute x1, starting transfers between devices, shards(): step2 = lax.ppermute(twice, 'x', [(0, 3), (1, 2)])  4.35 us
    ppermute x1, waiting for transfers between devices, shards(): back2 = lax.ppermute(second, 'x', [(3, 0), (2, 1)])  3.72 us
    ppermute x1, waiting for transfers between devices, shards(): back1 = lax.ppermute(onward, 'x', [(0, 1), (1, 0), (3, 2)])  3.65 us
  transfers between devices with their start and end apart: 8, of which 6 were waited for; matrix products, arithmetic and copies ran while one was open for 0% of the time, Pallas kernels for 10%

profile of v5, /device:TPU:1, one launch (start us, length us, event | category | flops | bytes accessed | tf_op | source)
XLA Modules:
  0.0 113.7 jit_solution(14538565839127526888)
XLA Ops:
  0.6 2.0 %shard_map.101 = f32[4,128,128]{2,1,0:T(8,128)} custom-call(bf16[4,256,128]{2,1,0:T(8,128)(2,1)} %refs_2_.3, bf16[4,256,128]{2,1,0:T(8,128)(2,1)} %refs_3_.3), custom_call_target="tpu_custom_call" | custom-call | flops 33554432 | bytes 1048576 | tf_op jit(solution)/shard_map/pallas_call | solution.py:109
  2.6 8.9 %all-gather = f32[8,128,128]{2,1,0:T(8,128)S(1)} all-gather(f32[4,128,128]{2,1,0:T(8,128)} %shard_map.101), channel_id=2, replica_groups=mesh['heads'=8,'z'=8,'x'=4,'core'=2] {'core'}, dimensions={0}, use_global_device_ids=true | all-gather | bytes 786432 | tf_op jit(solution)/shard_map/all_gather | solution.py:384
  12.2 1.9 %collective-permute-start = (f32[2,128,128]{2,1,0:T(8,128)}, f32[2,128,128]{2,1,0:T(8,128)S(1)}, u32[]{:S(2)}, u32[]{:S(2)}) collective-permute-start(f32[2,128,128]{2,1,0:T(8,128)} %shard_map.102.refs_0_), channel_id=1, source_target_pairs={{0,2},{2,0},{4,6},{6,4},{1,3},{3,1},{5,7},{7,5},{8,10},{10,8},{12,... | collective-permute-start | bytes 393224 | tf_op jit(solution)/shard_map/ppermute | solution.py:403
  14.2 8.4 %all-to-all-start = ((f32[32,8,128]{2,1,0:T(8,128)}), f32[32,8,128]{2,1,0:T(8,128)S(1)}, u32[]{:S(2)}, u32[]{:S(2)}) async-start(f32[32,8,128]{2,1,0:T(8,128)} %bitcast.1), calls=%async_computation | async-start | bytes 262144 | tf_op jit(solution)/shard_map/all_to_all | solution.py:380
  23.6 4.4 %collective-permute-start.1 = (f32[2,128,128]{2,1,0:T(8,128)S(1)}, f32[2,128,128]{2,1,0:T(8,128)S(1)}, u32[]{:S(2)}, u32[]{:S(2)}) collective-permute-start(f32[2,128,128]{2,1,0:T(8,128)S(1)} %shard_map.103.refs_1_), channel_id=1, source_target_pairs={{0,6},{2,4},{1,7},{3,5},{8,14},{10,12},{9,15},{11,13},{16,22},{18,... | collective-permute-start | bytes 393224 | tf_op jit(solution)/shard_map/ppermute | solution.py:409
  27.9 4.0 %all-to-all-done.refs_0_ = f32[32,8,128]{2,1,0:T(8,128)S(1)} async-done(((f32[32,8,128]{2,1,0:T(8,128)}), f32[32,8,128]{2,1,0:T(8,128)S(1)}, u32[]{:S(2)}, u32[]{:S(2)}) %all-to-all-start) | async-done | bytes 131104 | tf_op jit(solution)/shard_map/all_to_all | solution.py:380
  32.7 3.9 %all-to-all-start.1 = ((f32[32,3,8,128]{3,2,1,0:T(8,128)}), f32[32,3,8,128]{3,2,1,0:T(8,128)S(1)}, u32[]{:S(2)}, u32[]{:S(2)}) async-start(f32[32,3,8,128]{3,2,1,0:T(8,128)} %shard_map.104), calls=%async_computation.1 | async-start | bytes 786432 | tf_op jit(solution)/shard_map/all_to_all | solution.py:380
  36.7 4.0 %all-gather.2 = f32[4,2,128,128]{3,2,1,0:T(8,128)} all-gather(f32[2,2,128,128]{3,2,1,0:T(8,128)S(1)} %shard_map.105), channel_id=4, replica_groups=mesh['heads'=8,'z'=8,'x'=4,'core'=2] {'core'}, dimensions={0}, use_global_device_ids=true | all-gather | bytes 786432 | tf_op jit(solution)/shard_map/all_gather | solution.py:384
  40.6 3.9 %shard_map.106 = (f32[4,2,128,256]{3,2,1,0:T(8,128)}, bf16[4,384,128]{2,1,0:T(8,128)(2,1)}, bf16[4,128,256]{2,1,0:T(8,128)(2,1)}) custom-call(f32[15,4,256]{2,1,0:T(4,128)} %bitcast.19, f32[4,128]{1,0:T(4,128)} %refs_1_.5, f32[2,2,2,128,128]{4,3,2,1,0:T(8,128)} %bitcast.23, f32[2,4,128,128]{3,2,1,0:T(8,128)} %bitcast.16, bf16[4,256,128]{2,1,0:T(8,128)(2,1)} %refs_3_.2, ...), custom_call_target="tpu_custom_call" | custom-call | flops 17179869184 | bytes 4194304 | tf_op jit(solution)/shard_map/pallas_call | solution.py:109
  44.5 4.4 %all-to-all-done.1 = f32[32,3,8,128]{3,2,1,0:T(8,128)S(1)} async-done(((f32[32,3,8,128]{3,2,1,0:T(8,128)}), f32[32,3,8,128]{3,2,1,0:T(8,128)S(1)}, u32[]{:S(2)}, u32[]{:S(2)}) %all-to-all-start.1) | async-done | bytes 393248 | tf_op jit(solution)/shard_map/all_to_all | solution.py:380
  48.9 6.3 %all-gather.1 = f32[64,3,8,128]{3,2,1,0:T(8,128)S(1)} all-gather(f32[32,3,8,128]{3,2,1,0:T(8,128)S(1)} %all-to-all-done.1), channel_id=3, replica_groups=mesh['heads'=8,'z'=8,'x'=4,'core'=2] {'core'}, dimensions={0}, use_global_device_ids=true | all-gather | bytes 1179648 | tf_op jit(solution)/shard_map/all_gather | solution.py:384
  56.1 13.2 %all_to_all.25.refs_0_ = f32[8,4,128]{2,1,0:T(4,128)S(1)} all-to-all(f32[8,4,128]{2,1,0:T(4,128)S(1)} %get-tuple-element.29), channel_id=1, replica_groups=mesh['heads'=8,'z'=8,'x'=4,'core'=2] {'heads'}, dimensions={0} | all-to-all | bytes 32768 | tf_op jit(solution)/shard_map/all_to_all | solution.py:380
  70.6 3.8 %all-gather.3 = f32[64,3,8,128]{3,2,1,0:T(8,128)S(1)} all-gather(f32[32,3,8,128]{3,2,1,0:T(8,128)S(1)} %get-tuple-element.36), channel_id=5, replica_groups=mesh['heads'=8,'z'=8,'x'=4,'core'=2] {'core'}, dimensions={0}, use_global_device_ids=true | all-gather | bytes 1179648 | tf_op jit(solution)/shard_map/all_gather | solution.py:384
  75.2 3.9 %all-to-all-start.3 = ((f32[32,3,8,128]{3,2,1,0:T(8,128)}), f32[32,3,8,128]{3,2,1,0:T(8,128)S(1)}, u32[]{:S(2)}, u32[]{:S(2)}) async-start(f32[32,3,8,128]{3,2,1,0:T(8,128)} %shard_map.110), calls=%async_computation.3 | async-start | bytes 786432 | tf_op jit(solution)/shard_map/all_to_all | solution.py:380
  79.0 2.4 %all-gather.4 = f32[6,2,128,128]{3,2,1,0:T(8,128)S(1)} all-gather(f32[3,2,128,128]{3,2,1,0:T(8,128)S(1)} %get-tuple-element.38), channel_id=6, replica_groups=mesh['heads'=8,'z'=8,'x'=4,'core'=2] {'core'}, dimensions={0}, use_global_device_ids=true | all-gather | bytes 1179648 | tf_op jit(solution)/shard_map/all_gather | solution.py:384
  81.4 1.3 %collective-permute-start.2 = (f32[2,128,128]{2,1,0:T(8,128)S(1)}, f32[2,128,128]{2,1,0:T(8,128)S(1)}, u32[]{:S(2)}, u32[]{:S(2)}) collective-permute-start(f32[2,128,128]{2,1,0:T(8,128)S(1)} %get-tuple-element.39), channel_id=1, source_target_pairs={{6,0},{4,2},{7,1},{5,3},{14,8},{12,10},{15,9},{13,11},{22,16},{20,... | collective-permute-start | bytes 393224 | tf_op jit(solution)/shard_map/ppermute | solution.py:455
  82.7 5.2 %shard_map.108 = (bf16[4,256,128]{2,1,0:T(8,128)(2,1)}, bf16[4,256,128]{2,1,0:T(8,128)(2,1)}, f32[4,256,128]{2,1,0:T(8,128)}, f32[4,256,128]{2,1,0:T(8,128)}, f32[15,4,256]{2,1,0:T(4,128)}) custom-call(f32[8,4,128]{2,1,0:T(4,128)} %copy-done.11, f32[4,128]{1,0:T(4,128)} %refs_1_.5, f32[15,4,256]{2,1,0:T(4,128)} %bitcast.20, bf16[4,256,128]{2,1,0:T(8,128)(2,1)} %refs_3_.2, ...), custom_call_target="tpu_custom_call" | custom-call | flops 17179869184 | bytes 5242880 | tf_op jit(solution)/shard_map/pallas_call | solution.py:109
  88.0 3.7 %collective-permute-done.2.refs_1_.refs_2_ = f32[2,128,128]{2,1,0:T(8,128)S(1)} collective-permute-done((f32[2,128,128]{2,1,0:T(8,128)S(1)}, f32[2,128,128]{2,1,0:T(8,128)S(1)}, u32[]{:S(2)}, u32[]{:S(2)}) %collective-permute-start.2) | collective-permute-done | bytes 131104 | tf_op jit(solution)/shard_map/ppermute | solution.py:455
  91.7 1.8 %all-to-all-done.3.refs_0_ = f32[32,3,8,128]{3,2,1,0:T(8,128)S(1)} async-done(((f32[32,3,8,128]{3,2,1,0:T(8,128)}), f32[32,3,8,128]{3,2,1,0:T(8,128)S(1)}, u32[]{:S(2)}, u32[]{:S(2)}) %all-to-all-start.3) | async-done | bytes 393248 | tf_op jit(solution)/shard_map/all_to_all | solution.py:380
  94.2 4.9 %all-to-all-start.4 = ((f32[32,8,128]{2,1,0:T(8,128)}), f32[32,8,128]{2,1,0:T(8,128)S(1)}, u32[]{:S(2)}, u32[]{:S(2)}) async-start(f32[32,8,128]{2,1,0:T(8,128)} %shard_map.112.refs_2_), calls=%async_computation.4 | async-start | bytes 262144 | tf_op jit(solution)/shard_map/all_to_all | solution.py:380
  99.1 3.1 %collective-permute-start.3 = (f32[2,128,128]{2,1,0:T(8,128)S(1)}, f32[2,128,128]{2,1,0:T(8,128)S(1)}, u32[]{:S(2)}, u32[]{:S(2)}) collective-permute-start(f32[2,128,128]{2,1,0:T(8,128)S(1)} %shard_map.113), channel_id=1, source_target_pairs={{0,2},{2,0},{6,4},{1,3},{3,1},{7,5},{8,10},{10,8},{14,12},{9,11},{... | collective-permute-start | bytes 393224 | tf_op jit(solution)/shard_map/ppermute | solution.py:473
  102.2 3.7 %collective-permute-done.3.refs_1_ = f32[2,128,128]{2,1,0:T(8,128)S(1)} collective-permute-done((f32[2,128,128]{2,1,0:T(8,128)S(1)}, f32[2,128,128]{2,1,0:T(8,128)S(1)}, u32[]{:S(2)}, u32[]{:S(2)}) %collective-permute-start.3) | collective-permute-done | bytes 131104 | tf_op jit(solution)/shard_map/ppermute | solution.py:473
  105.9 2.5 %all-to-all-done.4 = f32[32,8,128]{2,1,0:T(8,128)S(1)} async-done(((f32[32,8,128]{2,1,0:T(8,128)}), f32[32,8,128]{2,1,0:T(8,128)S(1)}, u32[]{:S(2)}, u32[]{:S(2)}) %all-to-all-start.4) | async-done | bytes 131104 | tf_op jit(solution)/shard_map/all_to_all | solution.py:380
  108.5 4.1 %all-gather.5 = f32[4,128,128]{2,1,0:T(8,128)S(1)} all-gather(f32[2,128,128]{2,1,0:T(8,128)S(1)} %get-tuple-element.45), channel_id=7, replica_groups=mesh['heads'=8,'z'=8,'x'=4,'core'=2] {'core'}, dimensions={0}, use_global_device_ids=true | all-gather | bytes 393216 | tf_op jit(solution)/shard_map/all_gather | solution.py:384
  (38 shorter events, 7.2 us)
Async XLA Ops:
  11.5 12.0 %copy-start.2 = (f32[8,128,128]{2,1,0:T(8,128)}, f32[8,128,128]{2,1,0:T(8,128)S(1)}, u32[]{:S(2)}) copy-start(f32[8,128,128]{2,1,0:T(8,128)S(1)} %all-gather) | copy-start | bytes 1572868
  12.2 10.4 %collective-permute-start = (f32[2,128,128]{2,1,0:T(8,128)}, f32[2,128,128]{2,1,0:T(8,128)S(1)}, u32[]{:S(2)}, u32[]{:S(2)}) collective-permute-start(f32[2,128,128]{2,1,0:T(8,128)} %shard_map.102.refs_0_), channel_id=1, source_target_pairs={{0,2},{2,0},{4,6},{6,4},{1,3},{3,1},{5,7},{7,5},{8,10},{10,8},{12,... | collective-permute-start | bytes 393224 | tf_op jit(solution)/shard_map/ppermute | solution.py:403
  14.2 17.8 %all-to-all-start = ((f32[32,8,128]{2,1,0:T(8,128)}), f32[32,8,128]{2,1,0:T(8,128)S(1)}, u32[]{:S(2)}, u32[]{:S(2)}) async-start(f32[32,8,128]{2,1,0:T(8,128)} %bitcast.1), calls=%async_computation | async-start | bytes 262144 | tf_op jit(solution)/shard_map/all_to_all | solution.py:380
  23.6 13.0 %collective-permute-start.1 = (f32[2,128,128]{2,1,0:T(8,128)S(1)}, f32[2,128,128]{2,1,0:T(8,128)S(1)}, u32[]{:S(2)}, u32[]{:S(2)}) collective-permute-start(f32[2,128,128]{2,1,0:T(8,128)S(1)} %shard_map.103.refs_1_), channel_id=1, source_target_pairs={{0,6},{2,4},{1,7},{3,5},{8,14},{10,12},{9,15},{11,13},{16,22},{18,... | collective-permute-start | bytes 393224 | tf_op jit(solution)/shard_map/ppermute | solution.py:409
  32.7 16.2 %all-to-all-start.1 = ((f32[32,3,8,128]{3,2,1,0:T(8,128)}), f32[32,3,8,128]{3,2,1,0:T(8,128)S(1)}, u32[]{:S(2)}, u32[]{:S(2)}) async-start(f32[32,3,8,128]{3,2,1,0:T(8,128)} %shard_map.104), calls=%async_computation.1 | async-start | bytes 786432 | tf_op jit(solution)/shard_map/all_to_all | solution.py:380
  40.6 14.6 %copy-start.8 = (bf16[4,256,128]{2,1,0:T(8,128)(2,1)S(1)}, bf16[4,256,128]{2,1,0:T(8,128)(2,1)}, u32[]{:S(2)}) copy-start(bf16[4,256,128]{2,1,0:T(8,128)(2,1)} %refs_3_.2) | copy-start | bytes 786436
  44.5 10.7 %copy-start = (f32[4,2,128,256]{3,2,1,0:T(8,128)S(1)}, f32[4,2,128,256]{3,2,1,0:T(8,128)}, u32[]{:S(2)}) copy-start(f32[4,2,128,256]{3,2,1,0:T(8,128)} %get-tuple-element.28.refs_3_.refs_6_) | copy-start | bytes 3145732
  44.5 10.7 %copy-start.10 = (f32[4,15,256]{2,0,1:T(4,128)S(1)}, f32[4,15,256]{2,0,1:T(4,128)}, u32[]{:S(2)}) copy-start(f32[4,15,256]{2,0,1:T(4,128)} %param.9) | copy-start | bytes 184324
  55.2 0.9 copy-start.1
  55.3 14.1 %copy-start.9 = (bf16[4,128,256]{2,1,0:T(8,128)(2,1)S(1)}, bf16[4,128,256]{2,1,0:T(8,128)(2,1)}, u32[]{:S(2)}) copy-start(bf16[4,128,256]{2,1,0:T(8,128)(2,1)} %get-tuple-element.34.refs_4_) | copy-start | bytes 786436
  56.1 14.4 %copy-start.7 = (f32[4,128,256]{2,1,0:T(8,128)}, f32[4,128,256]{2,1,0:T(8,128)S(1)}, u32[]{:S(2)}) copy-start(f32[4,128,256]{2,1,0:T(8,128)S(1)} %get-tuple-element.30.refs_7_.refs_2_) | copy-start | bytes 1572868
  69.4 1.2 %copy-start.11 = (f32[8,4,128]{2,1,0:T(4,128)}, f32[8,4,128]{2,1,0:T(4,128)S(1)}, u32[]{:S(2)}) copy-start(f32[8,4,128]{2,1,0:T(4,128)S(1)} %all_to_all.25.refs_0_) | copy-start | bytes 49156
  75.2 18.3 %all-to-all-start.3 = ((f32[32,3,8,128]{3,2,1,0:T(8,128)}), f32[32,3,8,128]{3,2,1,0:T(8,128)S(1)}, u32[]{:S(2)}, u32[]{:S(2)}) async-start(f32[32,3,8,128]{3,2,1,0:T(8,128)} %shard_map.110), calls=%async_computation.3 | async-start | bytes 786432 | tf_op jit(solution)/shard_map/all_to_all | solution.py:380
  81.4 10.2 %collective-permute-start.2 = (f32[2,128,128]{2,1,0:T(8,128)S(1)}, f32[2,128,128]{2,1,0:T(8,128)S(1)}, u32[]{:S(2)}, u32[]{:S(2)}) collective-permute-start(f32[2,128,128]{2,1,0:T(8,128)S(1)} %get-tuple-element.39), channel_id=1, source_target_pairs={{6,0},{4,2},{7,1},{5,3},{14,8},{12,10},{15,9},{13,11},{22,16},{20,... | collective-permute-start | bytes 393224 | tf_op jit(solution)/shard_map/ppermute | solution.py:455
  94.2 14.3 %all-to-all-start.4 = ((f32[32,8,128]{2,1,0:T(8,128)}), f32[32,8,128]{2,1,0:T(8,128)S(1)}, u32[]{:S(2)}, u32[]{:S(2)}) async-start(f32[32,8,128]{2,1,0:T(8,128)} %shard_map.112.refs_2_), calls=%async_computation.4 | async-start | bytes 262144 | tf_op jit(solution)/shard_map/all_to_all | solution.py:380
  99.1 6.8 %collective-permute-start.3 = (f32[2,128,128]{2,1,0:T(8,128)S(1)}, f32[2,128,128]{2,1,0:T(8,128)S(1)}, u32[]{:S(2)}, u32[]{:S(2)}) collective-permute-start(f32[2,128,128]{2,1,0:T(8,128)S(1)} %shard_map.113), channel_id=1, source_target_pairs={{0,2},{2,0},{6,4},{1,3},{3,1},{7,5},{8,10},{10,8},{14,12},{9,11},{... | collective-permute-start | bytes 393224 | tf_op jit(solution)/shard_map/ppermute | solution.py:473
  108.4 4.2 %copy-start.4 = (bf16[4,256,128]{2,1,0:T(8,128)(2,1)S(1)}, bf16[4,256,128]{2,1,0:T(8,128)(2,1)}, u32[]{:S(2)}) copy-start(bf16[4,256,128]{2,1,0:T(8,128)(2,1)} %refs_3_.3) | copy-start | bytes 786436
  108.4 4.2 %copy-start.5 = (f32[4,256,128]{2,1,0:T(8,128)S(1)}, f32[4,256,128]{2,1,0:T(8,128)}, u32[]{:S(2)}) copy-start(f32[4,256,128]{2,1,0:T(8,128)} %get-tuple-element.46.refs_4_) | copy-start | bytes 1572868
  108.4 4.2 %copy-start.6 = (f32[4,256,128]{2,1,0:T(8,128)S(1)}, f32[4,256,128]{2,1,0:T(8,128)}, u32[]{:S(2)}) copy-start(f32[4,256,128]{2,1,0:T(8,128)} %get-tuple-element.47.refs_5_) | copy-start | bytes 1572868
  108.5 4.1 %copy-start.3 = (bf16[4,256,128]{2,1,0:T(8,128)(2,1)S(1)}, bf16[4,256,128]{2,1,0:T(8,128)(2,1)}, u32[]{:S(2)}) copy-start(bf16[4,256,128]{2,1,0:T(8,128)(2,1)} %refs_2_.3) | copy-start | bytes 786436

commit v6 on v5

--- a/solution.py
+++ b/solution.py
@@ -24,7 +24,7 @@
 ALONE = 60
 
 CTX = ("z", "x", "core")
-ROWS = ("z", "x")
+ROWS = ("x", "z")
 
 TOKENS = (NH, TOK, HD)
 TURNED = (NH, HD, TOK)
@@ -200,9 +200,9 @@
 def owner_forward_body(in_ref, out_ref):
     sums = []
     for z in range(8):
-        total = in_ref[4 * z]
+        total = in_ref[z]
         for x in range(1, 4):
-            total = total + in_ref[4 * z + x]
+            total = total + in_ref[8 * x + z]
         sums.append(total)
     nothing = jnp.zeros((8, HD), F32)
     pair0 = sums[0] + sums[1]
@@ -213,9 +213,9 @@
         second = (pair2 if z & 4 else pair0) if z & 2 else nothing
         third = four if z & 4 else nothing
         for x in range(4):
-            out_ref[4 * z + x, 0] = first
-            out_ref[4 * z + x, 1] = second
-            out_ref[4 * z + x, 2] = third
+            out_ref[8 * x + z, 0] = first
+            out_ref[8 * x + z, 1] = second
+            out_ref[8 * x + z, 2] = third
 
 
 def far_states(pc_ref, h):
@@ -306,9 +306,9 @@
     for m in range(PLANE):
         rows = []
         for z in range(8):
-            total = in_ref[4 * z, m]
+            total = in_ref[z, m]
             for x in range(1, 4):
-                total = total + in_ref[4 * z + x, m]
+                total = total + in_ref[8 * x + z, m]
             rows.append(total)
         grads.append(rows)
     pair2 = grads[1][2] + grads[1][3]
@@ -323,7 +323,7 @@
         if not z & 4:
             total = total + four
         for x in range(4):
-            out_ref[4 * z + x] = total
+            out_ref[8 * x + z] = total
 
 
 def back_body(
@@ -425,6 +425,7 @@
         tuple(range(8)),
         tuple(range(3)),
         ALONE,
+        whole_in=True,
         views={3: (MATRIX, lambda ref: ref.at[0])},
     )
     gathered = both_cores(arrived)

time: 114 us -> 114 us (level)
  waiting for transfers between devices: 20.1 us -> 16.8 us
  starting transfers between devices: 31.8 us -> 34.5 us
    all_to_all x4, waiting for transfers between devices: 12.7 us -> 9.19 us  [swap(): return lax.all_to_all(value, axes, split_axis=0, concat_axis=0, tiled=True)]
    all_to_all x4, starting transfers between devices: 21.1 us -> 23.7 us  [swap(): return lax.all_to_all(value, axes, split_axis=0, concat_axis=0, tiled=True)]
  transfers between devices with their start and end apart: 8 -> 8, of which waited for: 6 -> 5; matrix products, arithmetic and copies ran while one was open for 0% -> 0% of each run, Pallas kernels for 10% -> 9%
where the time goes in v6:
time: 114 us; the launch traced here: 113 us
  blocking collectives  43.2 us (38%)
  starting transfers between devices  34.5 us (30%)
  Pallas kernels  17.4 us (15%)
  waiting for transfers between devices  16.8 us (15%)
    all_gather x6, blocking collectives, both_cores(): return lax.all_gather(value, 'core', axis=0, tiled=False)  30 us
    all_to_all x4, starting transfers between devices, swap(): return lax.all_to_all(value, axes, split_axis=0, concat_axis=0, tiled=True)  23.7 us
    pallas_call x15, Pallas kernels, call(): pl.pallas_call(wrapped, out_shape=[jax.ShapeDtypeStruct(s, d) for s, d in...  17.4 us
    all_to_all x1, blocking collectives, swap(): return lax.all_to_all(value, axes, split_axis=0, concat_axis=0, tiled=True)  13.2 us
    all_to_all x4, waiting for transfers between devices, swap(): return lax.all_to_all(value, axes, split_axis=0, concat_axis=0, tiled=True)  9.19 us
    ppermute x1, starting transfers between devices, shards(): step2 = lax.ppermute(twice, 'x', [(0, 3), (1, 2)])  4.4 us
    ppermute x1, waiting for transfers between devices, shards(): back2 = lax.ppermute(second, 'x', [(3, 0), (2, 1)])  3.95 us
    ppermute x1, waiting for transfers between devices, shards(): back1 = lax.ppermute(onward, 'x', [(0, 1), (1, 0), (3, 2)])  3.67 us
  transfers between devices with their start and end apart: 8, of which 5 were waited for; matrix products, arithmetic and copies ran while one was open for 0% of the time, Pallas kernels for 9%

profile of v6, /device:TPU:1, one launch (start us, length us, event | category | flops | bytes accessed | tf_op | source)
XLA Modules:
  0.0 113.3 jit_solution(17999029505065877787)
XLA Ops:
  0.6 2.0 %shard_map.101 = f32[4,128,128]{2,1,0:T(8,128)} custom-call(bf16[4,256,128]{2,1,0:T(8,128)(2,1)} %refs_2_.3, bf16[4,256,128]{2,1,0:T(8,128)(2,1)} %refs_3_.3), custom_call_target="tpu_custom_call" | custom-call | flops 33554432 | bytes 1048576 | tf_op jit(solution)/shard_map/pallas_call | solution.py:109
  2.6 8.9 %all-gather = f32[8,128,128]{2,1,0:T(8,128)S(1)} all-gather(f32[4,128,128]{2,1,0:T(8,128)} %shard_map.101), channel_id=2, replica_groups=mesh['heads'=8,'z'=8,'x'=4,'core'=2] {'core'}, dimensions={0}, use_global_device_ids=true | all-gather | bytes 786432 | tf_op jit(solution)/shard_map/all_gather | solution.py:384
  12.2 1.9 %collective-permute-start = (f32[2,128,128]{2,1,0:T(8,128)}, f32[2,128,128]{2,1,0:T(8,128)S(1)}, u32[]{:S(2)}, u32[]{:S(2)}) collective-permute-start(f32[2,128,128]{2,1,0:T(8,128)} %shard_map.102.refs_0_), channel_id=1, source_target_pairs={{0,2},{2,0},{4,6},{6,4},{1,3},{3,1},{5,7},{7,5},{8,10},{10,8},{12,... | collective-permute-start | bytes 393224 | tf_op jit(solution)/shard_map/ppermute | solution.py:403
  14.2 8.4 %all-to-all-start = ((f32[32,8,128]{2,1,0:T(8,128)}), f32[32,8,128]{2,1,0:T(8,128)S(1)}, u32[]{:S(2)}, u32[]{:S(2)}) async-start(f32[32,8,128]{2,1,0:T(8,128)} %bitcast.1), calls=%async_computation | async-start | bytes 262144 | tf_op jit(solution)/shard_map/all_to_all | solution.py:380
  23.6 4.4 %collective-permute-start.1 = (f32[2,128,128]{2,1,0:T(8,128)S(1)}, f32[2,128,128]{2,1,0:T(8,128)S(1)}, u32[]{:S(2)}, u32[]{:S(2)}) collective-permute-start(f32[2,128,128]{2,1,0:T(8,128)S(1)} %shard_map.103.refs_1_), channel_id=1, source_target_pairs={{0,6},{2,4},{1,7},{3,5},{8,14},{10,12},{9,15},{11,13},{16,22},{18,... | collective-permute-start | bytes 393224 | tf_op jit(solution)/shard_map/ppermute | solution.py:409
  28.0 3.9 %all-to-all-done.refs_0_ = f32[32,8,128]{2,1,0:T(8,128)S(1)} async-done(((f32[32,8,128]{2,1,0:T(8,128)}), f32[32,8,128]{2,1,0:T(8,128)S(1)}, u32[]{:S(2)}, u32[]{:S(2)}) %all-to-all-start) | async-done | bytes 131104 | tf_op jit(solution)/shard_map/all_to_all | solution.py:380
  32.6 3.9 %all-to-all-start.1 = ((f32[32,3,8,128]{3,2,1,0:T(8,128)}), f32[32,3,8,128]{3,2,1,0:T(8,128)S(1)}, u32[]{:S(2)}, u32[]{:S(2)}) async-start(f32[32,3,8,128]{3,2,1,0:T(8,128)} %shard_map.104), calls=%async_computation.1 | async-start | bytes 786432 | tf_op jit(solution)/shard_map/all_to_all | solution.py:380
  36.6 3.9 %all-gather.2 = f32[4,2,128,128]{3,2,1,0:T(8,128)} all-gather(f32[2,2,128,128]{3,2,1,0:T(8,128)S(1)} %shard_map.105), channel_id=4, replica_groups=mesh['heads'=8,'z'=8,'x'=4,'core'=2] {'core'}, dimensions={0}, use_global_device_ids=true | all-gather | bytes 786432 | tf_op jit(solution)/shard_map/all_gather | solution.py:384
  40.5 3.5 %shard_map.106 = (f32[4,2,128,256]{3,2,1,0:T(8,128)}, bf16[4,384,128]{2,1,0:T(8,128)(2,1)}, bf16[4,128,256]{2,1,0:T(8,128)(2,1)}) custom-call(f32[15,4,256]{2,1,0:T(4,128)} %bitcast.19, f32[4,128]{1,0:T(4,128)} %refs_1_.5, f32[2,2,2,128,128]{4,3,2,1,0:T(8,128)} %bitcast.23, f32[2,4,128,128]{3,2,1,0:T(8,128)} %bitcast.16, bf16[4,256,128]{2,1,0:T(8,128)(2,1)} %refs_3_.2, ...), custom_call_target="tpu_custom_call" | custom-call | flops 17179869184 | bytes 4194304 | tf_op jit(solution)/shard_map/pallas_call | solution.py:109
  44.0 3.0 %all-to-all-done.1 = f32[32,3,8,128]{3,2,1,0:T(8,128)S(1)} async-done(((f32[32,3,8,128]{3,2,1,0:T(8,128)}), f32[32,3,8,128]{3,2,1,0:T(8,128)S(1)}, u32[]{:S(2)}, u32[]{:S(2)}) %all-to-all-start.1) | async-done | bytes 393248 | tf_op jit(solution)/shard_map/all_to_all | solution.py:380
  47.0 6.9 %all-gather.1 = f32[64,3,8,128]{3,2,1,0:T(8,128)S(1)} all-gather(f32[32,3,8,128]{3,2,1,0:T(8,128)S(1)} %all-to-all-done.1), channel_id=3, replica_groups=mesh['heads'=8,'z'=8,'x'=4,'core'=2] {'core'}, dimensions={0}, use_global_device_ids=true | all-gather | bytes 1179648 | tf_op jit(solution)/shard_map/all_gather | solution.py:384
  54.8 13.2 %all_to_all.25.refs_0_ = f32[8,4,128]{2,1,0:T(4,128)S(1)} all-to-all(f32[8,4,128]{2,1,0:T(4,128)S(1)} %get-tuple-element.29), channel_id=1, replica_groups=mesh['heads'=8,'z'=8,'x'=4,'core'=2] {'heads'}, dimensions={0} | all-to-all | bytes 32768 | tf_op jit(solution)/shard_map/all_to_all | solution.py:380
  68.0 1.2 %shard_map.109 = (f32[32,3,8,128]{3,2,1,0:T(8,128)S(1)}, f32[32,3,8,128]{3,2,1,0:T(8,128)S(1)}, f32[3,2,128,128]{3,2,1,0:T(8,128)S(1)}, f32[3,2,128,128]{3,2,1,0:T(8,128)S(1)}) custom-call(f32[8,4,128]{2,1,0:T(4,128)S(1)} %all_to_all.25.refs_0_, f32[15,4,256]{2,1,0:T(4,128)S(1)} %bitcast.22, f32[4,128,256]{2,1,0:T(8,128)S(1)} %get-tuple-element.30.refs_7_.refs_2_, ...), custom_call_target="tpu_custom_call" | custom-call | flops 268435456 | bytes 6291456 | tf_op jit(solution)/shard_map/pallas_call | solution.py:109
  69.2 3.8 %all-gather.3 = f32[64,3,8,128]{3,2,1,0:T(8,128)S(1)} all-gather(f32[32,3,8,128]{3,2,1,0:T(8,128)S(1)} %get-tuple-element.36), channel_id=5, replica_groups=mesh['heads'=8,'z'=8,'x'=4,'core'=2] {'core'}, dimensions={0}, use_global_device_ids=true | all-gather | bytes 1179648 | tf_op jit(solution)/shard_map/all_gather | solution.py:384
  73.8 5.0 %all-to-all-start.3 = ((f32[32,3,8,128]{3,2,1,0:T(8,128)}), f32[32,3,8,128]{3,2,1,0:T(8,128)S(1)}, u32[]{:S(2)}, u32[]{:S(2)}) async-start(f32[32,3,8,128]{3,2,1,0:T(8,128)} %shard_map.110), calls=%async_computation.3 | async-start | bytes 786432 | tf_op jit(solution)/shard_map/all_to_all | solution.py:380
  78.7 2.6 %all-gather.4 = f32[6,2,128,128]{3,2,1,0:T(8,128)S(1)} all-gather(f32[3,2,128,128]{3,2,1,0:T(8,128)S(1)} %get-tuple-element.38), channel_id=6, replica_groups=mesh['heads'=8,'z'=8,'x'=4,'core'=2] {'core'}, dimensions={0}, use_global_device_ids=true | all-gather | bytes 1179648 | tf_op jit(solution)/shard_map/all_gather | solution.py:384
  81.4 1.3 %collective-permute-start.2 = (f32[2,128,128]{2,1,0:T(8,128)S(1)}, f32[2,128,128]{2,1,0:T(8,128)S(1)}, u32[]{:S(2)}, u32[]{:S(2)}) collective-permute-start(f32[2,128,128]{2,1,0:T(8,128)S(1)} %get-tuple-element.39), channel_id=1, source_target_pairs={{6,0},{4,2},{7,1},{5,3},{14,8},{12,10},{15,9},{13,11},{22,16},{20,... | collective-permute-start | bytes 393224 | tf_op jit(solution)/shard_map/ppermute | solution.py:456
  82.7 5.2 %shard_map.108 = (bf16[4,256,128]{2,1,0:T(8,128)(2,1)}, bf16[4,256,128]{2,1,0:T(8,128)(2,1)}, f32[4,256,128]{2,1,0:T(8,128)}, f32[4,256,128]{2,1,0:T(8,128)}, f32[15,4,256]{2,1,0:T(4,128)}) custom-call(f32[8,4,128]{2,1,0:T(4,128)} %copy-done.11, f32[4,128]{1,0:T(4,128)} %refs_1_.5, f32[15,4,256]{2,1,0:T(4,128)} %bitcast.20, bf16[4,256,128]{2,1,0:T(8,128)(2,1)} %refs_3_.2, ...), custom_call_target="tpu_custom_call" | custom-call | flops 17179869184 | bytes 5242880 | tf_op jit(solution)/shard_map/pallas_call | solution.py:109
  88.0 4.0 %collective-permute-done.2.refs_1_.refs_2_ = f32[2,128,128]{2,1,0:T(8,128)S(1)} collective-permute-done((f32[2,128,128]{2,1,0:T(8,128)S(1)}, f32[2,128,128]{2,1,0:T(8,128)S(1)}, u32[]{:S(2)}, u32[]{:S(2)}) %collective-permute-start.2) | collective-permute-done | bytes 131104 | tf_op jit(solution)/shard_map/ppermute | solution.py:456
  92.6 6.5 %all-to-all-start.4 = ((f32[32,8,128]{2,1,0:T(8,128)}), f32[32,8,128]{2,1,0:T(8,128)S(1)}, u32[]{:S(2)}, u32[]{:S(2)}) async-start(f32[32,8,128]{2,1,0:T(8,128)} %shard_map.112.refs_2_), calls=%async_computation.4 | async-start | bytes 262144 | tf_op jit(solution)/shard_map/all_to_all | solution.py:380
  99.1 3.1 %collective-permute-start.3 = (f32[2,128,128]{2,1,0:T(8,128)S(1)}, f32[2,128,128]{2,1,0:T(8,128)S(1)}, u32[]{:S(2)}, u32[]{:S(2)}) collective-permute-start(f32[2,128,128]{2,1,0:T(8,128)S(1)} %shard_map.113), channel_id=1, source_target_pairs={{0,2},{2,0},{6,4},{1,3},{3,1},{7,5},{8,10},{10,8},{14,12},{9,11},{... | collective-permute-start | bytes 393224 | tf_op jit(solution)/shard_map/ppermute | solution.py:474
  102.2 3.7 %collective-permute-done.3.refs_1_ = f32[2,128,128]{2,1,0:T(8,128)S(1)} collective-permute-done((f32[2,128,128]{2,1,0:T(8,128)S(1)}, f32[2,128,128]{2,1,0:T(8,128)S(1)}, u32[]{:S(2)}, u32[]{:S(2)}) %collective-permute-start.3) | collective-permute-done | bytes 131104 | tf_op jit(solution)/shard_map/ppermute | solution.py:474
  105.9 2.3 %all-to-all-done.4 = f32[32,8,128]{2,1,0:T(8,128)S(1)} async-done(((f32[32,8,128]{2,1,0:T(8,128)}), f32[32,8,128]{2,1,0:T(8,128)S(1)}, u32[]{:S(2)}, u32[]{:S(2)}) %all-to-all-start.4) | async-done | bytes 131104 | tf_op jit(solution)/shard_map/all_to_all | solution.py:380
  108.3 3.9 %all-gather.5 = f32[4,128,128]{2,1,0:T(8,128)S(1)} all-gather(f32[2,128,128]{2,1,0:T(8,128)S(1)} %get-tuple-element.45), channel_id=7, replica_groups=mesh['heads'=8,'z'=8,'x'=4,'core'=2] {'core'}, dimensions={0}, use_global_device_ids=true | all-gather | bytes 393216 | tf_op jit(solution)/shard_map/all_gather | solution.py:384
  (38 shorter events, 6.0 us)
Async XLA Ops:
  11.5 12.0 %copy-start.2 = (f32[8,128,128]{2,1,0:T(8,128)}, f32[8,128,128]{2,1,0:T(8,128)S(1)}, u32[]{:S(2)}) copy-start(f32[8,128,128]{2,1,0:T(8,128)S(1)} %all-gather) | copy-start | bytes 1572868
  12.2 10.4 %collective-permute-start = (f32[2,128,128]{2,1,0:T(8,128)}, f32[2,128,128]{2,1,0:T(8,128)S(1)}, u32[]{:S(2)}, u32[]{:S(2)}) collective-permute-start(f32[2,128,128]{2,1,0:T(8,128)} %shard_map.102.refs_0_), channel_id=1, source_target_pairs={{0,2},{2,0},{4,6},{6,4},{1,3},{3,1},{5,7},{7,5},{8,10},{10,8},{12,... | collective-permute-start | bytes 393224 | tf_op jit(solution)/shard_map/ppermute | solution.py:403
  14.2 17.7 %all-to-all-start = ((f32[32,8,128]{2,1,0:T(8,128)}), f32[32,8,128]{2,1,0:T(8,128)S(1)}, u32[]{:S(2)}, u32[]{:S(2)}) async-start(f32[32,8,128]{2,1,0:T(8,128)} %bitcast.1), calls=%async_computation | async-start | bytes 262144 | tf_op jit(solution)/shard_map/all_to_all | solution.py:380
  23.6 12.9 %collective-permute-start.1 = (f32[2,128,128]{2,1,0:T(8,128)S(1)}, f32[2,128,128]{2,1,0:T(8,128)S(1)}, u32[]{:S(2)}, u32[]{:S(2)}) collective-permute-start(f32[2,128,128]{2,1,0:T(8,128)S(1)} %shard_map.103.refs_1_), channel_id=1, source_target_pairs={{0,6},{2,4},{1,7},{3,5},{8,14},{10,12},{9,15},{11,13},{16,22},{18,... | collective-permute-start | bytes 393224 | tf_op jit(solution)/shard_map/ppermute | solution.py:409
  32.6 14.4 %all-to-all-start.1 = ((f32[32,3,8,128]{3,2,1,0:T(8,128)}), f32[32,3,8,128]{3,2,1,0:T(8,128)S(1)}, u32[]{:S(2)}, u32[]{:S(2)}) async-start(f32[32,3,8,128]{3,2,1,0:T(8,128)} %shard_map.104), calls=%async_computation.1 | async-start | bytes 786432 | tf_op jit(solution)/shard_map/all_to_all | solution.py:380
  40.5 13.4 %copy-start.8 = (bf16[4,256,128]{2,1,0:T(8,128)(2,1)S(1)}, bf16[4,256,128]{2,1,0:T(8,128)(2,1)}, u32[]{:S(2)}) copy-start(bf16[4,256,128]{2,1,0:T(8,128)(2,1)} %refs_3_.2) | copy-start | bytes 786436
  44.0 9.9 %copy-start = (f32[4,2,128,256]{3,2,1,0:T(8,128)S(1)}, f32[4,2,128,256]{3,2,1,0:T(8,128)}, u32[]{:S(2)}) copy-start(f32[4,2,128,256]{3,2,1,0:T(8,128)} %get-tuple-element.28.refs_3_.refs_6_) | copy-start | bytes 3145732
  44.0 9.9 %copy-start.10 = (f32[4,15,256]{2,0,1:T(4,128)S(1)}, f32[4,15,256]{2,0,1:T(4,128)}, u32[]{:S(2)}) copy-start(f32[4,15,256]{2,0,1:T(4,128)} %param.9) | copy-start | bytes 184324
  53.9 0.9 copy-start.1
  53.9 14.1 %copy-start.9 = (bf16[4,128,256]{2,1,0:T(8,128)(2,1)S(1)}, bf16[4,128,256]{2,1,0:T(8,128)(2,1)}, u32[]{:S(2)}) copy-start(bf16[4,128,256]{2,1,0:T(8,128)(2,1)} %get-tuple-element.34.refs_4_) | copy-start | bytes 786436
  54.8 14.4 %copy-start.7 = (f32[4,128,256]{2,1,0:T(8,128)}, f32[4,128,256]{2,1,0:T(8,128)S(1)}, u32[]{:S(2)}) copy-start(f32[4,128,256]{2,1,0:T(8,128)S(1)} %get-tuple-element.30.refs_7_.refs_2_) | copy-start | bytes 1572868
  68.0 1.2 %copy-start.11 = (f32[8,4,128]{2,1,0:T(4,128)}, f32[8,4,128]{2,1,0:T(4,128)S(1)}, u32[]{:S(2)}) copy-start(f32[8,4,128]{2,1,0:T(4,128)S(1)} %all_to_all.25.refs_0_) | copy-start | bytes 49156
  73.8 18.1 %all-to-all-start.3 = ((f32[32,3,8,128]{3,2,1,0:T(8,128)}), f32[32,3,8,128]{3,2,1,0:T(8,128)S(1)}, u32[]{:S(2)}, u32[]{:S(2)}) async-start(f32[32,3,8,128]{3,2,1,0:T(8,128)} %shard_map.110), calls=%async_computation.3 | async-start | bytes 786432 | tf_op jit(solution)/shard_map/all_to_all | solution.py:380
  81.4 10.5 %collective-permute-start.2 = (f32[2,128,128]{2,1,0:T(8,128)S(1)}, f32[2,128,128]{2,1,0:T(8,128)S(1)}, u32[]{:S(2)}, u32[]{:S(2)}) collective-permute-start(f32[2,128,128]{2,1,0:T(8,128)S(1)} %get-tuple-element.39), channel_id=1, source_target_pairs={{6,0},{4,2},{7,1},{5,3},{14,8},{12,10},{15,9},{13,11},{22,16},{20,... | collective-permute-start | bytes 393224 | tf_op jit(solution)/shard_map/ppermute | solution.py:456
  92.6 15.6 %all-to-all-start.4 = ((f32[32,8,128]{2,1,0:T(8,128)}), f32[32,8,128]{2,1,0:T(8,128)S(1)}, u32[]{:S(2)}, u32[]{:S(2)}) async-start(f32[32,8,128]{2,1,0:T(8,128)} %shard_map.112.refs_2_), calls=%async_computation.4 | async-start | bytes 262144 | tf_op jit(solution)/shard_map/all_to_all | solution.py:380
  99.1 6.8 %collective-permute-start.3 = (f32[2,128,128]{2,1,0:T(8,128)S(1)}, f32[2,128,128]{2,1,0:T(8,128)S(1)}, u32[]{:S(2)}, u32[]{:S(2)}) collective-permute-start(f32[2,128,128]{2,1,0:T(8,128)S(1)} %shard_map.113), channel_id=1, source_target_pairs={{0,2},{2,0},{6,4},{1,3},{3,1},{7,5},{8,10},{10,8},{14,12},{9,11},{... | collective-permute-start | bytes 393224 | tf_op jit(solution)/shard_map/ppermute | solution.py:474
  108.2 4.0 %copy-start.4 = (bf16[4,256,128]{2,1,0:T(8,128)(2,1)S(1)}, bf16[4,256,128]{2,1,0:T(8,128)(2,1)}, u32[]{:S(2)}) copy-start(bf16[4,256,128]{2,1,0:T(8,128)(2,1)} %refs_3_.3) | copy-start | bytes 786436
  108.2 4.0 %copy-start.5 = (f32[4,256,128]{2,1,0:T(8,128)S(1)}, f32[4,256,128]{2,1,0:T(8,128)}, u32[]{:S(2)}) copy-start(f32[4,256,128]{2,1,0:T(8,128)} %get-tuple-element.46.refs_4_) | copy-start | bytes 1572868
  108.2 4.0 %copy-start.6 = (f32[4,256,128]{2,1,0:T(8,128)S(1)}, f32[4,256,128]{2,1,0:T(8,128)}, u32[]{:S(2)}) copy-start(f32[4,256,128]{2,1,0:T(8,128)} %get-tuple-element.47.refs_5_) | copy-start | bytes 1572868
  108.3 3.9 %copy-start.3 = (bf16[4,256,128]{2,1,0:T(8,128)(2,1)S(1)}, bf16[4,256,128]{2,1,0:T(8,128)(2,1)}, u32[]{:S(2)}) copy-start(bf16[4,256,128]{2,1,0:T(8,128)(2,1)} %refs_2_.3) | copy-start | bytes 786436
